TPU v7x, 256 devices: a whole 4x4x8 slice. The times are simulated.
256 devices in a mesh: orb: 64 (over z, x, core), rep: 4 (over y).
Axes of the slice: x: 4, y: 4, z: 8, core: 2. Of those that a mesh axis runs over, the one named last changes fastest.
Arguments:
- observed: float32 [512, 256], P('orb'), may hold values from -6 to 6
- weights: float32 [512, 256], P('orb'), may hold values from 0.25 to 4
- precision_prior: float32 [2048, 1024], P('orb', 'rep'), may hold values from 0.5 to 4
- footprint: bfloat16 [3072, 256, 1024], P('orb', None, 'rep'), may hold values from -0.1875 to 0.1875
- block_rows: int32 [3072], P('orb'), may hold values from 0 to 511, as said below
- block_cells: int32 [3072], P('orb'), may hold values from 0 to 2047, as said below
Outputs:
- solution: float32 [2048, 1024], P('orb', 'rep')
- residual: float32 [2048, 1024], P('orb', 'rep')
Inputs may be any that keep to these rules, and one draw needn't show every extreme that they name: `block_rows`: the listed blocks of orbit group g (rows g * 48 to (g + 1) * 48 - 1) name only sounding blocks g * 8 to (g + 1) * 8 - 1. `block_cells`: region group r holds cell-period blocks r * 32 to (r + 1) * 32 - 1. The first 2 listed blocks of every orbit group name cell-period blocks of one common region group; no orbit group names cell-period blocks of one region group in more than 2 of its listed blocks.
All inputs are finite; a program needn't handle non-finite values.
Results may differ from a plain program's by a relative error of at most 0.0015.
Values sent between devices are 32-bit elements; how exact they have to be, the bound alone decides.
No kernel may reach another device: no remote copies, remote signals or barrier semaphores. Data moves between devices by JAX's collectives and lax.ppermute only.
A program may use at most 64 MiB of HBM per device.

v0:
```python
import jax
import jax.numpy as jnp
from jax import lax
from jax.sharding import PartitionSpec as P

ITERS = 4


def per_device(observed, weights, precision_prior, footprint, block_rows, block_cells):
    highest = lax.Precision.HIGHEST
    sb_dev = observed.shape[0]
    cb_dev = precision_prior.shape[0]
    blocks_dev = block_cells.shape[0]
    width = precision_prior.shape[1]
    orbits = lax.axis_size("orb")
    capacity = max(2, 3 * blocks_dev // (2 * orbits))
    my_orbit = lax.axis_index("orb")
    local_rows = block_rows - my_orbit * sb_dev
    row_pick = (local_rows[None, :] == jnp.arange(sb_dev, dtype=jnp.int32)[:, None]).astype(
        jnp.float32
    )
    owners = block_cells // cb_dev
    slot_ids = block_cells % cb_dev
    order_ids = jnp.arange(blocks_dev, dtype=jnp.int32)
    earlier = (owners[:, None] == owners[None, :]) & (order_ids[None, :] < order_ids[:, None])
    places = owners * capacity + jnp.sum(earlier.astype(jnp.int32), axis=1)
    requests = (
        jnp.zeros((orbits * capacity,), jnp.int32)
        .at[places]
        .set(slot_ids + 1)
        .reshape(orbits, capacity)
    )
    requested = lax.all_to_all(requests, "orb", split_axis=0, concat_axis=0, tiled=True)
    serving = (
        requested.reshape(-1)[:, None] - 1 == jnp.arange(cb_dev, dtype=jnp.int32)[None, :]
    ).astype(jnp.float32)

    def deliver(contrib):
        outgoing = jnp.zeros((orbits * capacity, width), jnp.float32).at[places].set(contrib)
        incoming = lax.all_to_all(
            outgoing.reshape(orbits, capacity, width),
            "orb",
            split_axis=0,
            concat_axis=0,
            tiled=True,
        )
        return jnp.dot(serving.T, incoming.reshape(orbits * capacity, width), precision=highest)

    def adjoint(field):
        picked = jnp.take(field, local_rows, axis=0)
        contrib = jnp.einsum("bsc,bs->bc", footprint.astype(jnp.float32), picked, precision=highest)
        return deliver(contrib)

    def squares(vector):
        return lax.psum(jnp.sum(vector * vector), ("orb", "rep"))

    gradient = adjoint(weights * observed)
    solution = jnp.zeros_like(gradient)
    residual = gradient
    direction = gradient
    norm_now = squares(residual)
    for iteration in range(ITERS):
        pieces = jnp.dot(serving, direction, precision=highest).reshape(orbits, capacity, width)
        arrived = lax.all_to_all(pieces, "orb", split_axis=0, concat_axis=0, tiled=True)
        values = jnp.einsum(
            "bsc,bc->bs",
            footprint.astype(jnp.float32),
            jnp.take(arrived.reshape(orbits * capacity, width), places, axis=0),
            precision=highest,
        )
        partial_sums = jnp.dot(row_pick, values, precision=highest)
        image = adjoint(weights * lax.psum(partial_sums, "rep")) + precision_prior * direction
        curvature = lax.psum(jnp.sum(direction * image), ("orb", "rep"))
        alpha = norm_now / curvature
        solution = solution + alpha * direction
        residual = residual - alpha * image
        norm_next = squares(residual)
        direction = residual + norm_next / norm_now * direction
        norm_now = norm_next
    return (solution, residual)


def solution(mesh):
    in_specs = (
        P("orb", None),
        P("orb", None),
        P("orb", "rep"),
        P("orb", None, "rep"),
        P("orb"),
        P("orb"),
    )
    out_specs = (P("orb", "rep"), P("orb", "rep"))
    return jax.shard_map(
        per_device, mesh=mesh, in_specs=in_specs, out_specs=out_specs, check_vma=False
    )
```

profile of v0, /device:TPU:1, one launch (start us, length us, event | category | flops | bytes accessed | tf_op | source)
XLA Modules:
  0.0 804.6 jit_solution(16856146719951782547)
XLA Ops:
  3.0 13.0 %all-to-all-start = ((s32[64,1,2]{2,1,0:T(1,128)}), s32[64,1,2]{2,1,0:T(1,128)S(1)}, u32[]{:S(2)}, u32[]{:S(2)}) async-start(s32[64,1,2]{2,1,0:T(1,128)} %bitcast), calls=%async_computation | async-start | bytes 65536 | tf_op jit(solution)/shard_map/all_to_all | solution.py:33
  18.1 5.4 fusion.53
  25.3 10.0 %all-to-all-start.1 = ((f32[64,2,256]{2,1,0:T(2,128)}), f32[64,2,256]{2,1,0:T(2,128)S(1)}, u32[]{:S(2)}, u32[]{:S(2)}) async-start(f32[64,2,256]{2,1,0:T(2,128)} %reshape.85), calls=%async_computation.1 | async-start | bytes 262144 | tf_op jit(solution)/shard_map/all_to_all | solution.py:40
  35.5 10.9 %all-to-all-done.1 = f32[64,2,256]{2,1,0:T(2,128)S(1)} async-done(((f32[64,2,256]{2,1,0:T(2,128)}), f32[64,2,256]{2,1,0:T(2,128)S(1)}, u32[]{:S(2)}, u32[]{:S(2)}) %all-to-all-start.1) | async-done | bytes 131104 | tf_op jit(solution)/shard_map/all_to_all | solution.py:40
  47.8 4.4 all-to-all-start.2
  52.2 11.3 %all-to-all-done.2 = f32[64,2,256]{2,1,0:T(2,128)S(1)} async-done(((f32[64,2,256]{2,1,0:T(2,128)}), f32[64,2,256]{2,1,0:T(2,128)S(1)}, u32[]{:S(2)}, u32[]{:S(2)}) %all-to-all-start.2) | async-done | bytes 131104 | tf_op jit(solution)/shard_map/all_to_all | solution.py:64
  64.4 7.7 fusion.50
  72.3 8.8 %psum.85 = f32[8,256]{1,0:T(8,128)S(1)} all-reduce(f32[8,256]{1,0:T(8,128)S(1)} %fusion.25), channel_id=1, replica_groups=mesh['orb'=64,'rep'=4] {'rep'}, use_global_device_ids=true, to_apply=%region_5.8 | all-reduce | flops 2048 | bytes 16384 | tf_op jit(solution)/shard_map/psum | solution.py:72
  81.8 5.4 fusion.47
  88.1 17.1 %all_to_all.54 = f32[64,2,256]{2,1,0:T(2,128)S(1)} all-to-all(f32[64,2,256]{2,1,0:T(2,128)S(1)} %reshape.89), channel_id=1, replica_groups=mesh['orb'=64,'rep'=4] {'orb'}, dimensions={0} | all-to-all | bytes 262144 | tf_op jit(solution)/shard_map/all_to_all | solution.py:40
  106.2 72.8 %all-reduce = (f32[]{:T(128)}, f32[]{:T(128)}) all-reduce(f32[]{:T(128)} %get-tuple-element.5, f32[]{:T(128)} %get-tuple-element.4), channel_id=1, replica_groups=mesh['orb'=64,'rep'=4] {'orb','rep'}, use_global_device_ids=true, to_apply=%region_4.6 | all-reduce | flops 2 | bytes 16 | tf_op jit(solution)/shard_map/psum | solution.py:55
  180.9 73.5 %psum.87 = f32[]{:T(128)} all-reduce(f32[]{:T(128)} %multiply_reduce_fusion.5), channel_id=1, replica_groups=mesh['orb'=64,'rep'=4] {'orb','rep'}, use_global_device_ids=true, to_apply=%region_10.13 | all-reduce | flops 1 | bytes 8 | tf_op jit(solution)/shard_map/psum | solution.py:55
  256.1 17.0 %all_to_all.55 = f32[64,2,256]{2,1,0:T(2,128)S(1)} all-to-all(f32[64,2,256]{2,1,0:T(2,128)S(1)} %reshape.91), channel_id=1, replica_groups=mesh['orb'=64,'rep'=4] {'orb'}, dimensions={0} | all-to-all | bytes 262144 | tf_op jit(solution)/shard_map/all_to_all | solution.py:64
  273.9 7.7 fusion.44
  281.8 6.7 psum.88
  289.2 5.4 fusion.41
  295.5 16.9 %all_to_all.56 = f32[64,2,256]{2,1,0:T(2,128)S(1)} all-to-all(f32[64,2,256]{2,1,0:T(2,128)S(1)} %reshape.93), channel_id=1, replica_groups=mesh['orb'=64,'rep'=4] {'orb'}, dimensions={0} | all-to-all | bytes 262144 | tf_op jit(solution)/shard_map/all_to_all | solution.py:40
  313.4 72.7 %psum.89 = f32[]{:T(128)} all-reduce(f32[]{:T(128)} %get-tuple-element.19), channel_id=1, replica_groups=mesh['orb'=64,'rep'=4] {'orb','rep'}, use_global_device_ids=true, to_apply=%region_14.17 | all-reduce | flops 1 | bytes 8 | tf_op jit(solution)/shard_map/psum | solution.py:73
  388.0 73.7 %psum.90 = f32[]{:T(128)} all-reduce(f32[]{:T(128)} %get-tuple-element.10), channel_id=1, replica_groups=mesh['orb'=64,'rep'=4] {'orb','rep'}, use_global_device_ids=true, to_apply=%region_16.19 | all-reduce | flops 1 | bytes 8 | tf_op jit(solution)/shard_map/psum | solution.py:55
  463.4 17.7 %all_to_all.57 = f32[64,2,256]{2,1,0:T(2,128)S(1)} all-to-all(f32[64,2,256]{2,1,0:T(2,128)S(1)} %reshape.95), channel_id=1, replica_groups=mesh['orb'=64,'rep'=4] {'orb'}, dimensions={0} | all-to-all | bytes 262144 | tf_op jit(solution)/shard_map/all_to_all | solution.py:64
  481.9 7.7 fusion.38
  489.8 6.7 psum.91
  497.2 5.4 fusion.35
  503.5 16.9 %all_to_all.58 = f32[64,2,256]{2,1,0:T(2,128)S(1)} all-to-all(f32[64,2,256]{2,1,0:T(2,128)S(1)} %reshape.97), channel_id=1, replica_groups=mesh['orb'=64,'rep'=4] {'orb'}, dimensions={0} | all-to-all | bytes 262144 | tf_op jit(solution)/shard_map/all_to_all | solution.py:40
  521.4 72.7 %psum.92 = f32[]{:T(128)} all-reduce(f32[]{:T(128)} %get-tuple-element.21), channel_id=1, replica_groups=mesh['orb'=64,'rep'=4] {'orb','rep'}, use_global_device_ids=true, to_apply=%region_20.23 | all-reduce | flops 1 | bytes 8 | tf_op jit(solution)/shard_map/psum | solution.py:73
  596.0 73.5 %psum.93 = f32[]{:T(128)} all-reduce(f32[]{:T(128)} %get-tuple-element.8), channel_id=1, replica_groups=mesh['orb'=64,'rep'=4] {'orb','rep'}, use_global_device_ids=true, to_apply=%region_22.25 | all-reduce | flops 1 | bytes 8 | tf_op jit(solution)/shard_map/psum | solution.py:55
  671.2 18.0 %all_to_all.59 = f32[64,2,256]{2,1,0:T(2,128)S(1)} all-to-all(f32[64,2,256]{2,1,0:T(2,128)S(1)} %reshape.99), channel_id=1, replica_groups=mesh['orb'=64,'rep'=4] {'orb'}, dimensions={0} | all-to-all | bytes 262144 | tf_op jit(solution)/shard_map/all_to_all | solution.py:64
  690.0 7.7 fusion.32
  697.9 6.7 psum.94
  705.3 5.4 fusion.29
  711.5 17.0 %all_to_all.60 = f32[64,2,256]{2,1,0:T(2,128)S(1)} all-to-all(f32[64,2,256]{2,1,0:T(2,128)S(1)} %reshape.101), channel_id=1, replica_groups=mesh['orb'=64,'rep'=4] {'orb'}, dimensions={0} | all-to-all | bytes 262144 | tf_op jit(solution)/shard_map/all_to_all | solution.py:40
  729.5 72.7 %psum.95 = f32[]{:T(128)} all-reduce(f32[]{:T(128)} %get-tuple-element.23), channel_id=1, replica_groups=mesh['orb'=64,'rep'=4] {'orb','rep'}, use_global_device_ids=true, to_apply=%region_26.29 | all-reduce | flops 1 | bytes 8 | tf_op jit(solution)/shard_map/psum | solution.py:73
  (82 shorter events, 25.3 us)
Async XLA Ops:
  3.0 22.3 %all-to-all-start = ((s32[64,1,2]{2,1,0:T(1,128)}), s32[64,1,2]{2,1,0:T(1,128)S(1)}, u32[]{:S(2)}, u32[]{:S(2)}) async-start(s32[64,1,2]{2,1,0:T(1,128)} %bitcast), calls=%async_computation | async-start | bytes 65536 | tf_op jit(solution)/shard_map/all_to_all | solution.py:33
  18.1 63.0 %copy-start.1 = (f32[8,256]{1,0:T(8,128)S(1)}, f32[8,256]{1,0:T(8,128)}, u32[]{:S(2)}) copy-start(f32[8,256]{1,0:T(8,128)} %param.11) | copy-start | bytes 24580
  25.3 21.1 %all-to-all-start.1 = ((f32[64,2,256]{2,1,0:T(2,128)}), f32[64,2,256]{2,1,0:T(2,128)S(1)}, u32[]{:S(2)}, u32[]{:S(2)}) async-start(f32[64,2,256]{2,1,0:T(2,128)} %reshape.85), calls=%async_computation.1 | async-start | bytes 262144 | tf_op jit(solution)/shard_map/all_to_all | solution.py:40
  47.8 15.8 %all-to-all-start.2 = ((f32[64,2,256]{2,1,0:T(2,128)}), f32[64,2,256]{2,1,0:T(2,128)S(1)}, u32[]{:S(2)}, u32[]{:S(2)}) async-start(f32[64,2,256]{2,1,0:T(2,128)} %reshape.87), calls=%async_computation.2 | async-start | bytes 262144 | tf_op jit(solution)/shard_map/all_to_all | solution.py:64
  64.4 40.9 %copy-start = (f32[32,256]{1,0:T(8,128)S(1)}, f32[32,256]{1,0:T(8,128)}, u32[]{:S(2)}) copy-start(f32[32,256]{1,0:T(8,128)} %param.12) | copy-start | bytes 98308
where the time goes:
time: 815 us; the launch traced here: 805 us
  blocking collectives  661 us (81%)
  matrix products  63.3 us (8%)
  starting transfers between devices  27.4 us (3%)
  waiting for transfers between devices  22.5 us (3%)
  local copies, waits for them, and re-layouts  14 us (2%)
  between operations  10.8 us (1%)
    psum x4, blocking collectives, squares(): return lax.psum(jnp.sum(vector * vector), ('orb', 'rep'))  293 us
    psum x3, blocking collectives, per_device(): curvature = lax.psum(jnp.sum(direction * image), ('orb', 'rep'))  218 us
    all_to_all x4, blocking collectives, deliver(): lax.all_to_all(outgoing.reshape(orbits, capacity, width), 'orb', split_ax...  67.9 us
    all_to_all x3, blocking collectives, per_device(): lax.all_to_all(pieces, 'orb', split_axis=0, concat_axis=0, tiled=True)  52.7 us
    dot_general x4, matrix products, per_device(): jnp.einsum('bsc,bc->bs', footprint.astype(jnp.float32), jnp.take(arrived....  31 us
    psum x4, blocking collectives, per_device(): lax.psum(partial_sums, 'rep')  28.8 us
    dot_general x5, matrix products, adjoint(): jnp.einsum('bsc,bs->bc', footprint.astype(jnp.float32), picked, precision...  26.9 us
  transfers between devices with their start and end apart: 3, of which 3 were waited for; matrix products, arithmetic and copies ran while one was open for 1% of the time, Pallas kernels for 0%

commit v1 on v0

v1 whole, which is shorter than its diff:
```python
import functools

import jax
import jax.numpy as jnp
from jax import lax
from jax.experimental import pallas as pl
from jax.experimental.pallas import tpu as pltpu
from jax.sharding import PartitionSpec as P

ITERS = 4
CAP = 2
LANES = 128
MSG = 2 * CAP + 1
SUB = 16
F32 = jnp.float32
BF16 = jnp.bfloat16


def lane_ids(shape):
    return lax.broadcasted_iota(jnp.int32, shape, len(shape) - 1)


def three_parts(values):
    high = values.astype(BF16)
    rest = values - high.astype(F32)
    middle = rest.astype(BF16)
    low = (rest - middle.astype(F32)).astype(BF16)
    return high, middle, low


def spread(packed, field_ref):
    rows, soundings, _ = field_ref.shape
    for group in range(soundings // 8):
        for row in range(rows):
            lane = rows * group + row
            field_ref[row, 8 * group : 8 * group + 8, :] = jnp.broadcast_to(
                packed[:, lane : lane + 1], (8, LANES)
            )


def transposed_products(footprint_ref, field_ref, out_ref, blocks, row_of, place_of):
    soundings = footprint_ref.shape[1]

    def body(block, carry):
        row = row_of(block)
        place = place_of(block)
        left = jnp.zeros((SUB, LANES), F32)
        right = jnp.zeros((SUB, LANES), F32)
        for start in range(0, soundings, SUB):
            part = footprint_ref[block, start : start + SUB, :].astype(F32)
            z = field_ref[row, start : start + SUB, :]
            left = left + part[:, :LANES] * z
            right = right + part[:, LANES:] * z
        out_ref[pl.ds(place, 1), :] = jnp.sum(left, axis=0, keepdims=True)
        out_ref[pl.ds(place + 1, 1), :] = jnp.sum(right, axis=0, keepdims=True)
        return carry

    lax.fori_loop(0, blocks, body, 0)


def start_kernel(rows_ref, cells_ref, packed_ref, footprint_ref, out_ref, meta_ref, field_ref, count_ref):
    blocks = rows_ref.shape[0]
    rows = field_ref.shape[0]
    orbits = out_ref.shape[0] // MSG
    cells = 32
    out_ref[...] = jnp.zeros_like(out_ref)
    spread(packed_ref[...], field_ref)

    def clear(owner, carry):
        count_ref[owner] = 0
        return carry

    lax.fori_loop(0, orbits, clear, 0)

    def place_block(block, carry):
        cell = cells_ref[block]
        owner = cell // cells
        slot = cell % cells
        rank = count_ref[owner]
        count_ref[owner] = rank + 1
        meta_ref[block] = owner * MSG + 2 * rank
        meta_ref[blocks + block] = rows_ref[block] % rows
        scalars = pl.ds(owner * MSG + 2 * CAP, 1)
        out_ref[scalars, :] = jnp.where(
            lane_ids((1, LANES)) == rank, (slot + 1).astype(F32), out_ref[scalars, :]
        )
        return carry

    lax.fori_loop(0, blocks, place_block, 0)
    transposed_products(
        footprint_ref, field_ref, out_ref, blocks, lambda b: meta_ref[blocks + b], lambda b: meta_ref[b]
    )


def serve(residual, pick, scalars, out_ref):
    orbits = out_ref.shape[0] // MSG
    high, middle, low = three_parts(residual)
    stacked = jnp.concatenate([high, middle, low, jnp.zeros_like(high)], axis=0)
    pieces = jnp.dot(pick, stacked, preferred_element_type=F32)
    for slot in range(CAP):
        for half in range(2):
            out_ref[pl.ds(2 * slot + half, orbits, stride=MSG), :] = pieces[
                slot * orbits : (slot + 1) * orbits, half * LANES : (half + 1) * LANES
            ]
    out_ref[pl.ds(2 * CAP, orbits, stride=MSG), :] = jnp.broadcast_to(scalars, (orbits, LANES))


def gathered(in_ref, collect):
    orbits = in_ref.shape[0] // MSG
    slots = [
        jnp.concatenate(
            [in_ref[pl.ds(2 * slot + half, orbits, stride=MSG), :] for half in range(2)], axis=1
        )
        for slot in range(CAP)
    ]
    high, middle, low = three_parts(jnp.concatenate(slots, axis=0))
    return jnp.dot(collect, jnp.concatenate([high, middle, low], axis=0), preferred_element_type=F32)


def row_of_scalars(values):
    lanes = lane_ids((1, LANES))
    row = jnp.zeros((1, LANES), F32)
    for lane, value in enumerate(values):
        row = jnp.where(lanes == lane, value, row)
    return row


def total(values):
    return jnp.sum(jnp.sum(values, axis=0, keepdims=True), axis=1, keepdims=True)


def first_owner_kernel(in_ref, prior_ref, residual_ref, out_ref, collect_ref, pick_ref):
    orbits = in_ref.shape[0] // MSG
    cells = prior_ref.shape[0]
    ids = in_ref[pl.ds(2 * CAP, orbits, stride=MSG), :]
    lanes = lane_ids((orbits, LANES)).astype(F32)
    pick = jnp.concatenate(
        [(ids[:, slot : slot + 1] == lanes + 1.0).astype(F32) for slot in range(CAP)], axis=0
    )
    pick = jnp.where(lane_ids(pick.shape) < cells, pick, 0.0)
    collect = pick.T[:cells, :]
    collect_ref[...] = jnp.concatenate([collect] * 3, axis=1).astype(BF16)
    folds = [pick[:, :cells]] * 3 + [jnp.zeros((pick.shape[0], LANES - 3 * cells), F32)]
    pick_ref[...] = jnp.concatenate(folds, axis=1).astype(BF16)
    residual = gathered(in_ref, collect_ref[...])
    residual_ref[...] = residual
    squares = residual * residual
    scalars = row_of_scalars([total(squares), total(prior_ref[...] * squares)])
    serve(residual, pick_ref[...], scalars, out_ref)


def owner_kernel(
    last, first, in_ref, scalars_ref, prior_ref, collect_ref, pick_ref, residual_ref, direction_ref,
    solution_ref, new_residual_ref, new_solution_ref, new_direction_ref=None, out_ref=None
):
    orbits = in_ref.shape[0] // MSG
    prior = prior_ref[...]
    norm = scalars_ref[0:1, 0:1]
    weighted = scalars_ref[0:1, 1:2]
    beta = scalars_ref[0:1, 2:3]
    forward = jnp.sum(in_ref[pl.ds(2 * CAP, orbits, stride=MSG), :], axis=0, keepdims=True)[:, 0:1]
    alpha = norm / (forward + weighted)
    residual = residual_ref[...]
    direction = residual if first else residual + beta * direction_ref[...]
    image = gathered(in_ref, collect_ref[...]) + prior * direction
    solution = alpha * direction if first else solution_ref[...] + alpha * direction
    residual = residual - alpha * image
    new_residual_ref[...] = residual
    new_solution_ref[...] = solution
    if not last:
        new_direction_ref[...] = direction
        scaled = prior * residual
        scalars = row_of_scalars(
            [total(residual * residual), total(scaled * residual), total(scaled * direction)]
        )
        serve(residual, pick_ref[...], scalars, out_ref)


def forward_kernel(meta_ref, in_ref, footprint_ref, out_ref, sums_ref):
    blocks = footprint_ref.shape[0]
    rows, soundings, _ = sums_ref.shape
    orbits = in_ref.shape[0] // MSG
    sums_ref[...] = jnp.zeros_like(sums_ref)

    def body(block, carry):
        place = meta_ref[block]
        row = meta_ref[blocks + block]
        left = jnp.broadcast_to(in_ref[pl.ds(place, 1), :], (SUB, LANES))
        right = jnp.broadcast_to(in_ref[pl.ds(place + 1, 1), :], (SUB, LANES))
        for start in range(0, soundings, SUB):
            part = footprint_ref[block, start : start + SUB, :].astype(F32)
            sums_ref[row, start : start + SUB, :] += part[:, :LANES] * left + part[:, LANES:] * right
        return carry

    lax.fori_loop(0, blocks, body, 0)
    lanes = lane_ids((8, LANES))
    per_half = LANES // rows
    halves = []
    for half in range(soundings // 8 // per_half):
        packed = jnp.zeros((8, LANES), F32)
        for at in range(per_half):
            group = half * per_half + at
            for row in range(rows):
                summed = jnp.sum(sums_ref[row, 8 * group : 8 * group + 8, :], axis=1, keepdims=True)
                packed = jnp.where(lanes == rows * at + row, summed, packed)
        halves.append(packed)
    scalars = jnp.sum(in_ref[pl.ds(2 * CAP, orbits, stride=MSG), :], axis=0, keepdims=True)
    halves.append(jnp.broadcast_to(scalars, (8, LANES)))
    message = jnp.concatenate(halves, axis=0)
    for peer in range(out_ref.shape[0]):
        out_ref[peer] = message


def adjoint_kernel(
    first, meta_ref, in_ref, weights_ref, footprint_ref, image_ref, scalars_ref,
    out_ref, new_image_ref, new_scalars_ref, field_ref
):
    blocks = footprint_ref.shape[0]
    orbits = out_ref.shape[0] // MSG
    summed = in_ref[0]
    for peer in range(1, in_ref.shape[0]):
        summed = summed + in_ref[peer]
    forward = jnp.concatenate([summed[0:8], summed[8:16]], axis=1)
    norm = summed[16:17, 0:1]
    weighted = summed[16:17, 1:2]
    beta = jnp.zeros((1, 1), F32)
    if not first:
        beta = norm / scalars_ref[0:1, 0:1]
        cross = summed[16:17, 2:3]
        weighted = weighted + 2.0 * beta * cross + beta * beta * scalars_ref[0:1, 1:2]
        forward = forward + beta * image_ref[...]
    new_image_ref[...] = forward
    new_scalars_ref[...] = jnp.broadcast_to(row_of_scalars([norm, weighted, beta]), (8, LANES))
    field = weights_ref[...] * forward
    out_ref[...] = jnp.zeros_like(out_ref)
    out_ref[pl.ds(2 * CAP, orbits, stride=MSG), :] = jnp.broadcast_to(
        row_of_scalars([total(field * forward)]), (orbits, LANES)
    )
    spread(field, field_ref)
    transposed_products(
        footprint_ref, field_ref, out_ref, blocks, lambda b: meta_ref[blocks + b], lambda b: meta_ref[b]
    )


def call(kernel, out_shape, kinds, out_kinds=None, scratch=()):
    spaces = {"v": pltpu.VMEM, "s": pltpu.SMEM}
    single = not isinstance(out_shape, (list, tuple))
    out_kinds = out_kinds or "v" * (1 if single else len(out_shape))
    out_specs = [pl.BlockSpec(memory_space=spaces[kind]) for kind in out_kinds]
    return pl.pallas_call(
        kernel,
        out_shape=out_shape,
        in_specs=[pl.BlockSpec(memory_space=spaces[kind]) for kind in kinds],
        out_specs=out_specs[0] if single else out_specs,
        scratch_shapes=list(scratch),
        compiler_params=pltpu.CompilerParams(vmem_limit_bytes=32 * 1024 * 1024),
    )


def per_device(observed, weights, precision_prior, footprint, block_rows, block_cells):
    rows, soundings = observed.shape
    cells, width = precision_prior.shape
    blocks = footprint.shape[0]
    orbits = lax.axis_size("orb")
    reps = lax.axis_size("rep")
    shape = jax.ShapeDtypeStruct
    messages = shape((orbits * MSG, LANES), F32)
    packed_shape = shape((8, soundings * rows // 8), F32)
    scalar_shape = shape((8, LANES), F32)
    region = shape((cells, width), F32)
    field = pltpu.VMEM((rows, soundings, LANES), F32)

    def pack(values):
        return values.reshape(rows, soundings // 8, 8).transpose(2, 1, 0).reshape(packed_shape.shape)

    def exchange(array):
        array = array.reshape(orbits, 1, MSG * LANES)
        array = lax.all_to_all(array, "orb", split_axis=0, concat_axis=0, tiled=True)
        return array.reshape(messages.shape)

    footprint = pltpu.with_memory_space_constraint(footprint, pltpu.VMEM)
    packed_weights = pack(weights)
    outgoing, meta = call(
        start_kernel,
        [messages, shape((2 * blocks,), jnp.int32)],
        "ssvv",
        "vs",
        [field, pltpu.SMEM((orbits,), jnp.int32)],
    )(block_rows, block_cells, pack(weights * observed), footprint)
    incoming = exchange(outgoing)
    residual, outgoing, collect, pick = call(
        first_owner_kernel,
        [
            region,
            messages,
            shape((cells, 3 * CAP * orbits), BF16),
            shape((CAP * orbits, LANES), BF16),
        ],
        "vv",
    )(incoming, precision_prior)
    direction = solution = residual
    image = jnp.zeros(packed_shape.shape, F32)
    scalars = jnp.zeros(scalar_shape.shape, F32)
    for iteration in range(ITERS):
        first, last = iteration == 0, iteration == ITERS - 1
        partial = call(
            forward_kernel,
            shape((reps, 24, LANES), F32),
            "svv",
            scratch=[field],
        )(meta, exchange(outgoing), footprint)
        partial = lax.all_to_all(partial, "rep", split_axis=0, concat_axis=0, tiled=True)
        outgoing, image, scalars = call(
            functools.partial(adjoint_kernel, first),
            [messages, packed_shape, scalar_shape],
            "svvvvv",
            scratch=[field],
        )(meta, partial, packed_weights, footprint, image, scalars)
        incoming = exchange(outgoing)
        results = call(
            functools.partial(owner_kernel, last, first),
            [region, region] if last else [region, region, region, messages],
            "vvvvvvvv",
        )(incoming, scalars, precision_prior, collect, pick, residual, direction, solution)
        residual, solution = results[:2]
        if not last:
            direction, outgoing = results[2:]
    return (solution, residual)


def solution(mesh):
    in_specs = (
        P("orb", None),
        P("orb", None),
        P("orb", "rep"),
        P("orb", None, "rep"),
        P("orb"),
        P("orb"),
    )
    out_specs = (P("orb", "rep"), P("orb", "rep"))
    return jax.shard_map(
        per_device, mesh=mesh, in_specs=in_specs, out_specs=out_specs, check_vma=False
    )
```

time: 815 us -> 222 us (0.27); the launches traced: 805 us -> 221 us
  blocking collectives: 661 us -> 175 us
  matrix products: 63.3 us -> 0 us
  Pallas kernels: 0 us -> 29.3 us
  starting transfers between devices: 27.4 us -> 4.18 us
  waiting for transfers between devices: 22.5 us -> 3.98 us
  between operations: 10.8 us -> 0.74 us
    psum x11 -> x0, blocking collectives: 540 us -> none  [the longest x4 293 us: squares(): return lax.psum(jnp.sum(vector * vector), ('orb', 'rep'))]
    dot_general x22 -> x0, matrix products: 63.3 us -> none  [the longest x4 31 us: per_device(): jnp.einsum('bsc,bc->bs', footprint.astype(jnp.float32), jnp.take(arrived....]
    all_to_all x7 -> x12, blocking collectives: 121 us -> 175 us  [the longest x9 154 us: exchange(): lax.all_to_all(array, 'orb', split_axis=0, concat_axis=0, tiled=True)]
    pallas_call x0 -> x14, Pallas kernels: none -> 29.3 us  [the longest x4 12.4 us: per_device(): call(functools.partial(adjoint_kernel, first), [messages, packed_shape, s...]
    all_to_all x3 -> x1, starting transfers between devices: 27.4 us -> 4.18 us  [per_device(): lax.all_to_all(partial, 'rep', split_axis=0, concat_axis=0, tiled=True)]
    all_to_all x3 -> x1, waiting for transfers between devices: 22.5 us -> 3.98 us  [per_device(): lax.all_to_all(partial, 'rep', split_axis=0, concat_axis=0, tiled=True)]
  transfers between devices with their start and end apart: 3 -> 1, of which waited for: 3 -> 1; matrix products, arithmetic and copies ran while one was open for 1% -> 0% of each run, Pallas kernels for 0% -> 0%
where the time goes in v1:
time: 222 us; the launch traced here: 221 us
  blocking collectives  175 us (79%)
  Pallas kernels  29.3 us (13%)
  local copies, waits for them, and re-layouts  7.66 us (3%)
  starting transfers between devices  4.18 us (2%)
  waiting for transfers between devices  3.98 us (2%)
    all_to_all x9, blocking collectives, exchange(): lax.all_to_all(array, 'orb', split_axis=0, concat_axis=0, tiled=True)  154 us
    all_to_all x3, blocking collectives, per_device(): lax.all_to_all(partial, 'rep', split_axis=0, concat_axis=0, tiled=True)  20.2 us
    pallas_call x4, Pallas kernels, per_device(): call(functools.partial(adjoint_kernel, first), [messages, packed_shape, s...  12.4 us
    pallas_call x4, Pallas kernels, per_device(): call(forward_kernel, shape((reps, 24, LANES), F32), 'svv', scratch=[field])  10.2 us
    unnamed x16, local copies, waits for them, and re-layouts  6.89 us
    pallas_call x1, Pallas kernels, per_device(): call(start_kernel, [messages, shape((2 * blocks,), jnp.int32)], 'ssvv', '...  4.57 us
  transfers between devices with their start and end apart: 1, of which 1 were waited for; matrix products, arithmetic and copies ran while one was open for 0% of the time, Pallas kernels for 0%

profile of v1, /device:TPU:1, one launch (start us, length us, event | category | flops | bytes accessed | tf_op | source)
XLA Modules:
  0.0 221.2 jit_solution(15941757700317172914)
XLA Ops:
  0.6 0.7 mul.3
  1.8 2.8 %copy-done = bf16[48,256,256]{2,1,0:T(8,128)(2,1)S(1)} copy-done((bf16[48,256,256]{2,1,0:T(8,128)(2,1)S(1)}, bf16[48,256,256]{2,1,0:T(8,128)(2,1)}, u32[]{:S(2)}) %copy-start) | copy-done | bytes 6291480
  4.5 0.7 copy-done.5
  5.2 0.7 copy-done.6
  5.9 4.6 %shard_map.77 = (f32[320,128]{1,0:T(8,128)S(1)}, s32[96]{0:T(128)S(1)}) custom-call(s32[48]{0:T(128)S(1)} %copy-done.5, s32[48]{0:T(128)S(1)} %copy-done.6, f32[8,256]{1,0:T(8,128)S(1)} %reshape.71.packed_ref, bf16[48,256,256]{2,1,0:T(8,128)(2,1)S(1)} %copy-done), custom_call_target="tpu_custom_call" | custom-call | tf_op jit(solution)/shard_map/pallas_call | solution.py:283
  10.4 24.5 %all_to_all.65 = f32[64,1,640]{2,1,0:T(1,128)S(1)} all-to-all(f32[64,1,640]{2,1,0:T(1,128)S(1)} %bitcast.37), channel_id=1, replica_groups=mesh['orb'=64,'rep'=4] {'orb'}, dimensions={0} | all-to-all | bytes 327680 | tf_op jit(solution)/shard_map/all_to_all | solution.py:278
  34.9 0.4 shard_map.78
  35.3 15.6 %all_to_all.66 = f32[64,1,640]{2,1,0:T(1,128)S(1)} all-to-all(f32[64,1,640]{2,1,0:T(1,128)S(1)} %bitcast.36), channel_id=1, replica_groups=mesh['orb'=64,'rep'=4] {'orb'}, dimensions={0} | all-to-all | bytes 327680 | tf_op jit(solution)/shard_map/all_to_all | solution.py:278
  51.0 3.0 %shard_map.79 = f32[4,24,128]{2,1,0:T(8,128)} custom-call(s32[96]{0:T(128)S(1)} %get-tuple-element.33.meta_ref, f32[320,128]{1,0:T(8,128)S(1)} %bitcast.20, bf16[48,256,256]{2,1,0:T(8,128)(2,1)S(1)} %copy-done.1), custom_call_target="tpu_custom_call" | custom-call | tf_op jit(solution)/shard_map/pallas_call | solution.py:306
  54.0 4.2 %all-to-all-start.2 = ((f32[4,24,128]{2,1,0:T(8,128)}), f32[4,24,128]{2,1,0:T(8,128)S(1)}, u32[]{:S(2)}, u32[]{:S(2)}) async-start(f32[4,24,128]{2,1,0:T(8,128)} %shard_map.79), calls=%async_computation.2 | async-start | bytes 98304 | tf_op jit(solution)/shard_map/all_to_all | solution.py:312
  58.6 4.0 %all-to-all-done.2.in_ref = f32[4,24,128]{2,1,0:T(8,128)S(1)} async-done(((f32[4,24,128]{2,1,0:T(8,128)}), f32[4,24,128]{2,1,0:T(8,128)S(1)}, u32[]{:S(2)}, u32[]{:S(2)}) %all-to-all-start.2) | async-done | bytes 49184 | tf_op jit(solution)/shard_map/all_to_all | solution.py:312
  62.6 2.8 %copy-done.2 = bf16[48,256,256]{2,1,0:T(8,128)(2,1)S(1)} copy-done((bf16[48,256,256]{2,1,0:T(8,128)(2,1)S(1)}, bf16[48,256,256]{2,1,0:T(8,128)(2,1)}, u32[]{:S(2)}) %copy-start.2) | copy-done | bytes 6291480
  65.4 2.9 %shard_map.80 = (f32[320,128]{1,0:T(8,128)S(1)}, f32[8,256]{1,0:T(8,128)S(1)}, f32[8,128]{1,0:T(8,128)S(1)}) custom-call(s32[96]{0:T(128)S(1)} %get-tuple-element.33.meta_ref, f32[4,24,128]{2,1,0:T(8,128)S(1)} %all-to-all-done.2.in_ref, f32[8,256]{1,0:T(8,128)S(1)} %reshape.77.weights_ref, bf16[48,256,256]{2,1,0:T(8,128)(2,1)S(1)} %copy-done.2, ...), custom_call_target="tpu_custom_call" | custom-call | tf_op jit(solution)/shard_map/pallas_call | solution.py:313
  68.3 17.0 %all_to_all.67 = f32[64,1,640]{2,1,0:T(1,128)S(1)} all-to-all(f32[64,1,640]{2,1,0:T(1,128)S(1)} %bitcast.32), channel_id=1, replica_groups=mesh['orb'=64,'rep'=4] {'orb'}, dimensions={0} | all-to-all | bytes 327680 | tf_op jit(solution)/shard_map/all_to_all | solution.py:278
  85.6 15.6 %all_to_all.68 = f32[64,1,640]{2,1,0:T(1,128)S(1)} all-to-all(f32[64,1,640]{2,1,0:T(1,128)S(1)} %bitcast.33), channel_id=1, replica_groups=mesh['orb'=64,'rep'=4] {'orb'}, dimensions={0} | all-to-all | bytes 327680 | tf_op jit(solution)/shard_map/all_to_all | solution.py:278
  101.2 2.4 %shard_map.82 = f32[4,24,128]{2,1,0:T(8,128)S(1)} custom-call(s32[96]{0:T(128)S(1)} %get-tuple-element.33.meta_ref, f32[320,128]{1,0:T(8,128)S(1)} %bitcast.21, bf16[48,256,256]{2,1,0:T(8,128)(2,1)S(1)} %copy-done.3), custom_call_target="tpu_custom_call" | custom-call | tf_op jit(solution)/shard_map/pallas_call | solution.py:306
  103.6 6.7 %all_to_all.69.in_ref = f32[4,24,128]{2,1,0:T(8,128)S(1)} all-to-all(f32[4,24,128]{2,1,0:T(8,128)S(1)} %shard_map.82), channel_id=1, replica_groups=mesh['orb'=64,'rep'=4] {'rep'}, dimensions={0} | all-to-all | bytes 98304 | tf_op jit(solution)/shard_map/all_to_all | solution.py:312
  110.4 3.0 %shard_map.83 = (f32[320,128]{1,0:T(8,128)S(1)}, f32[8,256]{1,0:T(8,128)S(1)}, f32[8,128]{1,0:T(8,128)S(1)}) custom-call(s32[96]{0:T(128)S(1)} %get-tuple-element.33.meta_ref, f32[4,24,128]{2,1,0:T(8,128)S(1)} %all_to_all.69.in_ref, f32[8,256]{1,0:T(8,128)S(1)} %reshape.77.weights_ref, bf16[48,256,256]{2,1,0:T(8,128)(2,1)S(1)} %copy-done.3, ...), custom_call_target="tpu_custom_call" | custom-call | tf_op jit(solution)/shard_map/pallas_call | solution.py:313
  113.3 16.8 %all_to_all.70 = f32[64,1,640]{2,1,0:T(1,128)S(1)} all-to-all(f32[64,1,640]{2,1,0:T(1,128)S(1)} %bitcast.34), channel_id=1, replica_groups=mesh['orb'=64,'rep'=4] {'orb'}, dimensions={0} | all-to-all | bytes 327680 | tf_op jit(solution)/shard_map/all_to_all | solution.py:278
  130.1 0.3 shard_map.84
  130.4 15.6 %all_to_all.71 = f32[64,1,640]{2,1,0:T(1,128)S(1)} all-to-all(f32[64,1,640]{2,1,0:T(1,128)S(1)} %bitcast.29), channel_id=1, replica_groups=mesh['orb'=64,'rep'=4] {'orb'}, dimensions={0} | all-to-all | bytes 327680 | tf_op jit(solution)/shard_map/all_to_all | solution.py:278
  146.0 2.4 %shard_map.85 = f32[4,24,128]{2,1,0:T(8,128)S(1)} custom-call(s32[96]{0:T(128)S(1)} %get-tuple-element.33.meta_ref, f32[320,128]{1,0:T(8,128)S(1)} %bitcast.22, bf16[48,256,256]{2,1,0:T(8,128)(2,1)S(1)} %copy-done.3), custom_call_target="tpu_custom_call" | custom-call | tf_op jit(solution)/shard_map/pallas_call | solution.py:306
  148.4 6.7 %all_to_all.72.in_ref = f32[4,24,128]{2,1,0:T(8,128)S(1)} all-to-all(f32[4,24,128]{2,1,0:T(8,128)S(1)} %shard_map.85), channel_id=1, replica_groups=mesh['orb'=64,'rep'=4] {'rep'}, dimensions={0} | all-to-all | bytes 98304 | tf_op jit(solution)/shard_map/all_to_all | solution.py:312
  155.2 3.0 %shard_map.86 = (f32[320,128]{1,0:T(8,128)S(1)}, f32[8,256]{1,0:T(8,128)S(1)}, f32[8,128]{1,0:T(8,128)S(1)}) custom-call(s32[96]{0:T(128)S(1)} %get-tuple-element.33.meta_ref, f32[4,24,128]{2,1,0:T(8,128)S(1)} %all_to_all.72.in_ref, f32[8,256]{1,0:T(8,128)S(1)} %reshape.77.weights_ref, bf16[48,256,256]{2,1,0:T(8,128)(2,1)S(1)} %copy-done.3, ...), custom_call_target="tpu_custom_call" | custom-call | tf_op jit(solution)/shard_map/pallas_call | solution.py:313
  158.1 16.8 %all_to_all.73 = f32[64,1,640]{2,1,0:T(1,128)S(1)} all-to-all(f32[64,1,640]{2,1,0:T(1,128)S(1)} %bitcast.35), channel_id=1, replica_groups=mesh['orb'=64,'rep'=4] {'orb'}, dimensions={0} | all-to-all | bytes 327680 | tf_op jit(solution)/shard_map/all_to_all | solution.py:278
  174.9 0.3 shard_map.87
  175.2 15.8 %all_to_all.74 = f32[64,1,640]{2,1,0:T(1,128)S(1)} all-to-all(f32[64,1,640]{2,1,0:T(1,128)S(1)} %bitcast.30), channel_id=1, replica_groups=mesh['orb'=64,'rep'=4] {'orb'}, dimensions={0} | all-to-all | bytes 327680 | tf_op jit(solution)/shard_map/all_to_all | solution.py:278
  191.0 2.4 %shard_map.88 = f32[4,24,128]{2,1,0:T(8,128)S(1)} custom-call(s32[96]{0:T(128)S(1)} %get-tuple-element.33.meta_ref, f32[320,128]{1,0:T(8,128)S(1)} %bitcast.23, bf16[48,256,256]{2,1,0:T(8,128)(2,1)S(1)} %copy-done.3), custom_call_target="tpu_custom_call" | custom-call | tf_op jit(solution)/shard_map/pallas_call | solution.py:306
  193.4 6.7 %all_to_all.75.in_ref = f32[4,24,128]{2,1,0:T(8,128)S(1)} all-to-all(f32[4,24,128]{2,1,0:T(8,128)S(1)} %shard_map.88), channel_id=1, replica_groups=mesh['orb'=64,'rep'=4] {'rep'}, dimensions={0} | all-to-all | bytes 98304 | tf_op jit(solution)/shard_map/all_to_all | solution.py:312
  200.1 3.5 %shard_map.89 = (f32[320,128]{1,0:T(8,128)S(1)}, f32[8,256]{1,0:T(8,128)}, f32[8,128]{1,0:T(8,128)S(1)}) custom-call(s32[96]{0:T(128)S(1)} %get-tuple-element.33.meta_ref, f32[4,24,128]{2,1,0:T(8,128)S(1)} %all_to_all.75.in_ref, f32[8,256]{1,0:T(8,128)S(1)} %reshape.77.weights_ref, bf16[48,256,256]{2,1,0:T(8,128)(2,1)S(1)} %copy-done.3, ...), custom_call_target="tpu_custom_call" | custom-call | tf_op jit(solution)/shard_map/pallas_call | solution.py:313
  203.7 16.7 %all_to_all.76 = f32[64,1,640]{2,1,0:T(1,128)S(1)} all-to-all(f32[64,1,640]{2,1,0:T(1,128)S(1)} %bitcast.31), channel_id=1, replica_groups=mesh['orb'=64,'rep'=4] {'orb'}, dimensions={0} | all-to-all | bytes 327680 | tf_op jit(solution)/shard_map/all_to_all | solution.py:278
  220.4 0.8 shard_map.90
  (21 shorter events, 1.1 us)
Async XLA Ops:
  0.6 34.3 %copy-start.4 = (f32[32,256]{1,0:T(8,128)S(1)}, f32[32,256]{1,0:T(8,128)}, u32[]{:S(2)}) copy-start(f32[32,256]{1,0:T(8,128)} %prior_ref.9) | copy-start | bytes 98308
  1.8 2.8 %copy-start = (bf16[48,256,256]{2,1,0:T(8,128)(2,1)S(1)}, bf16[48,256,256]{2,1,0:T(8,128)(2,1)}, u32[]{:S(2)}) copy-start(bf16[48,256,256]{2,1,0:T(8,128)(2,1)} %footprint_ref.17) | copy-start | bytes 18874372
  4.5 0.7 copy-start.5
  5.2 0.7 copy-start.6
  5.9 45.1 %copy-start.1 = (bf16[48,256,256]{2,1,0:T(8,128)(2,1)S(1)}, bf16[48,256,256]{2,1,0:T(8,128)(2,1)}, u32[]{:S(2)}) copy-start(bf16[48,256,256]{2,1,0:T(8,128)(2,1)} %footprint_ref.17) | copy-start | bytes 18874372
  5.9 52.3 %copy-start.7 = (f32[8,256]{1,0:T(8,128)S(1)}, f32[8,256]{1,0:T(8,128)}, u32[]{:S(2)}) copy-start(f32[8,256]{1,0:T(8,128)} %param.7) | copy-start | bytes 24580
  54.0 8.6 %all-to-all-start.2 = ((f32[4,24,128]{2,1,0:T(8,128)}), f32[4,24,128]{2,1,0:T(8,128)S(1)}, u32[]{:S(2)}, u32[]{:S(2)}) async-start(f32[4,24,128]{2,1,0:T(8,128)} %shard_map.79), calls=%async_computation.2 | async-start | bytes 98304 | tf_op jit(solution)/shard_map/all_to_all | solution.py:312
  62.6 2.8 %copy-start.2 = (bf16[48,256,256]{2,1,0:T(8,128)(2,1)S(1)}, bf16[48,256,256]{2,1,0:T(8,128)(2,1)}, u32[]{:S(2)}) copy-start(bf16[48,256,256]{2,1,0:T(8,128)(2,1)} %footprint_ref.17) | copy-start | bytes 18874372
  65.4 35.9 %copy-start.3 = (bf16[48,256,256]{2,1,0:T(8,128)(2,1)S(1)}, bf16[48,256,256]{2,1,0:T(8,128)(2,1)}, u32[]{:S(2)}) copy-start(bf16[48,256,256]{2,1,0:T(8,128)(2,1)} %footprint_ref.17) | copy-start | bytes 18874372

commit v2 on v1

--- a/solution.py
+++ b/solution.py
@@ -38,12 +38,13 @@
             )
 
 
-def transposed_products(footprint_ref, field_ref, out_ref, blocks, row_of, place_of):
+def transposed_products(footprint_ref, field_ref, out_ref, meta_ref, first, last, together=4):
     soundings = footprint_ref.shape[1]
-
-    def body(block, carry):
-        row = row_of(block)
-        place = place_of(block)
+    blocks = footprint_ref.shape[0]
+
+    def product(block):
+        row = meta_ref[blocks + block]
+        place = meta_ref[block]
         left = jnp.zeros((SUB, LANES), F32)
         right = jnp.zeros((SUB, LANES), F32)
         for start in range(0, soundings, SUB):
@@ -53,24 +54,72 @@
             right = right + part[:, LANES:] * z
         out_ref[pl.ds(place, 1), :] = jnp.sum(left, axis=0, keepdims=True)
         out_ref[pl.ds(place + 1, 1), :] = jnp.sum(right, axis=0, keepdims=True)
+
+    def body(step, carry):
+        for at in range(together):
+            product(first + step * together + at)
         return carry
 
-    lax.fori_loop(0, blocks, body, 0)
-
-
-def start_kernel(rows_ref, cells_ref, packed_ref, footprint_ref, out_ref, meta_ref, field_ref, count_ref):
-    blocks = rows_ref.shape[0]
-    rows = field_ref.shape[0]
+    lax.fori_loop(0, (last - first) // together, body, 0)
+
+
+def in_columns(values):
+    rows, soundings = values.shape
+    parts = []
+    for start in range(0, soundings, LANES):
+        part = values[:, start : start + LANES]
+        parts.append(jnp.concatenate([part] * (LANES // rows), axis=0).T)
+    return jnp.concatenate(parts, axis=0)
+
+
+def start_kernel(
+    cells, rows_hbm, cells_hbm, observed_hbm, weights_hbm, footprint_hbm,
+    out_ref, meta_ref, packed_ref, footprint_ref,
+    field_ref, count_ref, rows_ref, cells_ref, observed_ref, weights_ref, sems, chunk_sems
+):
+    blocks = footprint_ref.shape[0]
+    rows, soundings = weights_ref.shape
     orbits = out_ref.shape[0] // MSG
-    cells = 32
+    chunks = chunk_sems.shape[0]
+    size = blocks // chunks
+    small = [
+        pltpu.make_async_copy(source, target, sems.at[at])
+        for at, (source, target) in enumerate(
+            [
+                (rows_hbm, rows_ref),
+                (cells_hbm, cells_ref),
+                (observed_hbm, observed_ref),
+                (weights_hbm, weights_ref),
+            ]
+        )
+    ]
+    for copy in small:
+        copy.start()
+    large = []
+    for chunk in range(chunks):
+        span = pl.ds(chunk * size, size)
+        large.append(
+            pltpu.make_async_copy(footprint_hbm.at[span], footprint_ref.at[span], chunk_sems.at[chunk])
+        )
+        large[-1].start()
     out_ref[...] = jnp.zeros_like(out_ref)
-    spread(packed_ref[...], field_ref)
-
-    def clear(owner, carry):
+    for owner in range(orbits):
         count_ref[owner] = 0
-        return carry
-
-    lax.fori_loop(0, orbits, clear, 0)
+    for copy in small:
+        copy.wait()
+    weights = weights_ref[...]
+    columns = in_columns(weights * observed_ref[...])
+    for row in range(rows):
+        field_ref[row] = jnp.broadcast_to(columns[:, row : row + 1], (soundings, LANES))
+    columns = in_columns(weights)
+    groups = LANES // rows
+    lanes = lane_ids((8, LANES)) // rows
+    for half in range(soundings // LANES):
+        packed = jnp.zeros((8, LANES), F32)
+        for at in range(groups):
+            start = half * LANES + 8 * at
+            packed = jnp.where(lanes == at, columns[start : start + 8, :], packed)
+        packed_ref[:, half * LANES : (half + 1) * LANES] = packed
 
     def place_block(block, carry):
         cell = cells_ref[block]
@@ -87,9 +136,11 @@
         return carry
 
     lax.fori_loop(0, blocks, place_block, 0)
-    transposed_products(
-        footprint_ref, field_ref, out_ref, blocks, lambda b: meta_ref[blocks + b], lambda b: meta_ref[b]
-    )
+    for chunk in range(chunks):
+        large[chunk].wait()
+        transposed_products(
+            footprint_ref, field_ref, out_ref, meta_ref, chunk * size, (chunk + 1) * size
+        )
 
 
 def serve(residual, pick, scalars, out_ref):
@@ -215,7 +266,6 @@
     first, meta_ref, in_ref, weights_ref, footprint_ref, image_ref, scalars_ref,
     out_ref, new_image_ref, new_scalars_ref, field_ref
 ):
-    blocks = footprint_ref.shape[0]
     orbits = out_ref.shape[0] // MSG
     summed = in_ref[0]
     for peer in range(1, in_ref.shape[0]):
@@ -237,13 +287,11 @@
         row_of_scalars([total(field * forward)]), (orbits, LANES)
     )
     spread(field, field_ref)
-    transposed_products(
-        footprint_ref, field_ref, out_ref, blocks, lambda b: meta_ref[blocks + b], lambda b: meta_ref[b]
-    )
+    transposed_products(footprint_ref, field_ref, out_ref, meta_ref, 0, footprint_ref.shape[0])
 
 
 def call(kernel, out_shape, kinds, out_kinds=None, scratch=()):
-    spaces = {"v": pltpu.VMEM, "s": pltpu.SMEM}
+    spaces = {"v": pltpu.VMEM, "s": pltpu.SMEM, "h": pl.ANY}
     single = not isinstance(out_shape, (list, tuple))
     out_kinds = out_kinds or "v" * (1 if single else len(out_shape))
     out_specs = [pl.BlockSpec(memory_space=spaces[kind]) for kind in out_kinds]
@@ -270,23 +318,36 @@
     region = shape((cells, width), F32)
     field = pltpu.VMEM((rows, soundings, LANES), F32)
 
-    def pack(values):
-        return values.reshape(rows, soundings // 8, 8).transpose(2, 1, 0).reshape(packed_shape.shape)
-
     def exchange(array):
         array = array.reshape(orbits, 1, MSG * LANES)
         array = lax.all_to_all(array, "orb", split_axis=0, concat_axis=0, tiled=True)
         return array.reshape(messages.shape)
 
-    footprint = pltpu.with_memory_space_constraint(footprint, pltpu.VMEM)
-    packed_weights = pack(weights)
-    outgoing, meta = call(
-        start_kernel,
-        [messages, shape((2 * blocks,), jnp.int32)],
-        "ssvv",
-        "vs",
-        [field, pltpu.SMEM((orbits,), jnp.int32)],
-    )(block_rows, block_cells, pack(weights * observed), footprint)
+    in_hbm = [
+        pltpu.with_memory_space_constraint(array, pltpu.HBM)
+        for array in (block_rows, block_cells, observed, weights, footprint)
+    ]
+    outgoing, meta, packed_weights, footprint = call(
+        functools.partial(start_kernel, cells),
+        [
+            messages,
+            pltpu.SMEM((2 * blocks,), jnp.int32),
+            packed_shape,
+            pltpu.VMEM(footprint.shape, footprint.dtype),
+        ],
+        "hhhhh",
+        "vsvv",
+        [
+            field,
+            pltpu.SMEM((orbits,), jnp.int32),
+            pltpu.SMEM((blocks,), jnp.int32),
+            pltpu.SMEM((blocks,), jnp.int32),
+            pltpu.VMEM(observed.shape, F32),
+            pltpu.VMEM(weights.shape, F32),
+            pltpu.SemaphoreType.DMA((4,)),
+            pltpu.SemaphoreType.DMA((6,)),
+        ],
+    )(*in_hbm)
     incoming = exchange(outgoing)
     residual, outgoing, collect, pick = call(
         first_owner_kernel,

time: 222 us -> 207 us (0.932)
  blocking collectives: 175 us -> 183 us
  local copies, waits for them, and re-layouts: 7.66 us -> 0.01 us
  Pallas kernels: 29.3 us -> 23.1 us
  starting transfers between devices: 4.18 us -> 0 us
  waiting for transfers between devices: 3.98 us -> 0 us
    all_to_all x3 -> x4, blocking collectives: 20.2 us -> 28.6 us  [per_device(): lax.all_to_all(partial, 'rep', split_axis=0, concat_axis=0, tiled=True)]
    unnamed x16 -> x2, local copies, waits for them, and re-layouts: 6.89 us -> 0.01 us
    all_to_all x1 -> x0, starting transfers between devices: 4.18 us -> none  [per_device(): lax.all_to_all(partial, 'rep', split_axis=0, concat_axis=0, tiled=True)]
    all_to_all x1 -> x0, waiting for transfers between devices: 3.98 us -> none  [per_device(): lax.all_to_all(partial, 'rep', split_axis=0, concat_axis=0, tiled=True)]
    pallas_call x4, Pallas kernels: 12.4 us -> 8.47 us  [per_device(): call(functools.partial(adjoint_kernel, first), [messages, packed_shape, s...]
    pallas_call x4, Pallas kernels: 10.2 us -> 7.38 us  [per_device(): call(forward_kernel, shape((reps, 24, LANES), F32), 'svv', scratch=[field])]
  transfers between devices with their start and end apart: 1 -> 0, of which waited for: 1 -> 0; matrix products, arithmetic and copies ran while one was open for 0% -> 0% of each run, Pallas kernels for 0% -> 0%
where the time goes in v2:
time: 207 us
  blocking collectives  183 us (88%)
  Pallas kernels  23.1 us (11%)
    all_to_all x9, blocking collectives, exchange(): lax.all_to_all(array, 'orb', split_axis=0, concat_axis=0, tiled=True)  154 us
    all_to_all x4, blocking collectives, per_device(): lax.all_to_all(partial, 'rep', split_axis=0, concat_axis=0, tiled=True)  28.6 us
    pallas_call x4, Pallas kernels, per_device(): call(functools.partial(adjoint_kernel, first), [messages, packed_shape, s...  8.47 us
    pallas_call x4, Pallas kernels, per_device(): call(forward_kernel, shape((reps, 24, LANES), F32), 'svv', scratch=[field])  7.38 us
    pallas_call x1, Pallas kernels, per_device(): call(functools.partial(start_kernel, cells), [messages, pltpu.SMEM((2 * b...  5.04 us

profile of v2, /device:TPU:1, one launch (start us, length us, event | category | flops | bytes accessed | tf_op | source)
XLA Modules:
  0.0 206.6 jit_solution(13261478095232454083)
XLA Ops:
  0.6 0.0 copy-start
  0.6 5.0 %shard_map.77 = (f32[320,128]{1,0:T(8,128)S(1)}, s32[96]{0:T(128)S(4)}, f32[8,256]{1,0:T(8,128)S(1)}, bf16[48,256,256]{2,1,0:T(8,128)(2,1)S(1)}) custom-call(s32[48]{0:T(128)} %rows_hbm.1, s32[48]{0:T(128)} %cells_hbm.1, f32[8,256]{1,0:T(8,128)} %observed_hbm.1, f32[8,256]{1,0:T(8,128)} %weights_hbm.1, bf16[48,256,256]{2,1,0:T(8,128)(2,1)} %footprint_hbm.1), custom_call_target="tpu_custom_call" | custom-call | tf_op jit(solution)/shard_map/pallas_call | solution.py:330
  5.7 24.5 %all_to_all.65 = f32[64,1,640]{2,1,0:T(1,128)S(1)} all-to-all(f32[64,1,640]{2,1,0:T(1,128)S(1)} %bitcast.35), channel_id=1, replica_groups=mesh['orb'=64,'rep'=4] {'orb'}, dimensions={0} | all-to-all | bytes 327680 | tf_op jit(solution)/shard_map/all_to_all | solution.py:323
  30.2 0.0 copy-done
  30.2 0.4 shard_map.78
  30.6 15.6 %all_to_all.66 = f32[64,1,640]{2,1,0:T(1,128)S(1)} all-to-all(f32[64,1,640]{2,1,0:T(1,128)S(1)} %bitcast.34), channel_id=1, replica_groups=mesh['orb'=64,'rep'=4] {'orb'}, dimensions={0} | all-to-all | bytes 327680 | tf_op jit(solution)/shard_map/all_to_all | solution.py:323
  46.2 1.8 shard_map.79
  48.0 8.4 %all_to_all.67.in_ref = f32[4,24,128]{2,1,0:T(8,128)S(1)} all-to-all(f32[4,24,128]{2,1,0:T(8,128)S(1)} %shard_map.79), channel_id=1, replica_groups=mesh['orb'=64,'rep'=4] {'rep'}, dimensions={0} | all-to-all | bytes 98304 | tf_op jit(solution)/shard_map/all_to_all | solution.py:373
  56.4 2.0 shard_map.80
  58.4 17.0 %all_to_all.68 = f32[64,1,640]{2,1,0:T(1,128)S(1)} all-to-all(f32[64,1,640]{2,1,0:T(1,128)S(1)} %bitcast.30), channel_id=1, replica_groups=mesh['orb'=64,'rep'=4] {'orb'}, dimensions={0} | all-to-all | bytes 327680 | tf_op jit(solution)/shard_map/all_to_all | solution.py:323
  75.4 0.3 shard_map.81
  75.8 15.6 %all_to_all.69 = f32[64,1,640]{2,1,0:T(1,128)S(1)} all-to-all(f32[64,1,640]{2,1,0:T(1,128)S(1)} %bitcast.31), channel_id=1, replica_groups=mesh['orb'=64,'rep'=4] {'orb'}, dimensions={0} | all-to-all | bytes 327680 | tf_op jit(solution)/shard_map/all_to_all | solution.py:323
  91.4 1.8 shard_map.82
  93.2 6.7 %all_to_all.70.in_ref = f32[4,24,128]{2,1,0:T(8,128)S(1)} all-to-all(f32[4,24,128]{2,1,0:T(8,128)S(1)} %shard_map.82), channel_id=1, replica_groups=mesh['orb'=64,'rep'=4] {'rep'}, dimensions={0} | all-to-all | bytes 98304 | tf_op jit(solution)/shard_map/all_to_all | solution.py:373
  100.0 2.0 shard_map.83
  102.0 16.8 %all_to_all.71 = f32[64,1,640]{2,1,0:T(1,128)S(1)} all-to-all(f32[64,1,640]{2,1,0:T(1,128)S(1)} %bitcast.32), channel_id=1, replica_groups=mesh['orb'=64,'rep'=4] {'orb'}, dimensions={0} | all-to-all | bytes 327680 | tf_op jit(solution)/shard_map/all_to_all | solution.py:323
  118.7 0.3 shard_map.84
  119.0 15.6 %all_to_all.72 = f32[64,1,640]{2,1,0:T(1,128)S(1)} all-to-all(f32[64,1,640]{2,1,0:T(1,128)S(1)} %bitcast.28), channel_id=1, replica_groups=mesh['orb'=64,'rep'=4] {'orb'}, dimensions={0} | all-to-all | bytes 327680 | tf_op jit(solution)/shard_map/all_to_all | solution.py:323
  134.6 1.8 shard_map.85
  136.5 6.7 %all_to_all.73.in_ref = f32[4,24,128]{2,1,0:T(8,128)S(1)} all-to-all(f32[4,24,128]{2,1,0:T(8,128)S(1)} %shard_map.85), channel_id=1, replica_groups=mesh['orb'=64,'rep'=4] {'rep'}, dimensions={0} | all-to-all | bytes 98304 | tf_op jit(solution)/shard_map/all_to_all | solution.py:373
  143.2 2.0 shard_map.86
  145.2 16.8 %all_to_all.74 = f32[64,1,640]{2,1,0:T(1,128)S(1)} all-to-all(f32[64,1,640]{2,1,0:T(1,128)S(1)} %bitcast.33), channel_id=1, replica_groups=mesh['orb'=64,'rep'=4] {'orb'}, dimensions={0} | all-to-all | bytes 327680 | tf_op jit(solution)/shard_map/all_to_all | solution.py:323
  162.0 0.3 shard_map.87
  162.3 15.6 %all_to_all.75 = f32[64,1,640]{2,1,0:T(1,128)S(1)} all-to-all(f32[64,1,640]{2,1,0:T(1,128)S(1)} %bitcast.29), channel_id=1, replica_groups=mesh['orb'=64,'rep'=4] {'orb'}, dimensions={0} | all-to-all | bytes 327680 | tf_op jit(solution)/shard_map/all_to_all | solution.py:323
  177.9 1.8 shard_map.88
  179.8 6.7 %all_to_all.76.in_ref = f32[4,24,128]{2,1,0:T(8,128)S(1)} all-to-all(f32[4,24,128]{2,1,0:T(8,128)S(1)} %shard_map.88), channel_id=1, replica_groups=mesh['orb'=64,'rep'=4] {'rep'}, dimensions={0} | all-to-all | bytes 98304 | tf_op jit(solution)/shard_map/all_to_all | solution.py:373
  186.5 2.5 %shard_map.89 = (f32[320,128]{1,0:T(8,128)S(1)}, f32[8,256]{1,0:T(8,128)}, f32[8,128]{1,0:T(8,128)S(1)}) custom-call(s32[96]{0:T(128)S(4)} %get-tuple-element.35.meta_ref, f32[4,24,128]{2,1,0:T(8,128)S(1)} %all_to_all.76.in_ref, f32[8,256]{1,0:T(8,128)S(1)} %get-tuple-element.39.weights_ref, bf16[48,256,256]{2,1,0:T(8,128)(2,1)S(1)} %get-tuple-element.38.footprint_ref, ...), custom_call_target="tpu_custom_call" | custom-call | tf_op jit(solution)/shard_map/pallas_call | solution.py:374
  189.0 16.7 %all_to_all.77 = f32[64,1,640]{2,1,0:T(1,128)S(1)} all-to-all(f32[64,1,640]{2,1,0:T(1,128)S(1)} %bitcast.27), channel_id=1, replica_groups=mesh['orb'=64,'rep'=4] {'orb'}, dimensions={0} | all-to-all | bytes 327680 | tf_op jit(solution)/shard_map/all_to_all | solution.py:323
  205.8 0.8 shard_map.90
  (2 shorter events, 0.0 us)
Async XLA Ops:
  0.6 29.5 %copy-start = (f32[32,256]{1,0:T(8,128)S(1)}, f32[32,256]{1,0:T(8,128)}, u32[]{:S(2)}) copy-start(f32[32,256]{1,0:T(8,128)} %prior_ref.9) | copy-start | bytes 98308

commit v3 on v2

v3 whole, which is shorter than its diff:
```python
import functools

import jax
import jax.numpy as jnp
from jax import lax
from jax.experimental import pallas as pl
from jax.experimental.pallas import tpu as pltpu
from jax.sharding import PartitionSpec as P

ITERS = 4
CORES = 2
CAP = 2 * CORES
FETCH = 2 * CAP
DELIVER = FETCH + 1
LANES = 128
SUB = 16
F32 = jnp.float32
BF16 = jnp.bfloat16


def lane_ids(shape):
    return lax.broadcasted_iota(jnp.int32, shape, len(shape) - 1)


def three_parts(values):
    high = values.astype(BF16)
    rest = values - high.astype(F32)
    middle = rest.astype(BF16)
    low = (rest - middle.astype(F32)).astype(BF16)
    return high, middle, low


def spread(packed, field_ref):
    rows, soundings, _ = field_ref.shape
    for group in range(soundings // 8):
        for row in range(rows):
            lane = rows * group + row
            field_ref[row, 8 * group : 8 * group + 8, :] = jnp.broadcast_to(
                packed[:, lane : lane + 1], (8, LANES)
            )


def transposed_product(footprint_ref, field_ref, out_ref, block, row, place):
    soundings = footprint_ref.shape[1]
    left = jnp.zeros((SUB, LANES), F32)
    right = jnp.zeros((SUB, LANES), F32)
    for start in range(0, soundings, SUB):
        part = footprint_ref[block, start : start + SUB, :].astype(F32)
        z = field_ref[row, start : start + SUB, :]
        left = left + part[:, :LANES] * z
        right = right + part[:, LANES:] * z
    out_ref[pl.ds(place, 1), :] = jnp.sum(left, axis=0, keepdims=True)
    out_ref[pl.ds(place + 1, 1), :] = jnp.sum(right, axis=0, keepdims=True)


def each(first, last, together, do):
    def body(step, carry):
        for at in range(together):
            do(first + step * together + at)
        return carry

    lax.fori_loop(0, (last - first) // together, body, 0)


def in_columns(values):
    rows, soundings = values.shape
    parts = []
    for start in range(0, soundings, LANES):
        part = values[:, start : start + LANES]
        parts.append(jnp.concatenate([part] * (LANES // rows), axis=0).T)
    return jnp.concatenate(parts, axis=0)


def start_kernel(
    cells, rows_hbm, cells_hbm, observed_hbm, weights_hbm, footprint_hbm,
    out_ref, meta_ref, packed_ref, footprint_ref,
    field_ref, count_ref, rows_ref, cells_ref, observed_ref, weights_ref, sems, chunk_sems
):
    blocks = footprint_ref.shape[0]
    rows, soundings = weights_ref.shape
    peers = out_ref.shape[0] // DELIVER
    chunks = chunk_sems.shape[0]
    size = blocks // chunks
    small = [
        pltpu.make_async_copy(source, target, sems.at[at])
        for at, (source, target) in enumerate(
            [
                (rows_hbm, rows_ref),
                (cells_hbm, cells_ref),
                (observed_hbm, observed_ref),
                (weights_hbm, weights_ref),
            ]
        )
    ]
    for copy in small:
        copy.start()
    large = []
    for chunk in range(chunks):
        span = pl.ds(chunk * size, size)
        large.append(
            pltpu.make_async_copy(footprint_hbm.at[span], footprint_ref.at[span], chunk_sems.at[chunk])
        )
        large[-1].start()
    out_ref[...] = jnp.zeros_like(out_ref)
    for peer in range(peers):
        count_ref[peer] = 0
    for copy in small:
        copy.wait()
    weights = weights_ref[...]
    columns = in_columns(weights * observed_ref[...])
    for row in range(rows):
        field_ref[row] = jnp.broadcast_to(columns[:, row : row + 1], (soundings, LANES))
    columns = in_columns(weights)
    groups = LANES // rows
    lanes = lane_ids((8, LANES)) // rows
    for half in range(soundings // LANES):
        packed = jnp.zeros((8, LANES), F32)
        for at in range(groups):
            start = half * LANES + 8 * at
            packed = jnp.where(lanes == at, columns[start : start + 8, :], packed)
        packed_ref[:, half * LANES : (half + 1) * LANES] = packed

    def product(block):
        cell = cells_ref[block]
        peer = cell // cells
        slot = cell % cells
        rank = count_ref[peer]
        count_ref[peer] = rank + 1
        row = rows_ref[block] % rows
        place = peer * DELIVER + 2 * rank
        meta_ref[block] = place
        meta_ref[blocks + block] = row
        meta_ref[2 * blocks + block] = peer * FETCH + 2 * rank
        scalars = pl.ds(peer * DELIVER + FETCH, 1)
        out_ref[scalars, :] = jnp.where(
            lane_ids((1, LANES)) == rank, (slot + 1).astype(F32), out_ref[scalars, :]
        )
        transposed_product(footprint_ref, field_ref, out_ref, block, row, place)

    for chunk in range(chunks):
        large[chunk].wait()
        each(chunk * size, (chunk + 1) * size, 4, product)


def serve(residual, pick, out_ref):
    peers = out_ref.shape[0] // FETCH
    high, middle, low = three_parts(residual)
    stacked = jnp.concatenate([high, middle, low, jnp.zeros_like(high)], axis=0)
    pieces = jnp.dot(pick, stacked, preferred_element_type=F32)
    for slot in range(CAP):
        for half in range(2):
            out_ref[pl.ds(2 * slot + half, peers, stride=FETCH), :] = pieces[
                slot * peers : (slot + 1) * peers, half * LANES : (half + 1) * LANES
            ]


def gathered(in_ref, collect):
    peers = in_ref.shape[0] // DELIVER
    slots = [
        jnp.concatenate(
            [in_ref[pl.ds(2 * slot + half, peers, stride=DELIVER), :] for half in range(2)], axis=1
        )
        for slot in range(CAP)
    ]
    high, middle, low = three_parts(jnp.concatenate(slots, axis=0))
    return jnp.dot(collect, jnp.concatenate([high, middle, low], axis=0), preferred_element_type=F32)


def arrived_scalars(in_ref):
    peers = in_ref.shape[0] // DELIVER
    row = jnp.sum(in_ref[pl.ds(FETCH, peers, stride=DELIVER), :], axis=0, keepdims=True)
    return jnp.broadcast_to(row, (8, LANES))


def row_of_scalars(values):
    lanes = lane_ids((8, LANES))
    row = jnp.zeros((8, LANES), F32)
    for lane, value in enumerate(values):
        row = jnp.where(lanes == lane, value, row)
    return row


def total(values):
    return jnp.sum(jnp.sum(values, axis=0, keepdims=True), axis=1, keepdims=True)


def first_gather_kernel(in_ref, prior_ref, half_ref, collect_ref, pick_ref):
    peers = in_ref.shape[0] // DELIVER
    own, width = prior_ref.shape
    cells = CORES * own
    ids = in_ref[pl.ds(FETCH, peers, stride=DELIVER), :]
    lanes = lane_ids((peers, LANES)).astype(F32)
    pick = jnp.concatenate(
        [(ids[:, slot : slot + 1] == lanes + 1.0).astype(F32) for slot in range(CAP)], axis=0
    )
    pick = jnp.where(lane_ids(pick.shape) < cells, pick, 0.0)
    collect = jnp.concatenate([pick.T[:cells, :]] * 3, axis=1).astype(BF16)
    collect_ref[...] = collect
    folds = [pick[:, :cells]] * 3 + [jnp.zeros((pick.shape[0], cells), F32)]
    pick_ref[...] = jnp.concatenate(folds, axis=1).astype(BF16)
    half_ref[0:cells, :] = gathered(in_ref, collect)
    half_ref[cells : cells + own, :] = prior_ref[...]


def gather_kernel(in_ref, collect_ref, half_ref):
    cells = collect_ref.shape[0]
    half_ref[0:cells, :] = gathered(in_ref, collect_ref[...])
    scalars = arrived_scalars(in_ref)
    half_ref[cells : cells + 8, :] = jnp.concatenate([scalars, jnp.zeros_like(scalars)], axis=1)


def partial_sums(prior, residual, direction=None):
    values = [0.5 * residual * residual, 0.5 * prior * residual * residual]
    if direction is not None:
        values.append(0.5 * prior * residual * direction)
    return row_of_scalars([total(value) for value in values])


def first_update_kernel(mine_ref, other_ref, pick_ref, prior_ref, residual_ref, sums_ref, out_ref):
    cells = residual_ref.shape[0]
    own = cells // CORES
    first = lax.axis_index("orb") % CORES == 0
    mine = mine_ref[cells : cells + own, :]
    other = other_ref[cells : cells + own, :]
    prior = jnp.concatenate([jnp.where(first, mine, other), jnp.where(first, other, mine)], axis=0)
    prior_ref[...] = prior
    residual = mine_ref[0:cells, :] + other_ref[0:cells, :]
    residual_ref[...] = residual
    sums_ref[...] = partial_sums(prior, residual)
    serve(residual, pick_ref[...], out_ref)


def update_kernel(first, last, *refs):
    mine_ref, other_ref, pick_ref, prior_ref, residual_ref, *refs = refs
    if not first:
        state_ref, direction_ref, image_ref, solution_ref, *refs = refs
    cells = residual_ref.shape[0]
    sums = mine_ref[cells : cells + 1, :] + other_ref[cells : cells + 1, :]
    norm, prior_rr, prior_rd, forward_rr, forward_rd = [sums[:, at : at + 1] for at in range(5)]
    prior = prior_ref[...]
    residual = residual_ref[...]
    image = mine_ref[0:cells, :] + other_ref[0:cells, :] + prior * residual
    beta = jnp.zeros((1, 1), F32)
    direction, prior_dd, forward_dd = residual, prior_rr, forward_rr
    if not first:
        beta = norm / state_ref[0:1, 0:1]
        prior_dd = prior_rr + beta * (2.0 * prior_rd + beta * state_ref[0:1, 1:2])
        forward_dd = forward_rr + beta * (2.0 * forward_rd + beta * state_ref[0:1, 2:3])
        direction = residual + beta * direction_ref[...]
        image = image + beta * image_ref[...]
    alpha = norm / (prior_dd + forward_dd)
    solution = alpha * direction if first else solution_ref[...] + alpha * direction
    residual = residual - alpha * image
    if last:
        new_solution_ref, new_residual_ref = refs
        own = cells // CORES
        core_first = lax.axis_index("orb") % CORES == 0
        new_solution_ref[...] = jnp.where(core_first, solution[:own], solution[own:])
        new_residual_ref[...] = jnp.where(core_first, residual[:own], residual[own:])
        return
    new_residual_ref, sums_ref, out_ref, new_state_ref, new_direction_ref, new_image_ref, new_solution_ref = refs
    serve(residual, pick_ref[...], out_ref)
    sums_ref[...] = partial_sums(prior, residual, direction)
    new_residual_ref[...] = residual
    new_state_ref[...] = row_of_scalars([norm, prior_dd, forward_dd, beta])
    new_direction_ref[...] = direction
    new_image_ref[...] = image
    new_solution_ref[...] = solution


def forward_kernel(meta_ref, in_ref, scalars_ref, footprint_ref, out_ref, sums_ref):
    blocks = footprint_ref.shape[0]
    rows, soundings, _ = sums_ref.shape
    sums_ref[...] = jnp.zeros_like(sums_ref)

    def product(block):
        row = meta_ref[blocks + block]
        place = meta_ref[2 * blocks + block]
        left = jnp.broadcast_to(in_ref[pl.ds(place, 1), :], (SUB, LANES))
        right = jnp.broadcast_to(in_ref[pl.ds(place + 1, 1), :], (SUB, LANES))
        for start in range(0, soundings, SUB):
            part = footprint_ref[block, start : start + SUB, :].astype(F32)
            sums_ref[row, start : start + SUB, :] += part[:, :LANES] * left + part[:, LANES:] * right

    each(0, blocks, 4, product)
    lanes = lane_ids((8, LANES))
    per_half = LANES // rows
    halves = []
    for half in range(soundings // 8 // per_half):
        packed = [jnp.zeros((8, LANES), F32) for _ in range(4)]
        for at in range(per_half):
            group = half * per_half + at
            for row in range(rows):
                summed = jnp.sum(sums_ref[row, 8 * group : 8 * group + 8, :], axis=1, keepdims=True)
                packed[row % 4] = jnp.where(lanes == rows * at + row, summed, packed[row % 4])
        halves.append((packed[0] + packed[1]) + (packed[2] + packed[3]))
    halves.append(scalars_ref[...])
    message = jnp.concatenate(halves, axis=0)
    for peer in range(out_ref.shape[0]):
        out_ref[peer] = message


def adjoint_kernel(iteration, last, *refs):
    meta_ref, in_ref, weights_ref, footprint_ref, *refs = refs
    if iteration > 0:
        state_ref, old_ref, *refs = refs
    if iteration > 1:
        older_ref, *refs = refs
    out_ref, *refs = refs
    blocks = footprint_ref.shape[0]
    peers = out_ref.shape[0] // DELIVER
    summed = in_ref[0]
    for peer in range(1, in_ref.shape[0]):
        summed = summed + in_ref[peer]
    forward = jnp.concatenate([summed[0:8], summed[8:16]], axis=1)
    field = weights_ref[...] * forward
    *refs, field_ref = refs
    out_ref[...] = jnp.zeros_like(out_ref)
    spread(field, field_ref)
    lanes = lane_ids((8, LANES))
    scalars = jnp.where(lanes == 3, total(field * forward), summed[16:24])
    if iteration > 0:
        direction = old_ref[...]
        if iteration > 1:
            direction = direction + state_ref[0:1, 3:4] * older_ref[...]
        scalars = jnp.where(lanes == 4, total(field * direction), scalars)
    if not last:
        refs[0][...] = forward
        if iteration > 0:
            refs[1][...] = direction
    out_ref[pl.ds(FETCH, peers, stride=DELIVER), :] = jnp.broadcast_to(scalars[0:1], (peers, LANES))

    def product(block):
        transposed_product(
            footprint_ref, field_ref, out_ref, block, meta_ref[blocks + block], meta_ref[block]
        )

    each(0, blocks, 4, product)


def call(kernel, out_shape, kinds, out_kinds=None, scratch=()):
    spaces = {"v": pltpu.VMEM, "s": pltpu.SMEM, "h": pl.ANY}
    out_kinds = out_kinds or "v" * len(out_shape)
    return pl.pallas_call(
        kernel,
        out_shape=out_shape,
        in_specs=[pl.BlockSpec(memory_space=spaces[kind]) for kind in kinds],
        out_specs=[pl.BlockSpec(memory_space=spaces[kind]) for kind in out_kinds],
        scratch_shapes=list(scratch),
        compiler_params=pltpu.CompilerParams(vmem_limit_bytes=32 * 1024 * 1024),
    )


def per_device(observed, weights, precision_prior, footprint, block_rows, block_cells):
    rows, soundings = observed.shape
    own, width = precision_prior.shape
    cells = CORES * own
    blocks = footprint.shape[0]
    orbits = lax.axis_size("orb")
    reps = lax.axis_size("rep")
    peers = orbits // CORES
    shape = jax.ShapeDtypeStruct
    fetched = shape((peers * FETCH, LANES), F32)
    delivered = shape((peers * DELIVER, LANES), F32)
    packed_shape = shape((8, soundings * rows // 8), F32)
    scalar_shape = shape((8, LANES), F32)
    region = shape((cells, width), F32)
    field = pltpu.VMEM((rows, soundings, LANES), F32)
    same_core = [[CORES * peer + core for peer in range(peers)] for core in range(CORES)]
    swapped = [(device, device ^ 1) for device in range(orbits)]

    def exchange(array):
        flat = array.reshape(peers, 1, array.shape[0] // peers * LANES)
        flat = lax.all_to_all(
            flat, "orb", split_axis=0, concat_axis=0, axis_index_groups=same_core, tiled=True
        )
        return flat.reshape(array.shape)

    def swap(array):
        return lax.ppermute(array, "orb", swapped)

    in_hbm = [
        pltpu.with_memory_space_constraint(array, pltpu.HBM)
        for array in (block_rows, block_cells, observed, weights, footprint)
    ]
    outgoing, meta, packed_weights, footprint = call(
        functools.partial(start_kernel, cells),
        [
            delivered,
            pltpu.SMEM((3 * blocks,), jnp.int32),
            packed_shape,
            pltpu.VMEM(footprint.shape, footprint.dtype),
        ],
        "hhhhh",
        "vsvv",
        [
            field,
            pltpu.SMEM((peers,), jnp.int32),
            pltpu.SMEM((blocks,), jnp.int32),
            pltpu.SMEM((blocks,), jnp.int32),
            pltpu.VMEM(observed.shape, F32),
            pltpu.VMEM(weights.shape, F32),
            pltpu.SemaphoreType.DMA((4,)),
            pltpu.SemaphoreType.DMA((6,)),
        ],
    )(*in_hbm)
    half, collect, pick = call(
        first_gather_kernel,
        [
            shape((cells + own, width), F32),
            shape((cells, 3 * CAP * peers), BF16),
            shape((CAP * peers, 4 * cells), BF16),
        ],
        "vv",
    )(exchange(outgoing), precision_prior)
    prior, residual, sums, outgoing = call(
        first_update_kernel, [region, region, scalar_shape, fetched], "vvv"
    )(half, swap(half), pick)
    state, history, images = None, (), ()
    for iteration in range(ITERS):
        first, last = iteration == 0, iteration == ITERS - 1
        (partial,) = call(
            forward_kernel, [shape((reps, 24, LANES), F32)], "svvv", scratch=[field]
        )(meta, exchange(outgoing), sums, footprint)
        partial = lax.all_to_all(partial, "rep", split_axis=0, concat_axis=0, tiled=True)
        operands = [meta, partial, packed_weights, footprint]
        operands += [] if first else [state, *images]
        outgoing, *images = call(
            functools.partial(adjoint_kernel, iteration, last),
            [delivered] + ([] if last else [packed_shape] * (1 if first else 2)),
            "s" + "v" * (len(operands) - 1),
            scratch=[field],
        )(*operands)
        (half,) = call(gather_kernel, [shape((cells + 8, width), F32)], "vv")(
            exchange(outgoing), collect
        )
        operands = [half, swap(half), pick, prior, residual]
        operands += [] if first else [state, *history]
        results = call(
            functools.partial(update_kernel, first, last),
            [shape((own, width), F32)] * 2
            if last
            else [region, scalar_shape, fetched, scalar_shape, region, region, region],
            "v" * len(operands),
        )(*operands)
        if not last:
            residual, sums, outgoing, state, *history = results
    return tuple(results)


def solution(mesh):
    in_specs = (
        P("orb", None),
        P("orb", None),
        P("orb", "rep"),
        P("orb", None, "rep"),
        P("orb"),
        P("orb"),
    )
    out_specs = (P("orb", "rep"), P("orb", "rep"))
    return jax.shard_map(
        per_device, mesh=mesh, in_specs=in_specs, out_specs=out_specs, check_vma=False
    )
```

time: 207 us -> 202 us (0.976)
  blocking collectives: 183 us -> 152 us
  starting transfers between devices: 0 us -> 19.4 us
  waiting for transfers between devices: 0 us -> 4.59 us
    all_to_all x9, blocking collectives: 154 us -> 123 us  [exchange(): lax.all_to_all(flat, 'orb', split_axis=0, concat_axis=0, axis_index_group...]
    ppermute x0 -> x5, starting transfers between devices: none -> 19.4 us  [swap(): return lax.ppermute(array, 'orb', swapped)]
    ppermute x0 -> x5, waiting for transfers between devices: none -> 4.59 us  [swap(): return lax.ppermute(array, 'orb', swapped)]
    pallas_call x14 -> x19, Pallas kernels: 23.1 us -> 24.5 us  [the longest x4 8.57 us: per_device(): call(functools.partial(adjoint_kernel, iteration, last), [delivered] + ([...]
  transfers between devices with their start and end apart: 0 -> 5, of which waited for: 0 -> 5; matrix products, arithmetic and copies ran while one was open for 0% -> 0% of each run, Pallas kernels for 0% -> 0%
where the time goes in v3:
time: 202 us; the launch traced here: 201 us
  blocking collectives  152 us (75%)
  Pallas kernels  24.5 us (12%)
  starting transfers between devices  19.4 us (10%)
  waiting for transfers between devices  4.59 us (2%)
    all_to_all x9, blocking collectives, exchange(): lax.all_to_all(flat, 'orb', split_axis=0, concat_axis=0, axis_index_group...  123 us
    all_to_all x4, blocking collectives, per_device(): lax.all_to_all(partial, 'rep', split_axis=0, concat_axis=0, tiled=True)  28.6 us
    ppermute x5, starting transfers between devices, swap(): return lax.ppermute(array, 'orb', swapped)  19.4 us
    pallas_call x4, Pallas kernels, per_device(): call(functools.partial(adjoint_kernel, iteration, last), [delivered] + ([...  8.57 us
    pallas_call x4, Pallas kernels, per_device(): call(forward_kernel, [shape((reps, 24, LANES), F32)], 'svvv', scratch=[fi...  7.36 us
    ppermute x5, waiting for transfers between devices, swap(): return lax.ppermute(array, 'orb', swapped)  4.59 us
    pallas_call x1, Pallas kernels, per_device(): call(functools.partial(start_kernel, cells), [delivered, pltpu.SMEM((3 *...  4.55 us
  transfers between devices with their start and end apart: 5, of which 5 were waited for; matrix products, arithmetic and copies ran while one was open for 0% of the time, Pallas kernels for 0%

profile of v3, /device:TPU:1, one launch (start us, length us, event | category | flops | bytes accessed | tf_op | source)
XLA Modules:
  0.0 201.0 jit_solution(7430898772687674657)
XLA Ops:
  0.6 4.6 %shard_map.77 = (f32[288,128]{1,0:T(8,128)S(1)}, s32[144]{0:T(256)S(4)}, f32[8,256]{1,0:T(8,128)S(1)}, bf16[48,256,256]{2,1,0:T(8,128)(2,1)S(1)}) custom-call(s32[48]{0:T(128)} %rows_hbm.1, s32[48]{0:T(128)} %cells_hbm.1, f32[8,256]{1,0:T(8,128)} %observed_hbm.1, f32[8,256]{1,0:T(8,128)} %weights_hbm.1, bf16[48,256,256]{2,1,0:T(8,128)(2,1)} %footprint_hbm.1), custom_call_target="tpu_custom_call" | custom-call | tf_op jit(solution)/shard_map/pallas_call | solution.py:386
  5.2 21.1 %all_to_all.65 = f32[32,1,1152]{2,1,0:T(1,128)S(1)} all-to-all(f32[32,1,1152]{2,1,0:T(1,128)S(1)} %bitcast.30), channel_id=1, replica_groups={{0,8,16,24,32,40,48,56,64,72,80,88,96,104,112,120,128,136,144,152,160,1..., dimensions={0} | all-to-all | bytes 294912 | tf_op jit(solution)/shard_map/all_to_all | solution.py:374
  26.6 2.4 %collective-permute-start = (f32[96,256]{1,0:T(8,128)S(1)}, f32[96,256]{1,0:T(8,128)S(1)}, u32[]{:S(2)}, u32[]{:S(2)}) collective-permute-start(f32[96,256]{1,0:T(8,128)S(1)} %get-tuple-element.44.mine_ref), channel_id=1, source_target_pairs={{0,4},{4,0},{8,12},{12,8},{16,20},{20,16},{24,28},{28,24},{32,36},... | collective-permute-start | bytes 294920 | tf_op jit(solution)/shard_map/ppermute | solution.py:380
  29.0 0.9 collective-permute-done.other_ref
  30.1 12.4 %all_to_all.66 = f32[32,1,1024]{2,1,0:T(1,128)S(1)} all-to-all(f32[32,1,1024]{2,1,0:T(1,128)S(1)} %bitcast.35), channel_id=1, replica_groups={{0,8,16,24,32,40,48,56,64,72,80,88,96,104,112,120,128,136,144,152,160,1..., dimensions={0} | all-to-all | bytes 262144 | tf_op jit(solution)/shard_map/all_to_all | solution.py:374
  42.5 1.8 shard_map.80
  44.3 8.4 %all_to_all.67.refs_1_ = f32[4,24,128]{2,1,0:T(8,128)S(1)} all-to-all(f32[4,24,128]{2,1,0:T(8,128)S(1)} %shard_map.80), channel_id=1, replica_groups=mesh['orb'=64,'rep'=4] {'rep'}, dimensions={0} | all-to-all | bytes 98304 | tf_op jit(solution)/shard_map/all_to_all | solution.py:425
  52.7 2.1 %shard_map.81 = (f32[288,128]{1,0:T(8,128)S(1)}, f32[8,256]{1,0:T(8,128)S(1)}) custom-call(s32[144]{0:T(256)S(4)} %get-tuple-element.42.meta_ref.refs_0_, f32[4,24,128]{2,1,0:T(8,128)S(1)} %all_to_all.67.refs_1_, f32[8,256]{1,0:T(8,128)S(1)} %get-tuple-element.49.refs_2_, bf16[48,256,256]{2,1,0:T(8,128)(2,1)S(1)} %get-tuple-element.48.footprint_ref.refs_3_), custom_call_target="tpu_custom_call" | custom-call | tf_op jit(solution)/shard_map/pallas_call | solution.py:428
  54.8 13.2 %all_to_all.68 = f32[32,1,1152]{2,1,0:T(1,128)S(1)} all-to-all(f32[32,1,1152]{2,1,0:T(1,128)S(1)} %bitcast.31), channel_id=1, replica_groups={{0,8,16,24,32,40,48,56,64,72,80,88,96,104,112,120,128,136,144,152,160,1..., dimensions={0} | all-to-all | bytes 294912 | tf_op jit(solution)/shard_map/all_to_all | solution.py:374
  68.3 4.4 %collective-permute-start.1 = (f32[72,256]{1,0:T(8,128)S(1)}, f32[72,256]{1,0:T(8,128)S(1)}, u32[]{:S(2)}, u32[]{:S(2)}) collective-permute-start(f32[72,256]{1,0:T(8,128)S(1)} %shard_map.82.refs_0_), channel_id=1, source_target_pairs={{0,4},{4,0},{8,12},{12,8},{16,20},{20,16},{24,28},{28,24},{32,36},... | collective-permute-start | bytes 221192 | tf_op jit(solution)/shard_map/ppermute | solution.py:380
  72.7 0.9 collective-permute-done.1.refs_1_
  74.0 12.4 %all_to_all.69 = f32[32,1,1024]{2,1,0:T(1,128)S(1)} all-to-all(f32[32,1,1024]{2,1,0:T(1,128)S(1)} %bitcast.34), channel_id=1, replica_groups={{0,8,16,24,32,40,48,56,64,72,80,88,96,104,112,120,128,136,144,152,160,1..., dimensions={0} | all-to-all | bytes 262144 | tf_op jit(solution)/shard_map/all_to_all | solution.py:374
  86.3 1.8 shard_map.84
  88.2 6.7 %all_to_all.70.refs_1_ = f32[4,24,128]{2,1,0:T(8,128)S(1)} all-to-all(f32[4,24,128]{2,1,0:T(8,128)S(1)} %shard_map.84), channel_id=1, replica_groups=mesh['orb'=64,'rep'=4] {'rep'}, dimensions={0} | all-to-all | bytes 98304 | tf_op jit(solution)/shard_map/all_to_all | solution.py:425
  94.9 2.1 %shard_map.85 = (f32[288,128]{1,0:T(8,128)S(1)}, f32[8,256]{1,0:T(8,128)S(1)}, f32[8,256]{1,0:T(8,128)S(1)}) custom-call(s32[144]{0:T(256)S(4)} %get-tuple-element.42.meta_ref.refs_0_, f32[4,24,128]{2,1,0:T(8,128)S(1)} %all_to_all.70.refs_1_, f32[8,256]{1,0:T(8,128)S(1)} %get-tuple-element.49.refs_2_, ...), custom_call_target="tpu_custom_call" | custom-call | tf_op jit(solution)/shard_map/pallas_call | solution.py:428
  97.1 13.1 %all_to_all.71 = f32[32,1,1152]{2,1,0:T(1,128)S(1)} all-to-all(f32[32,1,1152]{2,1,0:T(1,128)S(1)} %bitcast.29), channel_id=1, replica_groups={{0,8,16,24,32,40,48,56,64,72,80,88,96,104,112,120,128,136,144,152,160,1..., dimensions={0} | all-to-all | bytes 294912 | tf_op jit(solution)/shard_map/all_to_all | solution.py:374
  110.3 4.2 %collective-permute-start.2 = (f32[72,256]{1,0:T(8,128)S(1)}, f32[72,256]{1,0:T(8,128)S(1)}, u32[]{:S(2)}, u32[]{:S(2)}) collective-permute-start(f32[72,256]{1,0:T(8,128)S(1)} %shard_map.86.refs_0_), channel_id=1, source_target_pairs={{0,4},{4,0},{8,12},{12,8},{16,20},{20,16},{24,28},{28,24},{32,36},... | collective-permute-start | bytes 221192 | tf_op jit(solution)/shard_map/ppermute | solution.py:380
  114.6 0.9 collective-permute-done.2.refs_1_
  116.2 12.4 %all_to_all.72 = f32[32,1,1024]{2,1,0:T(1,128)S(1)} all-to-all(f32[32,1,1024]{2,1,0:T(1,128)S(1)} %bitcast.32), channel_id=1, replica_groups={{0,8,16,24,32,40,48,56,64,72,80,88,96,104,112,120,128,136,144,152,160,1..., dimensions={0} | all-to-all | bytes 262144 | tf_op jit(solution)/shard_map/all_to_all | solution.py:374
  128.5 1.8 shard_map.88
  130.4 6.7 %all_to_all.73.refs_1_ = f32[4,24,128]{2,1,0:T(8,128)S(1)} all-to-all(f32[4,24,128]{2,1,0:T(8,128)S(1)} %shard_map.88), channel_id=1, replica_groups=mesh['orb'=64,'rep'=4] {'rep'}, dimensions={0} | all-to-all | bytes 98304 | tf_op jit(solution)/shard_map/all_to_all | solution.py:425
  137.1 2.2 %shard_map.89 = (f32[288,128]{1,0:T(8,128)S(1)}, f32[8,256]{1,0:T(8,128)S(1)}, f32[8,256]{1,0:T(8,128)S(1)}) custom-call(s32[144]{0:T(256)S(4)} %get-tuple-element.42.meta_ref.refs_0_, f32[4,24,128]{2,1,0:T(8,128)S(1)} %all_to_all.73.refs_1_, f32[8,256]{1,0:T(8,128)S(1)} %get-tuple-element.49.refs_2_, ...), custom_call_target="tpu_custom_call" | custom-call | tf_op jit(solution)/shard_map/pallas_call | solution.py:428
  139.3 13.1 %all_to_all.74 = f32[32,1,1152]{2,1,0:T(1,128)S(1)} all-to-all(f32[32,1,1152]{2,1,0:T(1,128)S(1)} %bitcast.28), channel_id=1, replica_groups={{0,8,16,24,32,40,48,56,64,72,80,88,96,104,112,120,128,136,144,152,160,1..., dimensions={0} | all-to-all | bytes 294912 | tf_op jit(solution)/shard_map/all_to_all | solution.py:374
  152.5 4.2 %collective-permute-start.3 = (f32[72,256]{1,0:T(8,128)S(1)}, f32[72,256]{1,0:T(8,128)S(1)}, u32[]{:S(2)}, u32[]{:S(2)}) collective-permute-start(f32[72,256]{1,0:T(8,128)S(1)} %shard_map.90.refs_0_), channel_id=1, source_target_pairs={{0,4},{4,0},{8,12},{12,8},{16,20},{20,16},{24,28},{28,24},{32,36},... | collective-permute-start | bytes 221192 | tf_op jit(solution)/shard_map/ppermute | solution.py:380
  156.8 0.9 collective-permute-done.3.refs_1_
  158.3 12.4 %all_to_all.75 = f32[32,1,1024]{2,1,0:T(1,128)S(1)} all-to-all(f32[32,1,1024]{2,1,0:T(1,128)S(1)} %bitcast.33), channel_id=1, replica_groups={{0,8,16,24,32,40,48,56,64,72,80,88,96,104,112,120,128,136,144,152,160,1..., dimensions={0} | all-to-all | bytes 262144 | tf_op jit(solution)/shard_map/all_to_all | solution.py:374
  170.7 1.8 shard_map.92
  172.6 6.7 %all_to_all.76.refs_1_ = f32[4,24,128]{2,1,0:T(8,128)S(1)} all-to-all(f32[4,24,128]{2,1,0:T(8,128)S(1)} %shard_map.92), channel_id=1, replica_groups=mesh['orb'=64,'rep'=4] {'rep'}, dimensions={0} | all-to-all | bytes 98304 | tf_op jit(solution)/shard_map/all_to_all | solution.py:425
  179.3 2.2 %shard_map.93 = f32[288,128]{1,0:T(8,128)S(1)} custom-call(s32[144]{0:T(256)S(4)} %get-tuple-element.42.meta_ref.refs_0_, f32[4,24,128]{2,1,0:T(8,128)S(1)} %all_to_all.76.refs_1_, f32[8,256]{1,0:T(8,128)S(1)} %get-tuple-element.49.refs_2_, bf16[48,256,256]{2,1,0:T(8,128)(2,1)S(1)} %get-tuple-element.48.footprint_ref.refs_3_, ...), custom_call_target="tpu_custom_call" | custom-call | tf_op jit(solution)/shard_map/pallas_call | solution.py:428
  181.5 13.1 %all_to_all.77 = f32[32,1,1152]{2,1,0:T(1,128)S(1)} all-to-all(f32[32,1,1152]{2,1,0:T(1,128)S(1)} %bitcast.18), channel_id=1, replica_groups={{0,8,16,24,32,40,48,56,64,72,80,88,96,104,112,120,128,136,144,152,160,1..., dimensions={0} | all-to-all | bytes 294912 | tf_op jit(solution)/shard_map/all_to_all | solution.py:374
  194.7 4.2 %collective-permute-start.4 = (f32[72,256]{1,0:T(8,128)S(1)}, f32[72,256]{1,0:T(8,128)S(1)}, u32[]{:S(2)}, u32[]{:S(2)}) collective-permute-start(f32[72,256]{1,0:T(8,128)S(1)} %shard_map.94.refs_0_), channel_id=1, source_target_pairs={{0,4},{4,0},{8,12},{12,8},{16,20},{20,16},{24,28},{28,24},{32,36},... | collective-permute-start | bytes 221192 | tf_op jit(solution)/shard_map/ppermute | solution.py:380
  199.9 1.1 shard_map.95
  (12 shorter events, 3.8 us)
Async XLA Ops:
  0.6 25.7 %copy-start = (f32[32,256]{1,0:T(8,128)S(1)}, f32[32,256]{1,0:T(8,128)}, u32[]{:S(2)}) copy-start(f32[32,256]{1,0:T(8,128)} %prior_ref.1) | copy-start | bytes 98308
  26.6 3.3 %collective-permute-start = (f32[96,256]{1,0:T(8,128)S(1)}, f32[96,256]{1,0:T(8,128)S(1)}, u32[]{:S(2)}, u32[]{:S(2)}) collective-permute-start(f32[96,256]{1,0:T(8,128)S(1)} %get-tuple-element.44.mine_ref), channel_id=1, source_target_pairs={{0,4},{4,0},{8,12},{12,8},{16,20},{20,16},{24,28},{28,24},{32,36},... | collective-permute-start | bytes 294920 | tf_op jit(solution)/shard_map/ppermute | solution.py:380
  68.3 5.3 %collective-permute-start.1 = (f32[72,256]{1,0:T(8,128)S(1)}, f32[72,256]{1,0:T(8,128)S(1)}, u32[]{:S(2)}, u32[]{:S(2)}) collective-permute-start(f32[72,256]{1,0:T(8,128)S(1)} %shard_map.82.refs_0_), channel_id=1, source_target_pairs={{0,4},{4,0},{8,12},{12,8},{16,20},{20,16},{24,28},{28,24},{32,36},... | collective-permute-start | bytes 221192 | tf_op jit(solution)/shard_map/ppermute | solution.py:380
  110.3 5.1 %collective-permute-start.2 = (f32[72,256]{1,0:T(8,128)S(1)}, f32[72,256]{1,0:T(8,128)S(1)}, u32[]{:S(2)}, u32[]{:S(2)}) collective-permute-start(f32[72,256]{1,0:T(8,128)S(1)} %shard_map.86.refs_0_), channel_id=1, source_target_pairs={{0,4},{4,0},{8,12},{12,8},{16,20},{20,16},{24,28},{28,24},{32,36},... | collective-permute-start | bytes 221192 | tf_op jit(solution)/shard_map/ppermute | solution.py:380
  152.5 5.1 %collective-permute-start.3 = (f32[72,256]{1,0:T(8,128)S(1)}, f32[72,256]{1,0:T(8,128)S(1)}, u32[]{:S(2)}, u32[]{:S(2)}) collective-permute-start(f32[72,256]{1,0:T(8,128)S(1)} %shard_map.90.refs_0_), channel_id=1, source_target_pairs={{0,4},{4,0},{8,12},{12,8},{16,20},{20,16},{24,28},{28,24},{32,36},... | collective-permute-start | bytes 221192 | tf_op jit(solution)/shard_map/ppermute | solution.py:380
  194.7 5.1 %collective-permute-start.4 = (f32[72,256]{1,0:T(8,128)S(1)}, f32[72,256]{1,0:T(8,128)S(1)}, u32[]{:S(2)}, u32[]{:S(2)}) collective-permute-start(f32[72,256]{1,0:T(8,128)S(1)} %shard_map.94.refs_0_), channel_id=1, source_target_pairs={{0,4},{4,0},{8,12},{12,8},{16,20},{20,16},{24,28},{28,24},{32,36},... | collective-permute-start | bytes 221192 | tf_op jit(solution)/shard_map/ppermute | solution.py:380

commit v4 on v3

--- a/solution.py
+++ b/solution.py
@@ -14,6 +14,7 @@
 DELIVER = FETCH + 1
 LANES = 128
 SUB = 16
+IN_FLIGHT = 6
 F32 = jnp.float32
 BF16 = jnp.bfloat16
 
@@ -40,12 +41,14 @@
             )
 
 
-def transposed_product(footprint_ref, field_ref, out_ref, block, row, place):
+def transposed_product(footprint_ref, field_ref, out_ref, block, row, place, keep_ref=None):
     soundings = footprint_ref.shape[1]
     left = jnp.zeros((SUB, LANES), F32)
     right = jnp.zeros((SUB, LANES), F32)
     for start in range(0, soundings, SUB):
         part = footprint_ref[block, start : start + SUB, :].astype(F32)
+        if keep_ref is not None:
+            keep_ref[block, start : start + SUB, :] = part
         z = field_ref[row, start : start + SUB, :]
         left = left + part[:, :LANES] * z
         right = right + part[:, LANES:] * z
@@ -74,7 +77,7 @@
 def start_kernel(
     cells, rows_hbm, cells_hbm, observed_hbm, weights_hbm, footprint_hbm,
     out_ref, meta_ref, packed_ref, footprint_ref,
-    field_ref, count_ref, rows_ref, cells_ref, observed_ref, weights_ref, sems, chunk_sems
+    arrived_ref, field_ref, count_ref, rows_ref, cells_ref, observed_ref, weights_ref, sems, chunk_sems
 ):
     blocks = footprint_ref.shape[0]
     rows, soundings = weights_ref.shape
@@ -98,9 +101,10 @@
     for chunk in range(chunks):
         span = pl.ds(chunk * size, size)
         large.append(
-            pltpu.make_async_copy(footprint_hbm.at[span], footprint_ref.at[span], chunk_sems.at[chunk])
-        )
-        large[-1].start()
+            pltpu.make_async_copy(footprint_hbm.at[span], arrived_ref.at[span], chunk_sems.at[chunk])
+        )
+    for copy in large[:IN_FLIGHT]:
+        copy.start()
     out_ref[...] = jnp.zeros_like(out_ref)
     for peer in range(peers):
         count_ref[peer] = 0
@@ -135,10 +139,12 @@
         out_ref[scalars, :] = jnp.where(
             lane_ids((1, LANES)) == rank, (slot + 1).astype(F32), out_ref[scalars, :]
         )
-        transposed_product(footprint_ref, field_ref, out_ref, block, row, place)
+        transposed_product(arrived_ref, field_ref, out_ref, block, row, place, footprint_ref)
 
     for chunk in range(chunks):
         large[chunk].wait()
+        if chunk + IN_FLIGHT < chunks:
+            large[chunk + IN_FLIGHT].start()
         each(chunk * size, (chunk + 1) * size, 4, product)
 
 
@@ -216,7 +222,7 @@
     return row_of_scalars([total(value) for value in values])
 
 
-def first_update_kernel(mine_ref, other_ref, pick_ref, prior_ref, residual_ref, sums_ref, out_ref):
+def first_update_kernel(mine_ref, other_ref, pick_ref, prior_ref, residual_ref, out_ref):
     cells = residual_ref.shape[0]
     own = cells // CORES
     first = lax.axis_index("orb") % CORES == 0
@@ -226,46 +232,64 @@
     prior_ref[...] = prior
     residual = mine_ref[0:cells, :] + other_ref[0:cells, :]
     residual_ref[...] = residual
-    sums_ref[...] = partial_sums(prior, residual)
     serve(residual, pick_ref[...], out_ref)
 
 
 def update_kernel(first, last, *refs):
     mine_ref, other_ref, pick_ref, prior_ref, residual_ref, *refs = refs
     if not first:
-        state_ref, direction_ref, image_ref, solution_ref, *refs = refs
+        state_ref, image_ref, *refs = refs
+    if last:
+        direction_ref, solution_ref, *refs = refs
     cells = residual_ref.shape[0]
     sums = mine_ref[cells : cells + 1, :] + other_ref[cells : cells + 1, :]
     norm, prior_rr, prior_rd, forward_rr, forward_rd = [sums[:, at : at + 1] for at in range(5)]
-    prior = prior_ref[...]
     residual = residual_ref[...]
-    image = mine_ref[0:cells, :] + other_ref[0:cells, :] + prior * residual
+    image = mine_ref[0:cells, :] + other_ref[0:cells, :] + prior_ref[...] * residual
     beta = jnp.zeros((1, 1), F32)
-    direction, prior_dd, forward_dd = residual, prior_rr, forward_rr
+    prior_dd, forward_dd = prior_rr, forward_rr
     if not first:
         beta = norm / state_ref[0:1, 0:1]
         prior_dd = prior_rr + beta * (2.0 * prior_rd + beta * state_ref[0:1, 1:2])
         forward_dd = forward_rr + beta * (2.0 * forward_rd + beta * state_ref[0:1, 2:3])
-        direction = residual + beta * direction_ref[...]
         image = image + beta * image_ref[...]
     alpha = norm / (prior_dd + forward_dd)
-    solution = alpha * direction if first else solution_ref[...] + alpha * direction
-    residual = residual - alpha * image
+    new_residual = residual - alpha * image
     if last:
         new_solution_ref, new_residual_ref = refs
+        direction = residual + beta * direction_ref[...]
+        solution = solution_ref[...] + alpha * direction
         own = cells // CORES
         core_first = lax.axis_index("orb") % CORES == 0
         new_solution_ref[...] = jnp.where(core_first, solution[:own], solution[own:])
-        new_residual_ref[...] = jnp.where(core_first, residual[:own], residual[own:])
+        new_residual_ref[...] = jnp.where(core_first, new_residual[:own], new_residual[own:])
         return
-    new_residual_ref, sums_ref, out_ref, new_state_ref, new_direction_ref, new_image_ref, new_solution_ref = refs
-    serve(residual, pick_ref[...], out_ref)
-    sums_ref[...] = partial_sums(prior, residual, direction)
-    new_residual_ref[...] = residual
-    new_state_ref[...] = row_of_scalars([norm, prior_dd, forward_dd, beta])
+    new_residual_ref, out_ref, new_state_ref, new_image_ref = refs
+    serve(new_residual, pick_ref[...], out_ref)
+    new_residual_ref[...] = new_residual
+    new_state_ref[...] = row_of_scalars([norm, prior_dd, forward_dd, beta, alpha])
+    new_image_ref[...] = image
+
+
+def beside_kernel(first, state_ref, prior_ref, residual_ref, new_residual_ref, *refs):
+    if not first:
+        direction_ref, solution_ref, *refs = refs
+    sums_ref, new_direction_ref, new_solution_ref = refs
+    beta = state_ref[0:1, 3:4]
+    alpha = state_ref[0:1, 4:5]
+    direction = residual_ref[...]
+    if not first:
+        direction = direction + beta * direction_ref[...]
+    solution = alpha * direction
+    if not first:
+        solution = solution + solution_ref[...]
+    sums_ref[...] = partial_sums(prior_ref[...], new_residual_ref[...], direction)
     new_direction_ref[...] = direction
-    new_image_ref[...] = image
     new_solution_ref[...] = solution
+
+
+def first_sums_kernel(prior_ref, residual_ref, sums_ref):
+    sums_ref[...] = partial_sums(prior_ref[...], residual_ref[...])
 
 
 def forward_kernel(meta_ref, in_ref, scalars_ref, footprint_ref, out_ref, sums_ref):
@@ -276,11 +300,11 @@
     def product(block):
         row = meta_ref[blocks + block]
         place = meta_ref[2 * blocks + block]
-        left = jnp.broadcast_to(in_ref[pl.ds(place, 1), :], (SUB, LANES))
-        right = jnp.broadcast_to(in_ref[pl.ds(place + 1, 1), :], (SUB, LANES))
-        for start in range(0, soundings, SUB):
-            part = footprint_ref[block, start : start + SUB, :].astype(F32)
-            sums_ref[row, start : start + SUB, :] += part[:, :LANES] * left + part[:, LANES:] * right
+        left = jnp.broadcast_to(in_ref[pl.ds(place, 1), :], (2 * SUB, LANES))
+        right = jnp.broadcast_to(in_ref[pl.ds(place + 1, 1), :], (2 * SUB, LANES))
+        for start in range(0, soundings, 2 * SUB):
+            part = footprint_ref[block, start : start + 2 * SUB, :]
+            sums_ref[row, start : start + 2 * SUB, :] += part[:, :LANES] * left + part[:, LANES:] * right
 
     each(0, blocks, 4, product)
     lanes = lane_ids((8, LANES))
@@ -335,7 +359,7 @@
             footprint_ref, field_ref, out_ref, block, meta_ref[blocks + block], meta_ref[block]
         )
 
-    each(0, blocks, 4, product)
+    each(0, blocks, 8, product)
 
 
 def call(kernel, out_shape, kinds, out_kinds=None, scratch=()):
@@ -347,7 +371,7 @@
         in_specs=[pl.BlockSpec(memory_space=spaces[kind]) for kind in kinds],
         out_specs=[pl.BlockSpec(memory_space=spaces[kind]) for kind in out_kinds],
         scratch_shapes=list(scratch),
-        compiler_params=pltpu.CompilerParams(vmem_limit_bytes=32 * 1024 * 1024),
+        compiler_params=pltpu.CompilerParams(vmem_limit_bytes=16 * 1024 * 1024),
     )
 
 
@@ -389,11 +413,12 @@
             delivered,
             pltpu.SMEM((3 * blocks,), jnp.int32),
             packed_shape,
-            pltpu.VMEM(footprint.shape, footprint.dtype),
+            pltpu.VMEM(footprint.shape, F32),
         ],
         "hhhhh",
         "vsvv",
         [
+            pltpu.VMEM(footprint.shape, footprint.dtype),
             field,
             pltpu.SMEM((peers,), jnp.int32),
             pltpu.SMEM((blocks,), jnp.int32),
@@ -401,7 +426,7 @@
             pltpu.VMEM(observed.shape, F32),
             pltpu.VMEM(weights.shape, F32),
             pltpu.SemaphoreType.DMA((4,)),
-            pltpu.SemaphoreType.DMA((6,)),
+            pltpu.SemaphoreType.DMA((12,)),
         ],
     )(*in_hbm)
     half, collect, pick = call(
@@ -413,15 +438,17 @@
         ],
         "vv",
     )(exchange(outgoing), precision_prior)
-    prior, residual, sums, outgoing = call(
-        first_update_kernel, [region, region, scalar_shape, fetched], "vvv"
-    )(half, swap(half), pick)
-    state, history, images = None, (), ()
+    prior, residual, outgoing = call(first_update_kernel, [region, region, fetched], "vvv")(
+        half, swap(half), pick
+    )
+    incoming = exchange(outgoing)
+    (sums,) = call(first_sums_kernel, [scalar_shape], "vv")(prior, residual)
+    state, history, images, moved = None, [], [], []
     for iteration in range(ITERS):
         first, last = iteration == 0, iteration == ITERS - 1
         (partial,) = call(
             forward_kernel, [shape((reps, 24, LANES), F32)], "svvv", scratch=[field]
-        )(meta, exchange(outgoing), sums, footprint)
+        )(meta, incoming, sums, footprint)
         partial = lax.all_to_all(partial, "rep", split_axis=0, concat_axis=0, tiled=True)
         operands = [meta, partial, packed_weights, footprint]
         operands += [] if first else [state, *images]
@@ -435,16 +462,23 @@
             exchange(outgoing), collect
         )
         operands = [half, swap(half), pick, prior, residual]
-        operands += [] if first else [state, *history]
+        operands += [] if first else [state, *moved]
+        operands += history if last else []
         results = call(
             functools.partial(update_kernel, first, last),
-            [shape((own, width), F32)] * 2
-            if last
-            else [region, scalar_shape, fetched, scalar_shape, region, region, region],
+            [shape((own, width), F32)] * 2 if last else [region, fetched, scalar_shape, region],
             "v" * len(operands),
         )(*operands)
         if not last:
-            residual, sums, outgoing, state, *history = results
+            new_residual, outgoing, state, *moved = results
+            incoming = exchange(outgoing)
+            operands = [state, prior, residual, new_residual, *history]
+            sums, *history = call(
+                functools.partial(beside_kernel, first),
+                [scalar_shape, region, region],
+                "v" * len(operands),
+            )(*operands)
+            residual = new_residual
     return tuple(results)
 
 

time: 202 us -> 233 us (1.15)
  blocking collectives: 152 us -> 102 us
  waiting for transfers between devices: 4.59 us -> 43.4 us
  local copies, waits for them, and re-layouts: 0.01 us -> 28.1 us
  starting transfers between devices: 19.4 us -> 34.2 us
    all_to_all x9 -> x5, blocking collectives: 123 us -> 72 us  [exchange(): lax.all_to_all(flat, 'orb', split_axis=0, concat_axis=0, axis_index_group...]
    all_to_all x0 -> x4, waiting for transfers between devices: none -> 38.8 us  [exchange(): lax.all_to_all(flat, 'orb', split_axis=0, concat_axis=0, axis_index_group...]
    unnamed x2 -> x20, local copies, waits for them, and re-layouts: 0.01 us -> 28.1 us
    all_to_all x0 -> x4, starting transfers between devices: none -> 15.4 us  [exchange(): lax.all_to_all(flat, 'orb', split_axis=0, concat_axis=0, axis_index_group...]
  transfers between devices with their start and end apart: 5 -> 9, of which waited for: 5 -> 9; matrix products, arithmetic and copies ran while one was open for 0% -> 0% of each run, Pallas kernels for 0% -> 0%
where the time goes in v4:
time: 233 us; the launch traced here: 232 us
  blocking collectives  102 us (44%)
  waiting for transfers between devices  43.4 us (19%)
  starting transfers between devices  34.2 us (15%)
  local copies, waits for them, and re-layouts  28.1 us (12%)
  Pallas kernels  24.2 us (10%)
    all_to_all x5, blocking collectives, exchange(): lax.all_to_all(flat, 'orb', split_axis=0, concat_axis=0, axis_index_group...  72 us
    all_to_all x4, waiting for transfers between devices, exchange(): lax.all_to_all(flat, 'orb', split_axis=0, concat_axis=0, axis_index_group...  38.8 us
    all_to_all x4, blocking collectives, per_device(): lax.all_to_all(partial, 'rep', split_axis=0, concat_axis=0, tiled=True)  29.7 us
    unnamed x20, local copies, waits for them, and re-layouts  28.1 us
    ppermute x5, starting transfers between devices, swap(): return lax.ppermute(array, 'orb', swapped)  18.8 us
    all_to_all x4, starting transfers between devices, exchange(): lax.all_to_all(flat, 'orb', split_axis=0, concat_axis=0, axis_index_group...  15.4 us
    pallas_call x4, Pallas kernels, per_device(): call(functools.partial(adjoint_kernel, iteration, last), [delivered] + ([...  7.14 us
    pallas_call x4, Pallas kernels, per_device(): call(forward_kernel, [shape((reps, 24, LANES), F32)], 'svvv', scratch=[fi...  5.64 us
  transfers between devices with their start and end apart: 9, of which 9 were waited for; matrix products, arithmetic and copies ran while one was open for 0% of the time, Pallas kernels for 0%

profile of v4, /device:TPU:1, one launch (start us, length us, event | category | flops | bytes accessed | tf_op | source)
XLA Modules:
  0.0 232.4 jit_solution(9231563184614398908)
XLA Ops:
  0.6 4.2 %shard_map.77 = (f32[288,128]{1,0:T(8,128)S(1)}, s32[144]{0:T(256)S(4)}, f32[8,256]{1,0:T(8,128)S(1)}, f32[48,256,256]{2,1,0:T(8,128)S(1)}) custom-call(s32[48]{0:T(128)} %rows_hbm.1, s32[48]{0:T(128)} %cells_hbm.1, f32[8,256]{1,0:T(8,128)} %observed_hbm.1, f32[8,256]{1,0:T(8,128)} %weights_hbm.1, bf16[48,256,256]{2,1,0:T(8,128)(2,1)} %footprint_hbm.1), custom_call_target="tpu_custom_call" | custom-call | tf_op jit(solution)/shard_map/pallas_call | solution.py:410
  4.9 4.5 %copy-done = f32[48,256,256]{2,1,0:T(8,128)} copy-done((f32[48,256,256]{2,1,0:T(8,128)}, f32[48,256,256]{2,1,0:T(8,128)S(1)}, u32[]{:S(2)}) %copy-start) | copy-done | bytes 12582936
  9.4 21.1 %all_to_all.65 = f32[32,1,1152]{2,1,0:T(1,128)S(1)} all-to-all(f32[32,1,1152]{2,1,0:T(1,128)S(1)} %bitcast.30), channel_id=1, replica_groups={{0,8,16,24,32,40,48,56,64,72,80,88,96,104,112,120,128,136,144,152,160,1..., dimensions={0} | all-to-all | bytes 294912 | tf_op jit(solution)/shard_map/all_to_all | solution.py:398
  31.6 2.4 %collective-permute-start = (f32[96,256]{1,0:T(8,128)S(1)}, f32[96,256]{1,0:T(8,128)S(1)}, u32[]{:S(2)}, u32[]{:S(2)}) collective-permute-start(f32[96,256]{1,0:T(8,128)S(1)} %get-tuple-element.43.mine_ref), channel_id=1, source_target_pairs={{0,4},{4,0},{8,12},{12,8},{16,20},{20,16},{24,28},{28,24},{32,36},... | collective-permute-start | bytes 294920 | tf_op jit(solution)/shard_map/ppermute | solution.py:404
  35.7 3.9 %all-to-all-start.1 = ((f32[32,1,1024]{2,1,0:T(1,128)}), f32[32,1,1024]{2,1,0:T(1,128)S(1)}, u32[]{:S(2)}, u32[]{:S(2)}) async-start(f32[32,1,1024]{2,1,0:T(1,128)} %bitcast.2), calls=%async_computation.1 | async-start | bytes 262144 | tf_op jit(solution)/shard_map/all_to_all | solution.py:398
  39.6 9.7 %all-to-all-done.1 = f32[32,1,1024]{2,1,0:T(1,128)S(1)} async-done(((f32[32,1,1024]{2,1,0:T(1,128)}), f32[32,1,1024]{2,1,0:T(1,128)S(1)}, u32[]{:S(2)}, u32[]{:S(2)}) %all-to-all-start.1) | async-done | bytes 131104 | tf_op jit(solution)/shard_map/all_to_all | solution.py:398
  49.4 4.6 %copy-done.1 = f32[48,256,256]{2,1,0:T(8,128)S(1)} copy-done((f32[48,256,256]{2,1,0:T(8,128)S(1)}, f32[48,256,256]{2,1,0:T(8,128)}, u32[]{:S(2)}) %copy-start.1) | copy-done | bytes 12582936
  55.4 8.6 %all_to_all.66.refs_1_ = f32[4,24,128]{2,1,0:T(8,128)S(1)} all-to-all(f32[4,24,128]{2,1,0:T(8,128)S(1)} %shard_map.81), channel_id=1, replica_groups=mesh['orb'=64,'rep'=4] {'rep'}, dimensions={0} | all-to-all | bytes 98304 | tf_op jit(solution)/shard_map/all_to_all | solution.py:452
  65.5 12.7 %all_to_all.67 = f32[32,1,1152]{2,1,0:T(1,128)S(1)} all-to-all(f32[32,1,1152]{2,1,0:T(1,128)S(1)} %bitcast.31), channel_id=1, replica_groups={{0,8,16,24,32,40,48,56,64,72,80,88,96,104,112,120,128,136,144,152,160,1..., dimensions={0} | all-to-all | bytes 294912 | tf_op jit(solution)/shard_map/all_to_all | solution.py:398
  78.4 4.2 %collective-permute-start.1 = (f32[72,256]{1,0:T(8,128)S(1)}, f32[72,256]{1,0:T(8,128)S(1)}, u32[]{:S(2)}, u32[]{:S(2)}) collective-permute-start(f32[72,256]{1,0:T(8,128)S(1)} %shard_map.83.refs_0_), channel_id=1, source_target_pairs={{0,4},{4,0},{8,12},{12,8},{16,20},{20,16},{24,28},{28,24},{32,36},... | collective-permute-start | bytes 221192 | tf_op jit(solution)/shard_map/ppermute | solution.py:404
  84.6 3.9 %all-to-all-start.4 = ((f32[32,1,1024]{2,1,0:T(1,128)}), f32[32,1,1024]{2,1,0:T(1,128)S(1)}, u32[]{:S(2)}, u32[]{:S(2)}) async-start(f32[32,1,1024]{2,1,0:T(1,128)} %bitcast.6), calls=%async_computation.4 | async-start | bytes 262144 | tf_op jit(solution)/shard_map/all_to_all | solution.py:398
  88.6 9.7 %all-to-all-done.4 = f32[32,1,1024]{2,1,0:T(1,128)S(1)} async-done(((f32[32,1,1024]{2,1,0:T(1,128)}), f32[32,1,1024]{2,1,0:T(1,128)S(1)}, u32[]{:S(2)}, u32[]{:S(2)}) %all-to-all-start.4) | async-done | bytes 131104 | tf_op jit(solution)/shard_map/all_to_all | solution.py:398
  98.3 4.6 %copy-done.3 = f32[48,256,256]{2,1,0:T(8,128)S(1)} copy-done((f32[48,256,256]{2,1,0:T(8,128)S(1)}, f32[48,256,256]{2,1,0:T(8,128)}, u32[]{:S(2)}) %copy-start.3) | copy-done | bytes 12582936
  104.3 7.1 %all_to_all.68.refs_1_ = f32[4,24,128]{2,1,0:T(8,128)S(1)} all-to-all(f32[4,24,128]{2,1,0:T(8,128)S(1)} %shard_map.86), channel_id=1, replica_groups=mesh['orb'=64,'rep'=4] {'rep'}, dimensions={0} | all-to-all | bytes 98304 | tf_op jit(solution)/shard_map/all_to_all | solution.py:452
  111.5 1.9 shard_map.87
  113.3 12.7 %all_to_all.69 = f32[32,1,1152]{2,1,0:T(1,128)S(1)} all-to-all(f32[32,1,1152]{2,1,0:T(1,128)S(1)} %bitcast.29), channel_id=1, replica_groups={{0,8,16,24,32,40,48,56,64,72,80,88,96,104,112,120,128,136,144,152,160,1..., dimensions={0} | all-to-all | bytes 294912 | tf_op jit(solution)/shard_map/all_to_all | solution.py:398
  126.2 4.0 %collective-permute-start.2 = (f32[72,256]{1,0:T(8,128)S(1)}, f32[72,256]{1,0:T(8,128)S(1)}, u32[]{:S(2)}, u32[]{:S(2)}) collective-permute-start(f32[72,256]{1,0:T(8,128)S(1)} %shard_map.88.refs_0_), channel_id=1, source_target_pairs={{0,4},{4,0},{8,12},{12,8},{16,20},{20,16},{24,28},{28,24},{32,36},... | collective-permute-start | bytes 221192 | tf_op jit(solution)/shard_map/ppermute | solution.py:404
  132.5 3.9 %all-to-all-start.7 = ((f32[32,1,1024]{2,1,0:T(1,128)}), f32[32,1,1024]{2,1,0:T(1,128)S(1)}, u32[]{:S(2)}, u32[]{:S(2)}) async-start(f32[32,1,1024]{2,1,0:T(1,128)} %bitcast.10), calls=%async_computation.7 | async-start | bytes 262144 | tf_op jit(solution)/shard_map/all_to_all | solution.py:398
  136.5 9.7 %all-to-all-done.7 = f32[32,1,1024]{2,1,0:T(1,128)S(1)} async-done(((f32[32,1,1024]{2,1,0:T(1,128)}), f32[32,1,1024]{2,1,0:T(1,128)S(1)}, u32[]{:S(2)}, u32[]{:S(2)}) %all-to-all-start.7) | async-done | bytes 131104 | tf_op jit(solution)/shard_map/all_to_all | solution.py:398
  146.2 4.6 %copy-done.5 = f32[48,256,256]{2,1,0:T(8,128)S(1)} copy-done((f32[48,256,256]{2,1,0:T(8,128)S(1)}, f32[48,256,256]{2,1,0:T(8,128)}, u32[]{:S(2)}) %copy-start.5) | copy-done | bytes 12582936
  152.2 7.1 %all_to_all.70.refs_1_ = f32[4,24,128]{2,1,0:T(8,128)S(1)} all-to-all(f32[4,24,128]{2,1,0:T(8,128)S(1)} %shard_map.91), channel_id=1, replica_groups=mesh['orb'=64,'rep'=4] {'rep'}, dimensions={0} | all-to-all | bytes 98304 | tf_op jit(solution)/shard_map/all_to_all | solution.py:452
  159.3 1.9 shard_map.92
  161.2 12.7 %all_to_all.71 = f32[32,1,1152]{2,1,0:T(1,128)S(1)} all-to-all(f32[32,1,1152]{2,1,0:T(1,128)S(1)} %bitcast.28), channel_id=1, replica_groups={{0,8,16,24,32,40,48,56,64,72,80,88,96,104,112,120,128,136,144,152,160,1..., dimensions={0} | all-to-all | bytes 294912 | tf_op jit(solution)/shard_map/all_to_all | solution.py:398
  174.1 4.2 %collective-permute-start.3 = (f32[72,256]{1,0:T(8,128)S(1)}, f32[72,256]{1,0:T(8,128)S(1)}, u32[]{:S(2)}, u32[]{:S(2)}) collective-permute-start(f32[72,256]{1,0:T(8,128)S(1)} %shard_map.93.refs_0_), channel_id=1, source_target_pairs={{0,4},{4,0},{8,12},{12,8},{16,20},{20,16},{24,28},{28,24},{32,36},... | collective-permute-start | bytes 221192 | tf_op jit(solution)/shard_map/ppermute | solution.py:404
  180.5 3.9 %all-to-all-start.10 = ((f32[32,1,1024]{2,1,0:T(1,128)}), f32[32,1,1024]{2,1,0:T(1,128)S(1)}, u32[]{:S(2)}, u32[]{:S(2)}) async-start(f32[32,1,1024]{2,1,0:T(1,128)} %bitcast.14), calls=%async_computation.10 | async-start | bytes 262144 | tf_op jit(solution)/shard_map/all_to_all | solution.py:398
  184.6 9.7 %all-to-all-done.10 = f32[32,1,1024]{2,1,0:T(1,128)S(1)} async-done(((f32[32,1,1024]{2,1,0:T(1,128)}), f32[32,1,1024]{2,1,0:T(1,128)S(1)}, u32[]{:S(2)}, u32[]{:S(2)}) %all-to-all-start.10) | async-done | bytes 131104 | tf_op jit(solution)/shard_map/all_to_all | solution.py:398
  194.2 4.6 %copy-done.7 = f32[48,256,256]{2,1,0:T(8,128)S(1)} copy-done((f32[48,256,256]{2,1,0:T(8,128)S(1)}, f32[48,256,256]{2,1,0:T(8,128)}, u32[]{:S(2)}) %copy-start.7) | copy-done | bytes 12582936
  200.2 6.7 %all_to_all.72.refs_1_ = f32[4,24,128]{2,1,0:T(8,128)S(1)} all-to-all(f32[4,24,128]{2,1,0:T(8,128)S(1)} %shard_map.96), channel_id=1, replica_groups=mesh['orb'=64,'rep'=4] {'rep'}, dimensions={0} | all-to-all | bytes 98304 | tf_op jit(solution)/shard_map/all_to_all | solution.py:452
  207.0 4.6 %copy-done.8 = f32[48,256,256]{2,1,0:T(8,128)S(1)} copy-done((f32[48,256,256]{2,1,0:T(8,128)S(1)}, f32[48,256,256]{2,1,0:T(8,128)}, u32[]{:S(2)}) %copy-start.8) | copy-done | bytes 12582936
  211.6 1.9 shard_map.97
  213.4 12.7 %all_to_all.73 = f32[32,1,1152]{2,1,0:T(1,128)S(1)} all-to-all(f32[32,1,1152]{2,1,0:T(1,128)S(1)} %bitcast.23), channel_id=1, replica_groups={{0,8,16,24,32,40,48,56,64,72,80,88,96,104,112,120,128,136,144,152,160,1..., dimensions={0} | all-to-all | bytes 294912 | tf_op jit(solution)/shard_map/all_to_all | solution.py:398
  226.3 4.0 %collective-permute-start.4 = (f32[72,256]{1,0:T(8,128)S(1)}, f32[72,256]{1,0:T(8,128)S(1)}, u32[]{:S(2)}, u32[]{:S(2)}) collective-permute-start(f32[72,256]{1,0:T(8,128)S(1)} %shard_map.98.refs_0_), channel_id=1, source_target_pairs={{0,4},{4,0},{8,12},{12,8},{16,20},{20,16},{24,28},{28,24},{32,36},... | collective-permute-start | bytes 221192 | tf_op jit(solution)/shard_map/ppermute | solution.py:404
  (38 shorter events, 19.7 us)
Async XLA Ops:
  4.9 4.5 %copy-start = (f32[48,256,256]{2,1,0:T(8,128)}, f32[48,256,256]{2,1,0:T(8,128)S(1)}, u32[]{:S(2)}) copy-start(f32[48,256,256]{2,1,0:T(8,128)S(1)} %get-tuple-element.48.footprint_ref.refs_3_) | copy-start | bytes 37748740
  30.5 0.8 copy-start.9
  31.6 3.3 %collective-permute-start = (f32[96,256]{1,0:T(8,128)S(1)}, f32[96,256]{1,0:T(8,128)S(1)}, u32[]{:S(2)}, u32[]{:S(2)}) collective-permute-start(f32[96,256]{1,0:T(8,128)S(1)} %get-tuple-element.43.mine_ref), channel_id=1, source_target_pairs={{0,4},{4,0},{8,12},{12,8},{16,20},{20,16},{24,28},{28,24},{32,36},... | collective-permute-start | bytes 294920 | tf_op jit(solution)/shard_map/ppermute | solution.py:404
  35.7 13.7 %all-to-all-start.1 = ((f32[32,1,1024]{2,1,0:T(1,128)}), f32[32,1,1024]{2,1,0:T(1,128)S(1)}, u32[]{:S(2)}, u32[]{:S(2)}) async-start(f32[32,1,1024]{2,1,0:T(1,128)} %bitcast.2), calls=%async_computation.1 | async-start | bytes 262144 | tf_op jit(solution)/shard_map/all_to_all | solution.py:398
  49.4 4.6 %copy-start.1 = (f32[48,256,256]{2,1,0:T(8,128)S(1)}, f32[48,256,256]{2,1,0:T(8,128)}, u32[]{:S(2)}) copy-start(f32[48,256,256]{2,1,0:T(8,128)} %copy-done) | copy-start | bytes 37748740
  54.0 10.1 %copy-start.2 = (f32[48,256,256]{2,1,0:T(8,128)S(1)}, f32[48,256,256]{2,1,0:T(8,128)}, u32[]{:S(2)}) copy-start(f32[48,256,256]{2,1,0:T(8,128)} %copy-done) | copy-start | bytes 37748740
  78.4 5.2 %collective-permute-start.1 = (f32[72,256]{1,0:T(8,128)S(1)}, f32[72,256]{1,0:T(8,128)S(1)}, u32[]{:S(2)}, u32[]{:S(2)}) collective-permute-start(f32[72,256]{1,0:T(8,128)S(1)} %shard_map.83.refs_0_), channel_id=1, source_target_pairs={{0,4},{4,0},{8,12},{12,8},{16,20},{20,16},{24,28},{28,24},{32,36},... | collective-permute-start | bytes 221192 | tf_op jit(solution)/shard_map/ppermute | solution.py:404
  84.6 13.7 %all-to-all-start.4 = ((f32[32,1,1024]{2,1,0:T(1,128)}), f32[32,1,1024]{2,1,0:T(1,128)S(1)}, u32[]{:S(2)}, u32[]{:S(2)}) async-start(f32[32,1,1024]{2,1,0:T(1,128)} %bitcast.6), calls=%async_computation.4 | async-start | bytes 262144 | tf_op jit(solution)/shard_map/all_to_all | solution.py:398
  98.3 4.6 %copy-start.3 = (f32[48,256,256]{2,1,0:T(8,128)S(1)}, f32[48,256,256]{2,1,0:T(8,128)}, u32[]{:S(2)}) copy-start(f32[48,256,256]{2,1,0:T(8,128)} %copy-done) | copy-start | bytes 37748740
  102.9 8.6 %copy-start.4 = (f32[48,256,256]{2,1,0:T(8,128)S(1)}, f32[48,256,256]{2,1,0:T(8,128)}, u32[]{:S(2)}) copy-start(f32[48,256,256]{2,1,0:T(8,128)} %copy-done) | copy-start | bytes 37748740
  126.2 4.9 %collective-permute-start.2 = (f32[72,256]{1,0:T(8,128)S(1)}, f32[72,256]{1,0:T(8,128)S(1)}, u32[]{:S(2)}, u32[]{:S(2)}) collective-permute-start(f32[72,256]{1,0:T(8,128)S(1)} %shard_map.88.refs_0_), channel_id=1, source_target_pairs={{0,4},{4,0},{8,12},{12,8},{16,20},{20,16},{24,28},{28,24},{32,36},... | collective-permute-start | bytes 221192 | tf_op jit(solution)/shard_map/ppermute | solution.py:404
  132.5 13.7 %all-to-all-start.7 = ((f32[32,1,1024]{2,1,0:T(1,128)}), f32[32,1,1024]{2,1,0:T(1,128)S(1)}, u32[]{:S(2)}, u32[]{:S(2)}) async-start(f32[32,1,1024]{2,1,0:T(1,128)} %bitcast.10), calls=%async_computation.7 | async-start | bytes 262144 | tf_op jit(solution)/shard_map/all_to_all | solution.py:398
  146.2 4.6 %copy-start.5 = (f32[48,256,256]{2,1,0:T(8,128)S(1)}, f32[48,256,256]{2,1,0:T(8,128)}, u32[]{:S(2)}) copy-start(f32[48,256,256]{2,1,0:T(8,128)} %copy-done) | copy-start | bytes 37748740
  150.8 8.6 %copy-start.6 = (f32[48,256,256]{2,1,0:T(8,128)S(1)}, f32[48,256,256]{2,1,0:T(8,128)}, u32[]{:S(2)}) copy-start(f32[48,256,256]{2,1,0:T(8,128)} %copy-done) | copy-start | bytes 37748740
  174.1 5.1 %collective-permute-start.3 = (f32[72,256]{1,0:T(8,128)S(1)}, f32[72,256]{1,0:T(8,128)S(1)}, u32[]{:S(2)}, u32[]{:S(2)}) collective-permute-start(f32[72,256]{1,0:T(8,128)S(1)} %shard_map.93.refs_0_), channel_id=1, source_target_pairs={{0,4},{4,0},{8,12},{12,8},{16,20},{20,16},{24,28},{28,24},{32,36},... | collective-permute-start | bytes 221192 | tf_op jit(solution)/shard_map/ppermute | solution.py:404
  180.5 13.7 %all-to-all-start.10 = ((f32[32,1,1024]{2,1,0:T(1,128)}), f32[32,1,1024]{2,1,0:T(1,128)S(1)}, u32[]{:S(2)}, u32[]{:S(2)}) async-start(f32[32,1,1024]{2,1,0:T(1,128)} %bitcast.14), calls=%async_computation.10 | async-start | bytes 262144 | tf_op jit(solution)/shard_map/all_to_all | solution.py:398
  194.2 4.6 %copy-start.7 = (f32[48,256,256]{2,1,0:T(8,128)S(1)}, f32[48,256,256]{2,1,0:T(8,128)}, u32[]{:S(2)}) copy-start(f32[48,256,256]{2,1,0:T(8,128)} %copy-done) | copy-start | bytes 37748740
  207.0 4.6 %copy-start.8 = (f32[48,256,256]{2,1,0:T(8,128)S(1)}, f32[48,256,256]{2,1,0:T(8,128)}, u32[]{:S(2)}) copy-start(f32[48,256,256]{2,1,0:T(8,128)} %copy-done) | copy-start | bytes 37748740
  226.3 4.9 %collective-permute-start.4 = (f32[72,256]{1,0:T(8,128)S(1)}, f32[72,256]{1,0:T(8,128)S(1)}, u32[]{:S(2)}, u32[]{:S(2)}) collective-permute-start(f32[72,256]{1,0:T(8,128)S(1)} %shard_map.98.refs_0_), channel_id=1, source_target_pairs={{0,4},{4,0},{8,12},{12,8},{16,20},{20,16},{24,28},{28,24},{32,36},... | collective-permute-start | bytes 221192 | tf_op jit(solution)/shard_map/ppermute | solution.py:404

commit v5 on v3

--- a/solution.py
+++ b/solution.py
@@ -14,6 +14,7 @@
 DELIVER = FETCH + 1
 LANES = 128
 SUB = 16
+IN_FLIGHT = 6
 F32 = jnp.float32
 BF16 = jnp.bfloat16
 
@@ -40,12 +41,14 @@
             )
 
 
-def transposed_product(footprint_ref, field_ref, out_ref, block, row, place):
+def transposed_product(footprint_ref, field_ref, out_ref, block, row, place, keep_ref=None):
     soundings = footprint_ref.shape[1]
     left = jnp.zeros((SUB, LANES), F32)
     right = jnp.zeros((SUB, LANES), F32)
     for start in range(0, soundings, SUB):
         part = footprint_ref[block, start : start + SUB, :].astype(F32)
+        if keep_ref is not None:
+            keep_ref[block, start : start + SUB, :] = part
         z = field_ref[row, start : start + SUB, :]
         left = left + part[:, :LANES] * z
         right = right + part[:, LANES:] * z
@@ -74,7 +77,7 @@
 def start_kernel(
     cells, rows_hbm, cells_hbm, observed_hbm, weights_hbm, footprint_hbm,
     out_ref, meta_ref, packed_ref, footprint_ref,
-    field_ref, count_ref, rows_ref, cells_ref, observed_ref, weights_ref, sems, chunk_sems
+    arrived_ref, field_ref, count_ref, rows_ref, cells_ref, observed_ref, weights_ref, sems, chunk_sems
 ):
     blocks = footprint_ref.shape[0]
     rows, soundings = weights_ref.shape
@@ -98,9 +101,10 @@
     for chunk in range(chunks):
         span = pl.ds(chunk * size, size)
         large.append(
-            pltpu.make_async_copy(footprint_hbm.at[span], footprint_ref.at[span], chunk_sems.at[chunk])
-        )
-        large[-1].start()
+            pltpu.make_async_copy(footprint_hbm.at[span], arrived_ref.at[span], chunk_sems.at[chunk])
+        )
+    for copy in large[:IN_FLIGHT]:
+        copy.start()
     out_ref[...] = jnp.zeros_like(out_ref)
     for peer in range(peers):
         count_ref[peer] = 0
@@ -135,10 +139,12 @@
         out_ref[scalars, :] = jnp.where(
             lane_ids((1, LANES)) == rank, (slot + 1).astype(F32), out_ref[scalars, :]
         )
-        transposed_product(footprint_ref, field_ref, out_ref, block, row, place)
+        transposed_product(arrived_ref, field_ref, out_ref, block, row, place, footprint_ref)
 
     for chunk in range(chunks):
         large[chunk].wait()
+        if chunk + IN_FLIGHT < chunks:
+            large[chunk + IN_FLIGHT].start()
         each(chunk * size, (chunk + 1) * size, 4, product)
 
 
@@ -276,11 +282,11 @@
     def product(block):
         row = meta_ref[blocks + block]
         place = meta_ref[2 * blocks + block]
-        left = jnp.broadcast_to(in_ref[pl.ds(place, 1), :], (SUB, LANES))
-        right = jnp.broadcast_to(in_ref[pl.ds(place + 1, 1), :], (SUB, LANES))
-        for start in range(0, soundings, SUB):
-            part = footprint_ref[block, start : start + SUB, :].astype(F32)
-            sums_ref[row, start : start + SUB, :] += part[:, :LANES] * left + part[:, LANES:] * right
+        left = jnp.broadcast_to(in_ref[pl.ds(place, 1), :], (2 * SUB, LANES))
+        right = jnp.broadcast_to(in_ref[pl.ds(place + 1, 1), :], (2 * SUB, LANES))
+        for start in range(0, soundings, 2 * SUB):
+            part = footprint_ref[block, start : start + 2 * SUB, :]
+            sums_ref[row, start : start + 2 * SUB, :] += part[:, :LANES] * left + part[:, LANES:] * right
 
     each(0, blocks, 4, product)
     lanes = lane_ids((8, LANES))
@@ -335,7 +341,7 @@
             footprint_ref, field_ref, out_ref, block, meta_ref[blocks + block], meta_ref[block]
         )
 
-    each(0, blocks, 4, product)
+    each(0, blocks, 8, product)
 
 
 def call(kernel, out_shape, kinds, out_kinds=None, scratch=()):
@@ -347,7 +353,7 @@
         in_specs=[pl.BlockSpec(memory_space=spaces[kind]) for kind in kinds],
         out_specs=[pl.BlockSpec(memory_space=spaces[kind]) for kind in out_kinds],
         scratch_shapes=list(scratch),
-        compiler_params=pltpu.CompilerParams(vmem_limit_bytes=32 * 1024 * 1024),
+        compiler_params=pltpu.CompilerParams(vmem_limit_bytes=16 * 1024 * 1024),
     )
 
 
@@ -389,11 +395,12 @@
             delivered,
             pltpu.SMEM((3 * blocks,), jnp.int32),
             packed_shape,
-            pltpu.VMEM(footprint.shape, footprint.dtype),
+            pltpu.VMEM(footprint.shape, F32),
         ],
         "hhhhh",
         "vsvv",
         [
+            pltpu.VMEM(footprint.shape, footprint.dtype),
             field,
             pltpu.SMEM((peers,), jnp.int32),
             pltpu.SMEM((blocks,), jnp.int32),
@@ -401,7 +408,7 @@
             pltpu.VMEM(observed.shape, F32),
             pltpu.VMEM(weights.shape, F32),
             pltpu.SemaphoreType.DMA((4,)),
-            pltpu.SemaphoreType.DMA((6,)),
+            pltpu.SemaphoreType.DMA((12,)),
         ],
     )(*in_hbm)
     half, collect, pick = call(

time: 202 us -> 200 us (0.990)
  Pallas kernels: 24.5 us -> 21.7 us
where the time goes in v5:
time: 200 us; the launch traced here: 199 us
  blocking collectives  152 us (76%)
  Pallas kernels  21.7 us (11%)
  starting transfers between devices  19.6 us (10%)
  waiting for transfers between devices  4.59 us (2%)
    all_to_all x9, blocking collectives, exchange(): lax.all_to_all(flat, 'orb', split_axis=0, concat_axis=0, axis_index_group...  123 us
    all_to_all x4, blocking collectives, per_device(): lax.all_to_all(partial, 'rep', split_axis=0, concat_axis=0, tiled=True)  28.6 us
    ppermute x5, starting transfers between devices, swap(): return lax.ppermute(array, 'orb', swapped)  19.6 us
    pallas_call x4, Pallas kernels, per_device(): call(functools.partial(adjoint_kernel, iteration, last), [delivered] + ([...  7.54 us
    pallas_call x4, Pallas kernels, per_device(): call(forward_kernel, [shape((reps, 24, LANES), F32)], 'svvv', scratch=[fi...  5.97 us
    ppermute x5, waiting for transfers between devices, swap(): return lax.ppermute(array, 'orb', swapped)  4.59 us
    pallas_call x1, Pallas kernels, per_device(): call(functools.partial(start_kernel, cells), [delivered, pltpu.SMEM((3 *...  4.25 us
  transfers between devices with their start and end apart: 5, of which 5 were waited for; matrix products, arithmetic and copies ran while one was open for 0% of the time, Pallas kernels for 0%

profile of v5, /device:TPU:1, one launch (start us, length us, event | category | flops | bytes accessed | tf_op | source)
XLA Modules:
  0.0 199.2 jit_solution(13644561397450287517)
XLA Ops:
  0.6 4.2 %shard_map.77 = (f32[288,128]{1,0:T(8,128)S(1)}, s32[144]{0:T(256)S(4)}, f32[8,256]{1,0:T(8,128)S(1)}, f32[48,256,256]{2,1,0:T(8,128)S(1)}) custom-call(s32[48]{0:T(128)} %rows_hbm.1, s32[48]{0:T(128)} %cells_hbm.1, f32[8,256]{1,0:T(8,128)} %observed_hbm.1, f32[8,256]{1,0:T(8,128)} %weights_hbm.1, bf16[48,256,256]{2,1,0:T(8,128)(2,1)} %footprint_hbm.1), custom_call_target="tpu_custom_call" | custom-call | tf_op jit(solution)/shard_map/pallas_call | solution.py:392
  4.9 21.1 %all_to_all.65 = f32[32,1,1152]{2,1,0:T(1,128)S(1)} all-to-all(f32[32,1,1152]{2,1,0:T(1,128)S(1)} %bitcast.30), channel_id=1, replica_groups={{0,8,16,24,32,40,48,56,64,72,80,88,96,104,112,120,128,136,144,152,160,1..., dimensions={0} | all-to-all | bytes 294912 | tf_op jit(solution)/shard_map/all_to_all | solution.py:380
  27.1 2.4 %collective-permute-start = (f32[96,256]{1,0:T(8,128)S(1)}, f32[96,256]{1,0:T(8,128)S(1)}, u32[]{:S(2)}, u32[]{:S(2)}) collective-permute-start(f32[96,256]{1,0:T(8,128)S(1)} %get-tuple-element.44.mine_ref), channel_id=1, source_target_pairs={{0,4},{4,0},{8,12},{12,8},{16,20},{20,16},{24,28},{28,24},{32,36},... | collective-permute-start | bytes 294920 | tf_op jit(solution)/shard_map/ppermute | solution.py:386
  29.4 0.9 collective-permute-done.other_ref
  30.5 12.4 %all_to_all.66 = f32[32,1,1024]{2,1,0:T(1,128)S(1)} all-to-all(f32[32,1,1024]{2,1,0:T(1,128)S(1)} %bitcast.35), channel_id=1, replica_groups={{0,8,16,24,32,40,48,56,64,72,80,88,96,104,112,120,128,136,144,152,160,1..., dimensions={0} | all-to-all | bytes 262144 | tf_op jit(solution)/shard_map/all_to_all | solution.py:380
  42.9 1.5 shard_map.80
  44.4 8.4 %all_to_all.67.refs_1_ = f32[4,24,128]{2,1,0:T(8,128)S(1)} all-to-all(f32[4,24,128]{2,1,0:T(8,128)S(1)} %shard_map.80), channel_id=1, replica_groups=mesh['orb'=64,'rep'=4] {'rep'}, dimensions={0} | all-to-all | bytes 98304 | tf_op jit(solution)/shard_map/all_to_all | solution.py:432
  52.8 1.9 shard_map.81
  54.7 13.3 %all_to_all.68 = f32[32,1,1152]{2,1,0:T(1,128)S(1)} all-to-all(f32[32,1,1152]{2,1,0:T(1,128)S(1)} %bitcast.31), channel_id=1, replica_groups={{0,8,16,24,32,40,48,56,64,72,80,88,96,104,112,120,128,136,144,152,160,1..., dimensions={0} | all-to-all | bytes 294912 | tf_op jit(solution)/shard_map/all_to_all | solution.py:380
  68.1 4.4 %collective-permute-start.1 = (f32[72,256]{1,0:T(8,128)S(1)}, f32[72,256]{1,0:T(8,128)S(1)}, u32[]{:S(2)}, u32[]{:S(2)}) collective-permute-start(f32[72,256]{1,0:T(8,128)S(1)} %shard_map.82.refs_0_), channel_id=1, source_target_pairs={{0,4},{4,0},{8,12},{12,8},{16,20},{20,16},{24,28},{28,24},{32,36},... | collective-permute-start | bytes 221192 | tf_op jit(solution)/shard_map/ppermute | solution.py:386
  72.5 0.9 collective-permute-done.1.refs_1_
  73.8 12.4 %all_to_all.69 = f32[32,1,1024]{2,1,0:T(1,128)S(1)} all-to-all(f32[32,1,1024]{2,1,0:T(1,128)S(1)} %bitcast.34), channel_id=1, replica_groups={{0,8,16,24,32,40,48,56,64,72,80,88,96,104,112,120,128,136,144,152,160,1..., dimensions={0} | all-to-all | bytes 262144 | tf_op jit(solution)/shard_map/all_to_all | solution.py:380
  86.2 1.5 shard_map.84
  87.7 6.7 %all_to_all.70.refs_1_ = f32[4,24,128]{2,1,0:T(8,128)S(1)} all-to-all(f32[4,24,128]{2,1,0:T(8,128)S(1)} %shard_map.84), channel_id=1, replica_groups=mesh['orb'=64,'rep'=4] {'rep'}, dimensions={0} | all-to-all | bytes 98304 | tf_op jit(solution)/shard_map/all_to_all | solution.py:432
  94.4 1.9 shard_map.85
  96.3 13.1 %all_to_all.71 = f32[32,1,1152]{2,1,0:T(1,128)S(1)} all-to-all(f32[32,1,1152]{2,1,0:T(1,128)S(1)} %bitcast.29), channel_id=1, replica_groups={{0,8,16,24,32,40,48,56,64,72,80,88,96,104,112,120,128,136,144,152,160,1..., dimensions={0} | all-to-all | bytes 294912 | tf_op jit(solution)/shard_map/all_to_all | solution.py:380
  109.6 4.2 %collective-permute-start.2 = (f32[72,256]{1,0:T(8,128)S(1)}, f32[72,256]{1,0:T(8,128)S(1)}, u32[]{:S(2)}, u32[]{:S(2)}) collective-permute-start(f32[72,256]{1,0:T(8,128)S(1)} %shard_map.86.refs_0_), channel_id=1, source_target_pairs={{0,4},{4,0},{8,12},{12,8},{16,20},{20,16},{24,28},{28,24},{32,36},... | collective-permute-start | bytes 221192 | tf_op jit(solution)/shard_map/ppermute | solution.py:386
  113.8 0.9 collective-permute-done.2.refs_1_
  115.4 12.4 %all_to_all.72 = f32[32,1,1024]{2,1,0:T(1,128)S(1)} all-to-all(f32[32,1,1024]{2,1,0:T(1,128)S(1)} %bitcast.32), channel_id=1, replica_groups={{0,8,16,24,32,40,48,56,64,72,80,88,96,104,112,120,128,136,144,152,160,1..., dimensions={0} | all-to-all | bytes 262144 | tf_op jit(solution)/shard_map/all_to_all | solution.py:380
  127.8 1.5 shard_map.88
  129.3 6.7 %all_to_all.73.refs_1_ = f32[4,24,128]{2,1,0:T(8,128)S(1)} all-to-all(f32[4,24,128]{2,1,0:T(8,128)S(1)} %shard_map.88), channel_id=1, replica_groups=mesh['orb'=64,'rep'=4] {'rep'}, dimensions={0} | all-to-all | bytes 98304 | tf_op jit(solution)/shard_map/all_to_all | solution.py:432
  136.0 1.9 shard_map.89
  137.9 13.1 %all_to_all.74 = f32[32,1,1152]{2,1,0:T(1,128)S(1)} all-to-all(f32[32,1,1152]{2,1,0:T(1,128)S(1)} %bitcast.28), channel_id=1, replica_groups={{0,8,16,24,32,40,48,56,64,72,80,88,96,104,112,120,128,136,144,152,160,1..., dimensions={0} | all-to-all | bytes 294912 | tf_op jit(solution)/shard_map/all_to_all | solution.py:380
  151.2 4.4 %collective-permute-start.3 = (f32[72,256]{1,0:T(8,128)S(1)}, f32[72,256]{1,0:T(8,128)S(1)}, u32[]{:S(2)}, u32[]{:S(2)}) collective-permute-start(f32[72,256]{1,0:T(8,128)S(1)} %shard_map.90.refs_0_), channel_id=1, source_target_pairs={{0,4},{4,0},{8,12},{12,8},{16,20},{20,16},{24,28},{28,24},{32,36},... | collective-permute-start | bytes 221192 | tf_op jit(solution)/shard_map/ppermute | solution.py:386
  155.6 0.9 collective-permute-done.3.refs_1_
  157.2 12.4 %all_to_all.75 = f32[32,1,1024]{2,1,0:T(1,128)S(1)} all-to-all(f32[32,1,1024]{2,1,0:T(1,128)S(1)} %bitcast.33), channel_id=1, replica_groups={{0,8,16,24,32,40,48,56,64,72,80,88,96,104,112,120,128,136,144,152,160,1..., dimensions={0} | all-to-all | bytes 262144 | tf_op jit(solution)/shard_map/all_to_all | solution.py:380
  169.5 1.5 shard_map.92
  171.0 6.7 %all_to_all.76.refs_1_ = f32[4,24,128]{2,1,0:T(8,128)S(1)} all-to-all(f32[4,24,128]{2,1,0:T(8,128)S(1)} %shard_map.92), channel_id=1, replica_groups=mesh['orb'=64,'rep'=4] {'rep'}, dimensions={0} | all-to-all | bytes 98304 | tf_op jit(solution)/shard_map/all_to_all | solution.py:432
  177.8 1.9 shard_map.93
  179.7 13.1 %all_to_all.77 = f32[32,1,1152]{2,1,0:T(1,128)S(1)} all-to-all(f32[32,1,1152]{2,1,0:T(1,128)S(1)} %bitcast.23), channel_id=1, replica_groups={{0,8,16,24,32,40,48,56,64,72,80,88,96,104,112,120,128,136,144,152,160,1..., dimensions={0} | all-to-all | bytes 294912 | tf_op jit(solution)/shard_map/all_to_all | solution.py:380
  192.9 4.2 %collective-permute-start.4 = (f32[72,256]{1,0:T(8,128)S(1)}, f32[72,256]{1,0:T(8,128)S(1)}, u32[]{:S(2)}, u32[]{:S(2)}) collective-permute-start(f32[72,256]{1,0:T(8,128)S(1)} %shard_map.94.refs_0_), channel_id=1, source_target_pairs={{0,4},{4,0},{8,12},{12,8},{16,20},{20,16},{24,28},{28,24},{32,36},... | collective-permute-start | bytes 221192 | tf_op jit(solution)/shard_map/ppermute | solution.py:386
  198.1 1.1 shard_map.95
  (12 shorter events, 4.5 us)
Async XLA Ops:
  26.0 0.8 copy-start
  27.1 3.3 %collective-permute-start = (f32[96,256]{1,0:T(8,128)S(1)}, f32[96,256]{1,0:T(8,128)S(1)}, u32[]{:S(2)}, u32[]{:S(2)}) collective-permute-start(f32[96,256]{1,0:T(8,128)S(1)} %get-tuple-element.44.mine_ref), channel_id=1, source_target_pairs={{0,4},{4,0},{8,12},{12,8},{16,20},{20,16},{24,28},{28,24},{32,36},... | collective-permute-start | bytes 294920 | tf_op jit(solution)/shard_map/ppermute | solution.py:386
  68.1 5.3 %collective-permute-start.1 = (f32[72,256]{1,0:T(8,128)S(1)}, f32[72,256]{1,0:T(8,128)S(1)}, u32[]{:S(2)}, u32[]{:S(2)}) collective-permute-start(f32[72,256]{1,0:T(8,128)S(1)} %shard_map.82.refs_0_), channel_id=1, source_target_pairs={{0,4},{4,0},{8,12},{12,8},{16,20},{20,16},{24,28},{28,24},{32,36},... | collective-permute-start | bytes 221192 | tf_op jit(solution)/shard_map/ppermute | solution.py:386
  109.6 5.1 %collective-permute-start.2 = (f32[72,256]{1,0:T(8,128)S(1)}, f32[72,256]{1,0:T(8,128)S(1)}, u32[]{:S(2)}, u32[]{:S(2)}) collective-permute-start(f32[72,256]{1,0:T(8,128)S(1)} %shard_map.86.refs_0_), channel_id=1, source_target_pairs={{0,4},{4,0},{8,12},{12,8},{16,20},{20,16},{24,28},{28,24},{32,36},... | collective-permute-start | bytes 221192 | tf_op jit(solution)/shard_map/ppermute | solution.py:386
  151.2 5.3 %collective-permute-start.3 = (f32[72,256]{1,0:T(8,128)S(1)}, f32[72,256]{1,0:T(8,128)S(1)}, u32[]{:S(2)}, u32[]{:S(2)}) collective-permute-start(f32[72,256]{1,0:T(8,128)S(1)} %shard_map.90.refs_0_), channel_id=1, source_target_pairs={{0,4},{4,0},{8,12},{12,8},{16,20},{20,16},{24,28},{28,24},{32,36},... | collective-permute-start | bytes 221192 | tf_op jit(solution)/shard_map/ppermute | solution.py:386
  192.9 5.1 %collective-permute-start.4 = (f32[72,256]{1,0:T(8,128)S(1)}, f32[72,256]{1,0:T(8,128)S(1)}, u32[]{:S(2)}, u32[]{:S(2)}) collective-permute-start(f32[72,256]{1,0:T(8,128)S(1)} %shard_map.94.refs_0_), channel_id=1, source_target_pairs={{0,4},{4,0},{8,12},{12,8},{16,20},{20,16},{24,28},{28,24},{32,36},... | collective-permute-start | bytes 221192 | tf_op jit(solution)/shard_map/ppermute | solution.py:386

commit v6 on v5

--- a/solution.py
+++ b/solution.py
@@ -75,8 +75,8 @@
 
 
 def start_kernel(
-    cells, rows_hbm, cells_hbm, observed_hbm, weights_hbm, footprint_hbm,
-    out_ref, meta_ref, packed_ref, footprint_ref,
+    cells, rows_hbm, cells_hbm, observed_hbm, weights_hbm, prior_hbm, footprint_hbm,
+    out_ref, meta_ref, packed_ref, prior_ref, footprint_ref,
     arrived_ref, field_ref, count_ref, rows_ref, cells_ref, observed_ref, weights_ref, sems, chunk_sems
 ):
     blocks = footprint_ref.shape[0]
@@ -92,6 +92,7 @@
                 (cells_hbm, cells_ref),
                 (observed_hbm, observed_ref),
                 (weights_hbm, weights_ref),
+                (prior_hbm, prior_ref),
             ]
         )
     ]
@@ -108,7 +109,7 @@
     out_ref[...] = jnp.zeros_like(out_ref)
     for peer in range(peers):
         count_ref[peer] = 0
-    for copy in small:
+    for copy in small[:-1]:
         copy.wait()
     weights = weights_ref[...]
     columns = in_columns(weights * observed_ref[...])
@@ -146,6 +147,7 @@
         if chunk + IN_FLIGHT < chunks:
             large[chunk + IN_FLIGHT].start()
         each(chunk * size, (chunk + 1) * size, 4, product)
+    small[-1].wait()
 
 
 def serve(residual, pick, out_ref):
@@ -178,16 +180,32 @@
     return jnp.broadcast_to(row, (8, LANES))
 
 
-def row_of_scalars(values):
+def everywhere(values, lane):
+    return jnp.broadcast_to(values[:, lane : lane + 1], (8, LANES))
+
+
+def spanning(tile, shape):
+    rows, columns = shape
+    return jnp.concatenate([jnp.concatenate([tile] * (columns // LANES), axis=1)] * (rows // 8), axis=0)
+
+
+def lane_sums(values):
+    tiles = [
+        values[row : row + 8, column : column + LANES]
+        for row in range(0, values.shape[0], 8)
+        for column in range(0, values.shape[1], LANES)
+    ]
+    while len(tiles) > 1:
+        tiles = [sum(tiles[at : at + 2]) for at in range(0, len(tiles), 2)]
+    return jnp.broadcast_to(jnp.sum(tiles[0], axis=1, keepdims=True), (8, LANES))
+
+
+def in_lanes(sums, first=0):
     lanes = lane_ids((8, LANES))
-    row = jnp.zeros((8, LANES), F32)
-    for lane, value in enumerate(values):
-        row = jnp.where(lanes == lane, value, row)
-    return row
-
-
-def total(values):
-    return jnp.sum(jnp.sum(values, axis=0, keepdims=True), axis=1, keepdims=True)
+    packed = jnp.zeros((8, LANES), F32)
+    for lane, value in enumerate(sums, first):
+        packed = jnp.where(lanes == lane, value, packed)
+    return packed
 
 
 def first_gather_kernel(in_ref, prior_ref, half_ref, collect_ref, pick_ref):
@@ -216,10 +234,12 @@
 
 
 def partial_sums(prior, residual, direction=None):
-    values = [0.5 * residual * residual, 0.5 * prior * residual * residual]
+    halved = 0.5 * residual
+    weighted = prior * halved
+    values = [halved * residual, weighted * residual]
     if direction is not None:
-        values.append(0.5 * prior * residual * direction)
-    return row_of_scalars([total(value) for value in values])
+        values.append(weighted * direction)
+    return in_lanes([lane_sums(value) for value in values])
 
 
 def first_update_kernel(mine_ref, other_ref, pick_ref, prior_ref, residual_ref, sums_ref, out_ref):
@@ -240,35 +260,38 @@
     mine_ref, other_ref, pick_ref, prior_ref, residual_ref, *refs = refs
     if not first:
         state_ref, direction_ref, image_ref, solution_ref, *refs = refs
-    cells = residual_ref.shape[0]
-    sums = mine_ref[cells : cells + 1, :] + other_ref[cells : cells + 1, :]
-    norm, prior_rr, prior_rd, forward_rr, forward_rd = [sums[:, at : at + 1] for at in range(5)]
+    cells, width = residual_ref.shape
+    sums = mine_ref[cells : cells + 8, :LANES] + other_ref[cells : cells + 8, :LANES]
+    norm, prior_rr, prior_rd, forward_rr, forward_rd = [everywhere(sums, at) for at in range(5)]
     prior = prior_ref[...]
     residual = residual_ref[...]
     image = mine_ref[0:cells, :] + other_ref[0:cells, :] + prior * residual
-    beta = jnp.zeros((1, 1), F32)
     direction, prior_dd, forward_dd = residual, prior_rr, forward_rr
     if not first:
-        beta = norm / state_ref[0:1, 0:1]
-        prior_dd = prior_rr + beta * (2.0 * prior_rd + beta * state_ref[0:1, 1:2])
-        forward_dd = forward_rr + beta * (2.0 * forward_rd + beta * state_ref[0:1, 2:3])
-        direction = residual + beta * direction_ref[...]
-        image = image + beta * image_ref[...]
-    alpha = norm / (prior_dd + forward_dd)
+        beta = norm / state_ref[0:8, :]
+        prior_dd = prior_rr + beta * (2.0 * prior_rd + beta * state_ref[8:16, :])
+        forward_dd = forward_rr + beta * (2.0 * forward_rd + beta * state_ref[16:24, :])
+        wide = spanning(beta, (cells, width))
+        direction = residual + wide * direction_ref[...]
+        image = image + wide * image_ref[...]
+    alpha = spanning(norm / (prior_dd + forward_dd), (cells, width))
+    new_residual = residual - alpha * image
     solution = alpha * direction if first else solution_ref[...] + alpha * direction
-    residual = residual - alpha * image
     if last:
         new_solution_ref, new_residual_ref = refs
         own = cells // CORES
         core_first = lax.axis_index("orb") % CORES == 0
         new_solution_ref[...] = jnp.where(core_first, solution[:own], solution[own:])
-        new_residual_ref[...] = jnp.where(core_first, residual[:own], residual[own:])
+        new_residual_ref[...] = jnp.where(core_first, new_residual[:own], new_residual[own:])
         return
     new_residual_ref, sums_ref, out_ref, new_state_ref, new_direction_ref, new_image_ref, new_solution_ref = refs
-    serve(residual, pick_ref[...], out_ref)
-    sums_ref[...] = partial_sums(prior, residual, direction)
-    new_residual_ref[...] = residual
-    new_state_ref[...] = row_of_scalars([norm, prior_dd, forward_dd, beta])
+    serve(new_residual, pick_ref[...], out_ref)
+    sums_ref[...] = partial_sums(prior, new_residual, direction)
+    new_residual_ref[...] = new_residual
+    new_state_ref[0:8, :] = norm
+    new_state_ref[8:16, :] = prior_dd
+    new_state_ref[16:24, :] = forward_dd
+    new_state_ref[24:32, :] = jnp.zeros_like(norm) if first else beta
     new_direction_ref[...] = direction
     new_image_ref[...] = image
     new_solution_ref[...] = solution
@@ -323,18 +346,18 @@
     *refs, field_ref = refs
     out_ref[...] = jnp.zeros_like(out_ref)
     spread(field, field_ref)
-    lanes = lane_ids((8, LANES))
-    scalars = jnp.where(lanes == 3, total(field * forward), summed[16:24])
+    sums = [lane_sums(field * forward)]
     if iteration > 0:
         direction = old_ref[...]
         if iteration > 1:
-            direction = direction + state_ref[0:1, 3:4] * older_ref[...]
-        scalars = jnp.where(lanes == 4, total(field * direction), scalars)
+            direction = direction + spanning(state_ref[24:32, :], direction.shape) * older_ref[...]
+        sums.append(lane_sums(field * direction))
     if not last:
         refs[0][...] = forward
         if iteration > 0:
             refs[1][...] = direction
-    out_ref[pl.ds(FETCH, peers, stride=DELIVER), :] = jnp.broadcast_to(scalars[0:1], (peers, LANES))
+    scalars = jnp.sum(summed[16:24] + in_lanes(sums, 3), axis=0, keepdims=True)
+    out_ref[pl.ds(FETCH, peers, stride=DELIVER), :] = jnp.broadcast_to(scalars, (peers, LANES))
 
     def product(block):
         transposed_product(
@@ -370,6 +393,7 @@
     delivered = shape((peers * DELIVER, LANES), F32)
     packed_shape = shape((8, soundings * rows // 8), F32)
     scalar_shape = shape((8, LANES), F32)
+    state_shape = shape((32, LANES), F32)
     region = shape((cells, width), F32)
     field = pltpu.VMEM((rows, soundings, LANES), F32)
     same_core = [[CORES * peer + core for peer in range(peers)] for core in range(CORES)]
@@ -387,18 +411,19 @@
 
     in_hbm = [
         pltpu.with_memory_space_constraint(array, pltpu.HBM)
-        for array in (block_rows, block_cells, observed, weights, footprint)
+        for array in (block_rows, block_cells, observed, weights, precision_prior, footprint)
     ]
-    outgoing, meta, packed_weights, footprint = call(
+    outgoing, meta, packed_weights, own_prior, footprint = call(
         functools.partial(start_kernel, cells),
         [
             delivered,
             pltpu.SMEM((3 * blocks,), jnp.int32),
             packed_shape,
+            pltpu.VMEM(precision_prior.shape, F32),
             pltpu.VMEM(footprint.shape, F32),
         ],
-        "hhhhh",
-        "vsvv",
+        "hhhhhh",
+        "vsvvv",
         [
             pltpu.VMEM(footprint.shape, footprint.dtype),
             field,
@@ -407,7 +432,7 @@
             pltpu.SMEM((blocks,), jnp.int32),
             pltpu.VMEM(observed.shape, F32),
             pltpu.VMEM(weights.shape, F32),
-            pltpu.SemaphoreType.DMA((4,)),
+            pltpu.SemaphoreType.DMA((5,)),
             pltpu.SemaphoreType.DMA((12,)),
         ],
     )(*in_hbm)
@@ -419,7 +444,7 @@
             shape((CAP * peers, 4 * cells), BF16),
         ],
         "vv",
-    )(exchange(outgoing), precision_prior)
+    )(exchange(outgoing), own_prior)
     prior, residual, sums, outgoing = call(
         first_update_kernel, [region, region, scalar_shape, fetched], "vvv"
     )(half, swap(half), pick)
@@ -447,7 +472,7 @@
             functools.partial(update_kernel, first, last),
             [shape((own, width), F32)] * 2
             if last
-            else [region, scalar_shape, fetched, scalar_shape, region, region, region],
+            else [region, scalar_shape, fetched, state_shape, region, region, region],
             "v" * len(operands),
         )(*operands)
         if not last:

time: 200 us -> 198 us (0.990)
  no operation moved by 1% of the time
where the time goes in v6:
time: 198 us; the launch traced here: 197 us
  blocking collectives  152 us (77%)
  Pallas kernels  20.2 us (10%)
  starting transfers between devices  19.4 us (10%)
  waiting for transfers between devices  4.59 us (2%)
    all_to_all x9, blocking collectives, exchange(): lax.all_to_all(flat, 'orb', split_axis=0, concat_axis=0, axis_index_group...  123 us
    all_to_all x4, blocking collectives, per_device(): lax.all_to_all(partial, 'rep', split_axis=0, concat_axis=0, tiled=True)  28.6 us
    ppermute x5, starting transfers between devices, swap(): return lax.ppermute(array, 'orb', swapped)  19.4 us
    pallas_call x4, Pallas kernels, per_device(): call(functools.partial(adjoint_kernel, iteration, last), [delivered] + ([...  7.38 us
    pallas_call x4, Pallas kernels, per_device(): call(forward_kernel, [shape((reps, 24, LANES), F32)], 'svvv', scratch=[fi...  6.13 us
    ppermute x5, waiting for transfers between devices, swap(): return lax.ppermute(array, 'orb', swapped)  4.59 us
    pallas_call x1, Pallas kernels, per_device(): call(functools.partial(start_kernel, cells), [delivered, pltpu.SMEM((3 *...  4.1 us
  transfers between devices with their start and end apart: 5, of which 5 were waited for; matrix products, arithmetic and copies ran while one was open for 0% of the time, Pallas kernels for 0%

profile of v6, /device:TPU:1, one launch (start us, length us, event | category | flops | bytes accessed | tf_op | source)
XLA Modules:
  0.0 197.0 jit_solution(8852610570500188704)
XLA Ops:
  0.6 4.1 %shard_map.77 = (f32[288,128]{1,0:T(8,128)S(1)}, s32[144]{0:T(256)S(4)}, f32[8,256]{1,0:T(8,128)S(1)}, f32[32,256]{1,0:T(8,128)S(1)}, f32[48,256,256]{2,1,0:T(8,128)S(1)}) custom-call(s32[48]{0:T(128)} %rows_hbm.1, s32[48]{0:T(128)} %cells_hbm.1, f32[8,256]{1,0:T(8,128)} %observed_hbm.1, f32[8,256]{1,0:T(8,128)} %weights_hbm.1, f32[32,256]{1,0:T(8,128)} %prior_hbm.1, ...), custom_call_target="tpu_custom_call" | custom-call | tf_op jit(solution)/shard_map/pallas_call | solution.py:416
  4.7 21.1 %all_to_all.65 = f32[32,1,1152]{2,1,0:T(1,128)S(1)} all-to-all(f32[32,1,1152]{2,1,0:T(1,128)S(1)} %bitcast.29), channel_id=1, replica_groups={{0,8,16,24,32,40,48,56,64,72,80,88,96,104,112,120,128,136,144,152,160,1..., dimensions={0} | all-to-all | bytes 294912 | tf_op jit(solution)/shard_map/all_to_all | solution.py:404
  26.2 2.4 %collective-permute-start = (f32[96,256]{1,0:T(8,128)S(1)}, f32[96,256]{1,0:T(8,128)S(1)}, u32[]{:S(2)}, u32[]{:S(2)}) collective-permute-start(f32[96,256]{1,0:T(8,128)S(1)} %get-tuple-element.46.mine_ref), channel_id=1, source_target_pairs={{0,4},{4,0},{8,12},{12,8},{16,20},{20,16},{24,28},{28,24},{32,36},... | collective-permute-start | bytes 294920 | tf_op jit(solution)/shard_map/ppermute | solution.py:410
  28.5 0.9 collective-permute-done.other_ref
  29.6 12.4 %all_to_all.66 = f32[32,1,1024]{2,1,0:T(1,128)S(1)} all-to-all(f32[32,1,1024]{2,1,0:T(1,128)S(1)} %bitcast.35), channel_id=1, replica_groups={{0,8,16,24,32,40,48,56,64,72,80,88,96,104,112,120,128,136,144,152,160,1..., dimensions={0} | all-to-all | bytes 262144 | tf_op jit(solution)/shard_map/all_to_all | solution.py:404
  42.0 1.5 shard_map.80
  43.6 8.4 %all_to_all.67.refs_1_ = f32[4,24,128]{2,1,0:T(8,128)S(1)} all-to-all(f32[4,24,128]{2,1,0:T(8,128)S(1)} %shard_map.80), channel_id=1, replica_groups=mesh['orb'=64,'rep'=4] {'rep'}, dimensions={0} | all-to-all | bytes 98304 | tf_op jit(solution)/shard_map/all_to_all | solution.py:457
  51.9 1.8 shard_map.81
  53.8 13.3 %all_to_all.68 = f32[32,1,1152]{2,1,0:T(1,128)S(1)} all-to-all(f32[32,1,1152]{2,1,0:T(1,128)S(1)} %bitcast.31), channel_id=1, replica_groups={{0,8,16,24,32,40,48,56,64,72,80,88,96,104,112,120,128,136,144,152,160,1..., dimensions={0} | all-to-all | bytes 294912 | tf_op jit(solution)/shard_map/all_to_all | solution.py:404
  67.2 4.4 %collective-permute-start.1 = (f32[72,256]{1,0:T(8,128)S(1)}, f32[72,256]{1,0:T(8,128)S(1)}, u32[]{:S(2)}, u32[]{:S(2)}) collective-permute-start(f32[72,256]{1,0:T(8,128)S(1)} %shard_map.82.refs_0_), channel_id=1, source_target_pairs={{0,4},{4,0},{8,12},{12,8},{16,20},{20,16},{24,28},{28,24},{32,36},... | collective-permute-start | bytes 221192 | tf_op jit(solution)/shard_map/ppermute | solution.py:410
  71.6 0.9 collective-permute-done.1.refs_1_
  72.8 12.4 %all_to_all.69 = f32[32,1,1024]{2,1,0:T(1,128)S(1)} all-to-all(f32[32,1,1024]{2,1,0:T(1,128)S(1)} %bitcast.34), channel_id=1, replica_groups={{0,8,16,24,32,40,48,56,64,72,80,88,96,104,112,120,128,136,144,152,160,1..., dimensions={0} | all-to-all | bytes 262144 | tf_op jit(solution)/shard_map/all_to_all | solution.py:404
  85.2 1.5 shard_map.84
  86.7 6.7 %all_to_all.70.refs_1_ = f32[4,24,128]{2,1,0:T(8,128)S(1)} all-to-all(f32[4,24,128]{2,1,0:T(8,128)S(1)} %shard_map.84), channel_id=1, replica_groups=mesh['orb'=64,'rep'=4] {'rep'}, dimensions={0} | all-to-all | bytes 98304 | tf_op jit(solution)/shard_map/all_to_all | solution.py:457
  93.4 1.9 shard_map.85
  95.3 13.1 %all_to_all.71 = f32[32,1,1152]{2,1,0:T(1,128)S(1)} all-to-all(f32[32,1,1152]{2,1,0:T(1,128)S(1)} %bitcast.30), channel_id=1, replica_groups={{0,8,16,24,32,40,48,56,64,72,80,88,96,104,112,120,128,136,144,152,160,1..., dimensions={0} | all-to-all | bytes 294912 | tf_op jit(solution)/shard_map/all_to_all | solution.py:404
  108.6 4.2 %collective-permute-start.2 = (f32[72,256]{1,0:T(8,128)S(1)}, f32[72,256]{1,0:T(8,128)S(1)}, u32[]{:S(2)}, u32[]{:S(2)}) collective-permute-start(f32[72,256]{1,0:T(8,128)S(1)} %shard_map.86.refs_0_), channel_id=1, source_target_pairs={{0,4},{4,0},{8,12},{12,8},{16,20},{20,16},{24,28},{28,24},{32,36},... | collective-permute-start | bytes 221192 | tf_op jit(solution)/shard_map/ppermute | solution.py:410
  112.8 0.9 collective-permute-done.2.refs_1_
  114.0 12.4 %all_to_all.72 = f32[32,1,1024]{2,1,0:T(1,128)S(1)} all-to-all(f32[32,1,1024]{2,1,0:T(1,128)S(1)} %bitcast.32), channel_id=1, replica_groups={{0,8,16,24,32,40,48,56,64,72,80,88,96,104,112,120,128,136,144,152,160,1..., dimensions={0} | all-to-all | bytes 262144 | tf_op jit(solution)/shard_map/all_to_all | solution.py:404
  126.3 1.5 shard_map.88
  127.9 6.7 %all_to_all.73.refs_1_ = f32[4,24,128]{2,1,0:T(8,128)S(1)} all-to-all(f32[4,24,128]{2,1,0:T(8,128)S(1)} %shard_map.88), channel_id=1, replica_groups=mesh['orb'=64,'rep'=4] {'rep'}, dimensions={0} | all-to-all | bytes 98304 | tf_op jit(solution)/shard_map/all_to_all | solution.py:457
  134.6 1.9 shard_map.89
  136.5 13.1 %all_to_all.74 = f32[32,1,1152]{2,1,0:T(1,128)S(1)} all-to-all(f32[32,1,1152]{2,1,0:T(1,128)S(1)} %bitcast.28), channel_id=1, replica_groups={{0,8,16,24,32,40,48,56,64,72,80,88,96,104,112,120,128,136,144,152,160,1..., dimensions={0} | all-to-all | bytes 294912 | tf_op jit(solution)/shard_map/all_to_all | solution.py:404
  149.7 4.2 %collective-permute-start.3 = (f32[72,256]{1,0:T(8,128)S(1)}, f32[72,256]{1,0:T(8,128)S(1)}, u32[]{:S(2)}, u32[]{:S(2)}) collective-permute-start(f32[72,256]{1,0:T(8,128)S(1)} %shard_map.90.refs_0_), channel_id=1, source_target_pairs={{0,4},{4,0},{8,12},{12,8},{16,20},{20,16},{24,28},{28,24},{32,36},... | collective-permute-start | bytes 221192 | tf_op jit(solution)/shard_map/ppermute | solution.py:410
  154.0 0.9 collective-permute-done.3.refs_1_
  155.2 12.5 %all_to_all.75 = f32[32,1,1024]{2,1,0:T(1,128)S(1)} all-to-all(f32[32,1,1024]{2,1,0:T(1,128)S(1)} %bitcast.33), channel_id=1, replica_groups={{0,8,16,24,32,40,48,56,64,72,80,88,96,104,112,120,128,136,144,152,160,1..., dimensions={0} | all-to-all | bytes 262144 | tf_op jit(solution)/shard_map/all_to_all | solution.py:404
  167.7 1.5 shard_map.92
  169.2 6.7 %all_to_all.76.refs_1_ = f32[4,24,128]{2,1,0:T(8,128)S(1)} all-to-all(f32[4,24,128]{2,1,0:T(8,128)S(1)} %shard_map.92), channel_id=1, replica_groups=mesh['orb'=64,'rep'=4] {'rep'}, dimensions={0} | all-to-all | bytes 98304 | tf_op jit(solution)/shard_map/all_to_all | solution.py:457
  176.0 1.9 shard_map.93
  177.8 13.1 %all_to_all.77 = f32[32,1,1152]{2,1,0:T(1,128)S(1)} all-to-all(f32[32,1,1152]{2,1,0:T(1,128)S(1)} %bitcast.23), channel_id=1, replica_groups={{0,8,16,24,32,40,48,56,64,72,80,88,96,104,112,120,128,136,144,152,160,1..., dimensions={0} | all-to-all | bytes 294912 | tf_op jit(solution)/shard_map/all_to_all | solution.py:404
  191.1 4.2 %collective-permute-start.4 = (f32[72,256]{1,0:T(8,128)S(1)}, f32[72,256]{1,0:T(8,128)S(1)}, u32[]{:S(2)}, u32[]{:S(2)}) collective-permute-start(f32[72,256]{1,0:T(8,128)S(1)} %shard_map.94.refs_0_), channel_id=1, source_target_pairs={{0,4},{4,0},{8,12},{12,8},{16,20},{20,16},{24,28},{28,24},{32,36},... | collective-permute-start | bytes 221192 | tf_op jit(solution)/shard_map/ppermute | solution.py:410
  195.3 0.9 collective-permute-done.4.refs_1_
  (10 shorter events, 2.6 us)
Async XLA Ops:
  26.2 3.3 %collective-permute-start = (f32[96,256]{1,0:T(8,128)S(1)}, f32[96,256]{1,0:T(8,128)S(1)}, u32[]{:S(2)}, u32[]{:S(2)}) collective-permute-start(f32[96,256]{1,0:T(8,128)S(1)} %get-tuple-element.46.mine_ref), channel_id=1, source_target_pairs={{0,4},{4,0},{8,12},{12,8},{16,20},{20,16},{24,28},{28,24},{32,36},... | collective-permute-start | bytes 294920 | tf_op jit(solution)/shard_map/ppermute | solution.py:410
  67.2 5.3 %collective-permute-start.1 = (f32[72,256]{1,0:T(8,128)S(1)}, f32[72,256]{1,0:T(8,128)S(1)}, u32[]{:S(2)}, u32[]{:S(2)}) collective-permute-start(f32[72,256]{1,0:T(8,128)S(1)} %shard_map.82.refs_0_), channel_id=1, source_target_pairs={{0,4},{4,0},{8,12},{12,8},{16,20},{20,16},{24,28},{28,24},{32,36},... | collective-permute-start | bytes 221192 | tf_op jit(solution)/shard_map/ppermute | solution.py:410
  108.6 5.1 %collective-permute-start.2 = (f32[72,256]{1,0:T(8,128)S(1)}, f32[72,256]{1,0:T(8,128)S(1)}, u32[]{:S(2)}, u32[]{:S(2)}) collective-permute-start(f32[72,256]{1,0:T(8,128)S(1)} %shard_map.86.refs_0_), channel_id=1, source_target_pairs={{0,4},{4,0},{8,12},{12,8},{16,20},{20,16},{24,28},{28,24},{32,36},... | collective-permute-start | bytes 221192 | tf_op jit(solution)/shard_map/ppermute | solution.py:410
  149.7 5.1 %collective-permute-start.3 = (f32[72,256]{1,0:T(8,128)S(1)}, f32[72,256]{1,0:T(8,128)S(1)}, u32[]{:S(2)}, u32[]{:S(2)}) collective-permute-start(f32[72,256]{1,0:T(8,128)S(1)} %shard_map.90.refs_0_), channel_id=1, source_target_pairs={{0,4},{4,0},{8,12},{12,8},{16,20},{20,16},{24,28},{28,24},{32,36},... | collective-permute-start | bytes 221192 | tf_op jit(solution)/shard_map/ppermute | solution.py:410
  191.1 5.1 %collective-permute-start.4 = (f32[72,256]{1,0:T(8,128)S(1)}, f32[72,256]{1,0:T(8,128)S(1)}, u32[]{:S(2)}, u32[]{:S(2)}) collective-permute-start(f32[72,256]{1,0:T(8,128)S(1)} %shard_map.94.refs_0_), channel_id=1, source_target_pairs={{0,4},{4,0},{8,12},{12,8},{16,20},{20,16},{24,28},{28,24},{32,36},... | collective-permute-start | bytes 221192 | tf_op jit(solution)/shard_map/ppermute | solution.py:410

commit v7 on v6

--- a/solution.py
+++ b/solution.py
@@ -324,13 +324,11 @@
                 packed[row % 4] = jnp.where(lanes == rows * at + row, summed, packed[row % 4])
         halves.append((packed[0] + packed[1]) + (packed[2] + packed[3]))
     halves.append(scalars_ref[...])
-    message = jnp.concatenate(halves, axis=0)
-    for peer in range(out_ref.shape[0]):
-        out_ref[peer] = message
+    out_ref[...] = jnp.concatenate(halves, axis=0)
 
 
 def adjoint_kernel(iteration, last, *refs):
-    meta_ref, in_ref, weights_ref, footprint_ref, *refs = refs
+    meta_ref, own_ref, next_ref, previous_ref, opposite_ref, weights_ref, footprint_ref, *refs = refs
     if iteration > 0:
         state_ref, old_ref, *refs = refs
     if iteration > 1:
@@ -338,9 +336,7 @@
     out_ref, *refs = refs
     blocks = footprint_ref.shape[0]
     peers = out_ref.shape[0] // DELIVER
-    summed = in_ref[0]
-    for peer in range(1, in_ref.shape[0]):
-        summed = summed + in_ref[peer]
+    summed = (own_ref[...] + opposite_ref[...]) + (next_ref[...] + previous_ref[...])
     forward = jnp.concatenate([summed[0:8], summed[8:16]], axis=1)
     field = weights_ref[...] * forward
     *refs, field_ref = refs
@@ -452,10 +448,13 @@
     for iteration in range(ITERS):
         first, last = iteration == 0, iteration == ITERS - 1
         (partial,) = call(
-            forward_kernel, [shape((reps, 24, LANES), F32)], "svvv", scratch=[field]
+            forward_kernel, [shape((24, LANES), F32)], "svvv", scratch=[field]
         )(meta, exchange(outgoing), sums, footprint)
-        partial = lax.all_to_all(partial, "rep", split_axis=0, concat_axis=0, tiled=True)
-        operands = [meta, partial, packed_weights, footprint]
+        others = [
+            lax.ppermute(partial, "rep", [(device, (device + by) % reps) for device in range(reps)])
+            for by in (1, 3, 2)
+        ]
+        operands = [meta, partial, *others, packed_weights, footprint]
         operands += [] if first else [state, *images]
         outgoing, *images = call(
             functools.partial(adjoint_kernel, iteration, last),

time: 198 us -> 194 us (0.980)
  blocking collectives: 152 us -> 124 us
  waiting for transfers between devices: 4.59 us -> 18 us
  starting transfers between devices: 19.4 us -> 30.5 us
    all_to_all x4 -> x0, blocking collectives: 28.6 us -> none  [per_device(): lax.all_to_all(partial, 'rep', split_axis=0, concat_axis=0, tiled=True)]
    ppermute x0 -> x12, waiting for transfers between devices: none -> 13.4 us  [per_device(): lax.ppermute(partial, 'rep', [(device, (device + by) % reps) for device i...]
    ppermute x0 -> x12, starting transfers between devices: none -> 10.3 us  [per_device(): lax.ppermute(partial, 'rep', [(device, (device + by) % reps) for device i...]
  transfers between devices with their start and end apart: 5 -> 17, of which waited for: 5 -> 13; matrix products, arithmetic and copies ran while one was open for 0% -> 0% of each run, Pallas kernels for 0% -> 0%
where the time goes in v7:
time: 194 us; the launch traced here: 193 us
  blocking collectives  124 us (64%)
  starting transfers between devices  30.5 us (16%)
  Pallas kernels  20.2 us (10%)
  waiting for transfers between devices  18 us (9%)
    all_to_all x9, blocking collectives, exchange(): lax.all_to_all(flat, 'orb', split_axis=0, concat_axis=0, axis_index_group...  124 us
    ppermute x5, starting transfers between devices, swap(): return lax.ppermute(array, 'orb', swapped)  20.2 us
    ppermute x12, waiting for transfers between devices, per_device(): lax.ppermute(partial, 'rep', [(device, (device + by) % reps) for device i...  13.4 us
    ppermute x12, starting transfers between devices, per_device(): lax.ppermute(partial, 'rep', [(device, (device + by) % reps) for device i...  10.3 us
    pallas_call x4, Pallas kernels, per_device(): call(functools.partial(adjoint_kernel, iteration, last), [delivered] + ([...  7.38 us
    pallas_call x4, Pallas kernels, per_device(): call(forward_kernel, [shape((24, LANES), F32)], 'svvv', scratch=[field])  6.11 us
    ppermute x5, waiting for transfers between devices, swap(): return lax.ppermute(array, 'orb', swapped)  4.59 us
    pallas_call x1, Pallas kernels, per_device(): call(functools.partial(start_kernel, cells), [delivered, pltpu.SMEM((3 *...  4.1 us
  transfers between devices with their start and end apart: 17, of which 13 were waited for; matrix products, arithmetic and copies ran while one was open for 0% of the time, Pallas kernels for 0%

profile of v7, /device:TPU:1, one launch (start us, length us, event | category | flops | bytes accessed | tf_op | source)
XLA Modules:
  0.0 193.3 jit_solution(1449810604517898193)
XLA Ops:
  0.6 4.1 %shard_map.77 = (f32[288,128]{1,0:T(8,128)S(1)}, s32[144]{0:T(256)S(4)}, f32[8,256]{1,0:T(8,128)S(1)}, f32[32,256]{1,0:T(8,128)S(1)}, f32[48,256,256]{2,1,0:T(8,128)S(1)}) custom-call(s32[48]{0:T(128)} %rows_hbm.1, s32[48]{0:T(128)} %cells_hbm.1, f32[8,256]{1,0:T(8,128)} %observed_hbm.1, f32[8,256]{1,0:T(8,128)} %weights_hbm.1, f32[32,256]{1,0:T(8,128)} %prior_hbm.1, ...), custom_call_target="tpu_custom_call" | custom-call | tf_op jit(solution)/shard_map/pallas_call | solution.py:412
  4.7 21.1 %all_to_all.45 = f32[32,1,1152]{2,1,0:T(1,128)S(1)} all-to-all(f32[32,1,1152]{2,1,0:T(1,128)S(1)} %bitcast.31), channel_id=1, replica_groups={{0,8,16,24,32,40,48,56,64,72,80,88,96,104,112,120,128,136,144,152,160,1..., dimensions={0} | all-to-all | bytes 294912 | tf_op jit(solution)/shard_map/all_to_all | solution.py:400
  26.2 2.4 %collective-permute-start = (f32[96,256]{1,0:T(8,128)S(1)}, f32[96,256]{1,0:T(8,128)S(1)}, u32[]{:S(2)}, u32[]{:S(2)}) collective-permute-start(f32[96,256]{1,0:T(8,128)S(1)} %get-tuple-element.46.mine_ref), channel_id=1, source_target_pairs={{0,4},{4,0},{8,12},{12,8},{16,20},{20,16},{24,28},{28,24},{32,36},... | collective-permute-start | bytes 294920 | tf_op jit(solution)/shard_map/ppermute | solution.py:406
  29.6 12.4 %all_to_all.46 = f32[32,1,1024]{2,1,0:T(1,128)S(1)} all-to-all(f32[32,1,1024]{2,1,0:T(1,128)S(1)} %bitcast.35), channel_id=1, replica_groups={{0,8,16,24,32,40,48,56,64,72,80,88,96,104,112,120,128,136,144,152,160,1..., dimensions={0} | all-to-all | bytes 262144 | tf_op jit(solution)/shard_map/all_to_all | solution.py:400
  42.0 1.5 shard_map.80.refs_1_
  43.6 3.0 %collective-permute-start.3 = (f32[24,128]{1,0:T(8,128)S(1)}, f32[24,128]{1,0:T(8,128)S(1)}, u32[]{:S(2)}, u32[]{:S(2)}) collective-permute-start(f32[24,128]{1,0:T(8,128)S(1)} %shard_map.80.refs_1_), channel_id=1, source_target_pairs={{0,2},{1,3},{2,0},{3,1},{4,6},{5,7},{6,4},{7,5},{8,10},{9,11},{10,... | collective-permute-start | bytes 36872 | tf_op jit(solution)/shard_map/ppermute | solution.py:454
  49.1 2.0 %collective-permute-done.1.refs_2_ = f32[24,128]{1,0:T(8,128)S(1)} collective-permute-done((f32[24,128]{1,0:T(8,128)S(1)}, f32[24,128]{1,0:T(8,128)S(1)}, u32[]{:S(2)}, u32[]{:S(2)}) %collective-permute-start.1) | collective-permute-done | bytes 12320 | tf_op jit(solution)/shard_map/ppermute | solution.py:454
  51.1 1.8 shard_map.81
  52.9 13.2 %all_to_all.47 = f32[32,1,1152]{2,1,0:T(1,128)S(1)} all-to-all(f32[32,1,1152]{2,1,0:T(1,128)S(1)} %bitcast.30), channel_id=1, replica_groups={{0,8,16,24,32,40,48,56,64,72,80,88,96,104,112,120,128,136,144,152,160,1..., dimensions={0} | all-to-all | bytes 294912 | tf_op jit(solution)/shard_map/all_to_all | solution.py:400
  66.3 4.6 %collective-permute-start.4 = (f32[72,256]{1,0:T(8,128)S(1)}, f32[72,256]{1,0:T(8,128)S(1)}, u32[]{:S(2)}, u32[]{:S(2)}) collective-permute-start(f32[72,256]{1,0:T(8,128)S(1)} %shard_map.82.refs_0_), channel_id=1, source_target_pairs={{0,4},{4,0},{8,12},{12,8},{16,20},{20,16},{24,28},{28,24},{32,36},... | collective-permute-start | bytes 221192 | tf_op jit(solution)/shard_map/ppermute | solution.py:406
  72.1 12.4 %all_to_all.48 = f32[32,1,1024]{2,1,0:T(1,128)S(1)} all-to-all(f32[32,1,1024]{2,1,0:T(1,128)S(1)} %bitcast.34), channel_id=1, replica_groups={{0,8,16,24,32,40,48,56,64,72,80,88,96,104,112,120,128,136,144,152,160,1..., dimensions={0} | all-to-all | bytes 262144 | tf_op jit(solution)/shard_map/all_to_all | solution.py:400
  84.5 1.5 shard_map.84.refs_1_
  86.4 1.7 collective-permute-start.6
  88.1 2.1 %collective-permute-done.7.refs_4_ = f32[24,128]{1,0:T(8,128)S(1)} collective-permute-done((f32[24,128]{1,0:T(8,128)S(1)}, f32[24,128]{1,0:T(8,128)S(1)}, u32[]{:S(2)}, u32[]{:S(2)}) %collective-permute-start.7) | collective-permute-done | bytes 12320 | tf_op jit(solution)/shard_map/ppermute | solution.py:454
  90.2 1.7 collective-permute-done.5.refs_2_
  91.9 1.9 shard_map.85
  93.7 13.5 %all_to_all.49 = f32[32,1,1152]{2,1,0:T(1,128)S(1)} all-to-all(f32[32,1,1152]{2,1,0:T(1,128)S(1)} %bitcast.29), channel_id=1, replica_groups={{0,8,16,24,32,40,48,56,64,72,80,88,96,104,112,120,128,136,144,152,160,1..., dimensions={0} | all-to-all | bytes 294912 | tf_op jit(solution)/shard_map/all_to_all | solution.py:400
  107.3 4.4 %collective-permute-start.8 = (f32[72,256]{1,0:T(8,128)S(1)}, f32[72,256]{1,0:T(8,128)S(1)}, u32[]{:S(2)}, u32[]{:S(2)}) collective-permute-start(f32[72,256]{1,0:T(8,128)S(1)} %shard_map.86.refs_0_), channel_id=1, source_target_pairs={{0,4},{4,0},{8,12},{12,8},{16,20},{20,16},{24,28},{28,24},{32,36},... | collective-permute-start | bytes 221192 | tf_op jit(solution)/shard_map/ppermute | solution.py:406
  113.0 12.4 %all_to_all.50 = f32[32,1,1024]{2,1,0:T(1,128)S(1)} all-to-all(f32[32,1,1024]{2,1,0:T(1,128)S(1)} %bitcast.32), channel_id=1, replica_groups={{0,8,16,24,32,40,48,56,64,72,80,88,96,104,112,120,128,136,144,152,160,1..., dimensions={0} | all-to-all | bytes 262144 | tf_op jit(solution)/shard_map/all_to_all | solution.py:400
  125.3 1.5 shard_map.88.refs_1_
  128.5 2.5 %collective-permute-done.11.refs_4_ = f32[24,128]{1,0:T(8,128)S(1)} collective-permute-done((f32[24,128]{1,0:T(8,128)S(1)}, f32[24,128]{1,0:T(8,128)S(1)}, u32[]{:S(2)}, u32[]{:S(2)}) %collective-permute-start.11) | collective-permute-done | bytes 12320 | tf_op jit(solution)/shard_map/ppermute | solution.py:454
  131.7 1.9 shard_map.89
  133.5 13.1 %all_to_all.51 = f32[32,1,1152]{2,1,0:T(1,128)S(1)} all-to-all(f32[32,1,1152]{2,1,0:T(1,128)S(1)} %bitcast.28), channel_id=1, replica_groups={{0,8,16,24,32,40,48,56,64,72,80,88,96,104,112,120,128,136,144,152,160,1..., dimensions={0} | all-to-all | bytes 294912 | tf_op jit(solution)/shard_map/all_to_all | solution.py:400
  146.8 4.6 %collective-permute-start.12 = (f32[72,256]{1,0:T(8,128)S(1)}, f32[72,256]{1,0:T(8,128)S(1)}, u32[]{:S(2)}, u32[]{:S(2)}) collective-permute-start(f32[72,256]{1,0:T(8,128)S(1)} %shard_map.90.refs_0_), channel_id=1, source_target_pairs={{0,4},{4,0},{8,12},{12,8},{16,20},{20,16},{24,28},{28,24},{32,36},... | collective-permute-start | bytes 221192 | tf_op jit(solution)/shard_map/ppermute | solution.py:406
  152.6 12.3 %all_to_all.52 = f32[32,1,1024]{2,1,0:T(1,128)S(1)} all-to-all(f32[32,1,1024]{2,1,0:T(1,128)S(1)} %bitcast.33), channel_id=1, replica_groups={{0,8,16,24,32,40,48,56,64,72,80,88,96,104,112,120,128,136,144,152,160,1..., dimensions={0} | all-to-all | bytes 262144 | tf_op jit(solution)/shard_map/all_to_all | solution.py:400
  164.9 1.5 shard_map.92.refs_1_
  167.1 1.1 collective-permute-start.14
  168.6 2.0 %collective-permute-done.15.refs_4_ = f32[24,128]{1,0:T(8,128)S(1)} collective-permute-done((f32[24,128]{1,0:T(8,128)S(1)}, f32[24,128]{1,0:T(8,128)S(1)}, u32[]{:S(2)}, u32[]{:S(2)}) %collective-permute-start.15) | collective-permute-done | bytes 12320 | tf_op jit(solution)/shard_map/ppermute | solution.py:454
  170.6 1.4 collective-permute-done.13.refs_2_
  172.0 1.9 shard_map.93
  173.8 13.5 %all_to_all.53 = f32[32,1,1152]{2,1,0:T(1,128)S(1)} all-to-all(f32[32,1,1152]{2,1,0:T(1,128)S(1)} %bitcast.23), channel_id=1, replica_groups={{0,8,16,24,32,40,48,56,64,72,80,88,96,104,112,120,128,136,144,152,160,1..., dimensions={0} | all-to-all | bytes 294912 | tf_op jit(solution)/shard_map/all_to_all | solution.py:400
  187.5 4.2 %collective-permute-start.16 = (f32[72,256]{1,0:T(8,128)S(1)}, f32[72,256]{1,0:T(8,128)S(1)}, u32[]{:S(2)}, u32[]{:S(2)}) collective-permute-start(f32[72,256]{1,0:T(8,128)S(1)} %shard_map.94.refs_0_), channel_id=1, source_target_pairs={{0,4},{4,0},{8,12},{12,8},{16,20},{20,16},{24,28},{28,24},{32,36},... | collective-permute-start | bytes 221192 | tf_op jit(solution)/shard_map/ppermute | solution.py:406
  (30 shorter events, 13.5 us)
Async XLA Ops:
  26.2 3.3 %collective-permute-start = (f32[96,256]{1,0:T(8,128)S(1)}, f32[96,256]{1,0:T(8,128)S(1)}, u32[]{:S(2)}, u32[]{:S(2)}) collective-permute-start(f32[96,256]{1,0:T(8,128)S(1)} %get-tuple-element.46.mine_ref), channel_id=1, source_target_pairs={{0,4},{4,0},{8,12},{12,8},{16,20},{20,16},{24,28},{28,24},{32,36},... | collective-permute-start | bytes 294920 | tf_op jit(solution)/shard_map/ppermute | solution.py:406
  43.6 4.5 %collective-permute-start.3 = (f32[24,128]{1,0:T(8,128)S(1)}, f32[24,128]{1,0:T(8,128)S(1)}, u32[]{:S(2)}, u32[]{:S(2)}) collective-permute-start(f32[24,128]{1,0:T(8,128)S(1)} %shard_map.80.refs_1_), channel_id=1, source_target_pairs={{0,2},{1,3},{2,0},{3,1},{4,6},{5,7},{6,4},{7,5},{8,10},{9,11},{10,... | collective-permute-start | bytes 36872 | tf_op jit(solution)/shard_map/ppermute | solution.py:454
  46.6 2.5 %collective-permute-start.2 = (f32[24,128]{1,0:T(8,128)S(1)}, f32[24,128]{1,0:T(8,128)S(1)}, u32[]{:S(2)}, u32[]{:S(2)}) collective-permute-start(f32[24,128]{1,0:T(8,128)S(1)} %shard_map.80.refs_1_), channel_id=1, source_target_pairs={{0,3},{1,0},{2,1},{3,2},{4,7},{5,4},{6,5},{7,6},{8,11},{9,8},{10,9... | collective-permute-start | bytes 36872 | tf_op jit(solution)/shard_map/ppermute | solution.py:454
  47.3 3.8 %collective-permute-start.1 = (f32[24,128]{1,0:T(8,128)S(1)}, f32[24,128]{1,0:T(8,128)S(1)}, u32[]{:S(2)}, u32[]{:S(2)}) collective-permute-start(f32[24,128]{1,0:T(8,128)S(1)} %shard_map.80.refs_1_), channel_id=1, source_target_pairs={{0,1},{1,2},{2,3},{3,0},{4,5},{5,6},{6,7},{7,4},{8,9},{9,10},{10,1... | collective-permute-start | bytes 36872 | tf_op jit(solution)/shard_map/ppermute | solution.py:454
  66.3 5.6 %collective-permute-start.4 = (f32[72,256]{1,0:T(8,128)S(1)}, f32[72,256]{1,0:T(8,128)S(1)}, u32[]{:S(2)}, u32[]{:S(2)}) collective-permute-start(f32[72,256]{1,0:T(8,128)S(1)} %shard_map.82.refs_0_), channel_id=1, source_target_pairs={{0,4},{4,0},{8,12},{12,8},{16,20},{20,16},{24,28},{28,24},{32,36},... | collective-permute-start | bytes 221192 | tf_op jit(solution)/shard_map/ppermute | solution.py:406
  86.0 4.1 %collective-permute-start.7 = (f32[24,128]{1,0:T(8,128)S(1)}, f32[24,128]{1,0:T(8,128)S(1)}, u32[]{:S(2)}, u32[]{:S(2)}) collective-permute-start(f32[24,128]{1,0:T(8,128)S(1)} %shard_map.84.refs_1_), channel_id=1, source_target_pairs={{0,2},{1,3},{2,0},{3,1},{4,6},{5,7},{6,4},{7,5},{8,10},{9,11},{10,... | collective-permute-start | bytes 36872 | tf_op jit(solution)/shard_map/ppermute | solution.py:454
  86.4 3.7 %collective-permute-start.6 = (f32[24,128]{1,0:T(8,128)S(1)}, f32[24,128]{1,0:T(8,128)S(1)}, u32[]{:S(2)}, u32[]{:S(2)}) collective-permute-start(f32[24,128]{1,0:T(8,128)S(1)} %shard_map.84.refs_1_), channel_id=1, source_target_pairs={{0,3},{1,0},{2,1},{3,2},{4,7},{5,4},{6,5},{7,6},{8,11},{9,8},{10,9... | collective-permute-start | bytes 36872 | tf_op jit(solution)/shard_map/ppermute | solution.py:454
  88.1 3.8 %collective-permute-start.5 = (f32[24,128]{1,0:T(8,128)S(1)}, f32[24,128]{1,0:T(8,128)S(1)}, u32[]{:S(2)}, u32[]{:S(2)}) collective-permute-start(f32[24,128]{1,0:T(8,128)S(1)} %shard_map.84.refs_1_), channel_id=1, source_target_pairs={{0,1},{1,2},{2,3},{3,0},{4,5},{5,6},{6,7},{7,4},{8,9},{9,10},{10,1... | collective-permute-start | bytes 36872 | tf_op jit(solution)/shard_map/ppermute | solution.py:454
  107.3 5.3 %collective-permute-start.8 = (f32[72,256]{1,0:T(8,128)S(1)}, f32[72,256]{1,0:T(8,128)S(1)}, u32[]{:S(2)}, u32[]{:S(2)}) collective-permute-start(f32[72,256]{1,0:T(8,128)S(1)} %shard_map.86.refs_0_), channel_id=1, source_target_pairs={{0,4},{4,0},{8,12},{12,8},{16,20},{20,16},{24,28},{28,24},{32,36},... | collective-permute-start | bytes 221192 | tf_op jit(solution)/shard_map/ppermute | solution.py:406
  126.8 4.1 %collective-permute-start.11 = (f32[24,128]{1,0:T(8,128)S(1)}, f32[24,128]{1,0:T(8,128)S(1)}, u32[]{:S(2)}, u32[]{:S(2)}) collective-permute-start(f32[24,128]{1,0:T(8,128)S(1)} %shard_map.88.refs_1_), channel_id=1, source_target_pairs={{0,2},{1,3},{2,0},{3,1},{4,6},{5,7},{6,4},{7,5},{8,10},{9,11},{10,... | collective-permute-start | bytes 36872 | tf_op jit(solution)/shard_map/ppermute | solution.py:454
  126.9 4.0 %collective-permute-start.10 = (f32[24,128]{1,0:T(8,128)S(1)}, f32[24,128]{1,0:T(8,128)S(1)}, u32[]{:S(2)}, u32[]{:S(2)}) collective-permute-start(f32[24,128]{1,0:T(8,128)S(1)} %shard_map.88.refs_1_), channel_id=1, source_target_pairs={{0,3},{1,0},{2,1},{3,2},{4,7},{5,4},{6,5},{7,6},{8,11},{9,8},{10,9... | collective-permute-start | bytes 36872 | tf_op jit(solution)/shard_map/ppermute | solution.py:454
  127.9 3.8 %collective-permute-start.9 = (f32[24,128]{1,0:T(8,128)S(1)}, f32[24,128]{1,0:T(8,128)S(1)}, u32[]{:S(2)}, u32[]{:S(2)}) collective-permute-start(f32[24,128]{1,0:T(8,128)S(1)} %shard_map.88.refs_1_), channel_id=1, source_target_pairs={{0,1},{1,2},{2,3},{3,0},{4,5},{5,6},{6,7},{7,4},{8,9},{9,10},{10,1... | collective-permute-start | bytes 36872 | tf_op jit(solution)/shard_map/ppermute | solution.py:454
  146.8 5.5 %collective-permute-start.12 = (f32[72,256]{1,0:T(8,128)S(1)}, f32[72,256]{1,0:T(8,128)S(1)}, u32[]{:S(2)}, u32[]{:S(2)}) collective-permute-start(f32[72,256]{1,0:T(8,128)S(1)} %shard_map.90.refs_0_), channel_id=1, source_target_pairs={{0,4},{4,0},{8,12},{12,8},{16,20},{20,16},{24,28},{28,24},{32,36},... | collective-permute-start | bytes 221192 | tf_op jit(solution)/shard_map/ppermute | solution.py:406
  166.5 4.1 %collective-permute-start.15 = (f32[24,128]{1,0:T(8,128)S(1)}, f32[24,128]{1,0:T(8,128)S(1)}, u32[]{:S(2)}, u32[]{:S(2)}) collective-permute-start(f32[24,128]{1,0:T(8,128)S(1)} %shard_map.92.refs_1_), channel_id=1, source_target_pairs={{0,2},{1,3},{2,0},{3,1},{4,6},{5,7},{6,4},{7,5},{8,10},{9,11},{10,... | collective-permute-start | bytes 36872 | tf_op jit(solution)/shard_map/ppermute | solution.py:454
  167.1 3.5 %collective-permute-start.14 = (f32[24,128]{1,0:T(8,128)S(1)}, f32[24,128]{1,0:T(8,128)S(1)}, u32[]{:S(2)}, u32[]{:S(2)}) collective-permute-start(f32[24,128]{1,0:T(8,128)S(1)} %shard_map.92.refs_1_), channel_id=1, source_target_pairs={{0,3},{1,0},{2,1},{3,2},{4,7},{5,4},{6,5},{7,6},{8,11},{9,8},{10,9... | collective-permute-start | bytes 36872 | tf_op jit(solution)/shard_map/ppermute | solution.py:454
  168.2 3.8 %collective-permute-start.13 = (f32[24,128]{1,0:T(8,128)S(1)}, f32[24,128]{1,0:T(8,128)S(1)}, u32[]{:S(2)}, u32[]{:S(2)}) collective-permute-start(f32[24,128]{1,0:T(8,128)S(1)} %shard_map.92.refs_1_), channel_id=1, source_target_pairs={{0,1},{1,2},{2,3},{3,0},{4,5},{5,6},{6,7},{7,4},{8,9},{9,10},{10,1... | collective-permute-start | bytes 36872 | tf_op jit(solution)/shard_map/ppermute | solution.py:454
  187.5 5.1 %collective-permute-start.16 = (f32[72,256]{1,0:T(8,128)S(1)}, f32[72,256]{1,0:T(8,128)S(1)}, u32[]{:S(2)}, u32[]{:S(2)}) collective-permute-start(f32[72,256]{1,0:T(8,128)S(1)} %shard_map.94.refs_0_), channel_id=1, source_target_pairs={{0,4},{4,0},{8,12},{12,8},{16,20},{20,16},{24,28},{28,24},{32,36},... | collective-permute-start | bytes 221192 | tf_op jit(solution)/shard_map/ppermute | solution.py:406

commit v8 on v7

--- a/solution.py
+++ b/solution.py
@@ -83,6 +83,8 @@
     rows, soundings = weights_ref.shape
     peers = out_ref.shape[0] // DELIVER
     chunks = chunk_sems.shape[0]
+    shift = cells.bit_length() - 1
+    assert cells == 1 << shift and rows & (rows - 1) == 0
     size = blocks // chunks
     small = [
         pltpu.make_async_copy(source, target, sems.at[at])
@@ -127,18 +129,19 @@
 
     def product(block):
         cell = cells_ref[block]
-        peer = cell // cells
-        slot = cell % cells
+        peer = lax.shift_right_logical(cell, shift)
+        slot = cell & (cells - 1)
         rank = count_ref[peer]
         count_ref[peer] = rank + 1
-        row = rows_ref[block] % rows
+        row = rows_ref[block] & (rows - 1)
         place = peer * DELIVER + 2 * rank
         meta_ref[block] = place
         meta_ref[blocks + block] = row
         meta_ref[2 * blocks + block] = peer * FETCH + 2 * rank
-        scalars = pl.ds(peer * DELIVER + FETCH, 1)
-        out_ref[scalars, :] = jnp.where(
-            lane_ids((1, LANES)) == rank, (slot + 1).astype(F32), out_ref[scalars, :]
+        pltpu.store(
+            out_ref.at[pl.ds(peer * DELIVER + FETCH, 1), :],
+            jnp.full((1, LANES), (slot + 1).astype(F32)),
+            mask=lane_ids((1, LANES)) == rank,
         )
         transposed_product(arrived_ref, field_ref, out_ref, block, row, place, footprint_ref)
 
@@ -342,6 +345,13 @@
     *refs, field_ref = refs
     out_ref[...] = jnp.zeros_like(out_ref)
     spread(field, field_ref)
+    def product(block):
+        transposed_product(
+            footprint_ref, field_ref, out_ref, block, meta_ref[blocks + block], meta_ref[block]
+        )
+
+    together = 8
+    each(0, blocks - together, together, product)
     sums = [lane_sums(field * forward)]
     if iteration > 0:
         direction = old_ref[...]
@@ -354,13 +364,8 @@
             refs[1][...] = direction
     scalars = jnp.sum(summed[16:24] + in_lanes(sums, 3), axis=0, keepdims=True)
     out_ref[pl.ds(FETCH, peers, stride=DELIVER), :] = jnp.broadcast_to(scalars, (peers, LANES))
-
-    def product(block):
-        transposed_product(
-            footprint_ref, field_ref, out_ref, block, meta_ref[blocks + block], meta_ref[block]
-        )
-
-    each(0, blocks, 8, product)
+    for block in range(blocks - together, blocks):
+        product(block)
 
 
 def call(kernel, out_shape, kinds, out_kinds=None, scratch=()):
@@ -451,7 +456,7 @@
             forward_kernel, [shape((24, LANES), F32)], "svvv", scratch=[field]
         )(meta, exchange(outgoing), sums, footprint)
         others = [
-            lax.ppermute(partial, "rep", [(device, (device + by) % reps) for device in range(reps)])
+            lax.ppermute(partial, "rep", [(device, device ^ by) for device in range(reps)])
             for by in (1, 3, 2)
         ]
         operands = [meta, partial, *others, packed_weights, footprint]

time: 194 us -> 192 us (0.990)
  waiting for transfers between devices: 18 us -> 14.9 us
    ppermute x12, waiting for transfers between devices: 13.4 us -> 10.3 us  [per_device(): lax.ppermute(partial, 'rep', [(device, device ^ by) for device in range(r...]
where the time goes in v8:
time: 192 us
  blocking collectives  124 us (65%)
  starting transfers between devices  32.3 us (17%)
  Pallas kernels  20.2 us (11%)
  waiting for transfers between devices  14.9 us (8%)
    all_to_all x9, blocking collectives, exchange(): lax.all_to_all(flat, 'orb', split_axis=0, concat_axis=0, axis_index_group...  124 us
    ppermute x5, starting transfers between devices, swap(): return lax.ppermute(array, 'orb', swapped)  20.1 us
    ppermute x12, starting transfers between devices, per_device(): lax.ppermute(partial, 'rep', [(device, device ^ by) for device in range(r...  12.2 us
    ppermute x12, waiting for transfers between devices, per_device(): lax.ppermute(partial, 'rep', [(device, device ^ by) for device in range(r...  10.3 us
    pallas_call x4, Pallas kernels, per_device(): call(functools.partial(adjoint_kernel, iteration, last), [delivered] + ([...  7.32 us
    pallas_call x4, Pallas kernels, per_device(): call(forward_kernel, [shape((24, LANES), F32)], 'svvv', scratch=[field])  6.13 us
    ppermute x5, waiting for transfers between devices, swap(): return lax.ppermute(array, 'orb', swapped)  4.59 us
    pallas_call x1, Pallas kernels, per_device(): call(functools.partial(start_kernel, cells), [delivered, pltpu.SMEM((3 *...  4.07 us
  transfers between devices with their start and end apart: 17, of which 13 were waited for; matrix products, arithmetic and copies ran while one was open for 0% of the time, Pallas kernels for 0%

profile of v8, /device:TPU:1, one launch (start us, length us, event | category | flops | bytes accessed | tf_op | source)
XLA Modules:
  0.0 191.8 jit_solution(18228864298491888096)
XLA Ops:
  0.6 4.1 %shard_map.77 = (f32[288,128]{1,0:T(8,128)S(1)}, s32[144]{0:T(256)S(4)}, f32[8,256]{1,0:T(8,128)S(1)}, f32[32,256]{1,0:T(8,128)S(1)}, f32[48,256,256]{2,1,0:T(8,128)S(1)}) custom-call(s32[48]{0:T(128)} %rows_hbm.1, s32[48]{0:T(128)} %cells_hbm.1, f32[8,256]{1,0:T(8,128)} %observed_hbm.1, f32[8,256]{1,0:T(8,128)} %weights_hbm.1, f32[32,256]{1,0:T(8,128)} %prior_hbm.1, ...), custom_call_target="tpu_custom_call" | custom-call | tf_op jit(solution)/shard_map/pallas_call | solution.py:417
  4.7 21.1 %all_to_all.45 = f32[32,1,1152]{2,1,0:T(1,128)S(1)} all-to-all(f32[32,1,1152]{2,1,0:T(1,128)S(1)} %bitcast.31), channel_id=1, replica_groups={{0,8,16,24,32,40,48,56,64,72,80,88,96,104,112,120,128,136,144,152,160,1..., dimensions={0} | all-to-all | bytes 294912 | tf_op jit(solution)/shard_map/all_to_all | solution.py:405
  26.1 2.4 %collective-permute-start = (f32[96,256]{1,0:T(8,128)S(1)}, f32[96,256]{1,0:T(8,128)S(1)}, u32[]{:S(2)}, u32[]{:S(2)}) collective-permute-start(f32[96,256]{1,0:T(8,128)S(1)} %get-tuple-element.46.mine_ref), channel_id=1, source_target_pairs={{0,4},{4,0},{8,12},{12,8},{16,20},{20,16},{24,28},{28,24},{32,36},... | collective-permute-start | bytes 294920 | tf_op jit(solution)/shard_map/ppermute | solution.py:411
  29.6 12.4 %all_to_all.46 = f32[32,1,1024]{2,1,0:T(1,128)S(1)} all-to-all(f32[32,1,1024]{2,1,0:T(1,128)S(1)} %bitcast.35), channel_id=1, replica_groups={{0,8,16,24,32,40,48,56,64,72,80,88,96,104,112,120,128,136,144,152,160,1..., dimensions={0} | all-to-all | bytes 262144 | tf_op jit(solution)/shard_map/all_to_all | solution.py:405
  42.0 1.5 shard_map.80.refs_1_
  43.5 3.0 %collective-permute-start.3 = (f32[24,128]{1,0:T(8,128)S(1)}, f32[24,128]{1,0:T(8,128)S(1)}, u32[]{:S(2)}, u32[]{:S(2)}) collective-permute-start(f32[24,128]{1,0:T(8,128)S(1)} %shard_map.80.refs_1_), channel_id=1, source_target_pairs={{0,2},{1,3},{2,0},{3,1},{4,6},{5,7},{6,4},{7,5},{8,10},{9,11},{10,... | collective-permute-start | bytes 36872 | tf_op jit(solution)/shard_map/ppermute | solution.py:459
  47.7 2.8 %collective-permute-done.2.refs_3_ = f32[24,128]{1,0:T(8,128)S(1)} collective-permute-done((f32[24,128]{1,0:T(8,128)S(1)}, f32[24,128]{1,0:T(8,128)S(1)}, u32[]{:S(2)}, u32[]{:S(2)}) %collective-permute-start.2) | collective-permute-done | bytes 12320 | tf_op jit(solution)/shard_map/ppermute | solution.py:459
  50.5 1.8 shard_map.81
  52.4 13.0 %all_to_all.47 = f32[32,1,1152]{2,1,0:T(1,128)S(1)} all-to-all(f32[32,1,1152]{2,1,0:T(1,128)S(1)} %bitcast.30), channel_id=1, replica_groups={{0,8,16,24,32,40,48,56,64,72,80,88,96,104,112,120,128,136,144,152,160,1..., dimensions={0} | all-to-all | bytes 294912 | tf_op jit(solution)/shard_map/all_to_all | solution.py:405
  65.6 4.4 %collective-permute-start.4 = (f32[72,256]{1,0:T(8,128)S(1)}, f32[72,256]{1,0:T(8,128)S(1)}, u32[]{:S(2)}, u32[]{:S(2)}) collective-permute-start(f32[72,256]{1,0:T(8,128)S(1)} %shard_map.82.refs_0_), channel_id=1, source_target_pairs={{0,4},{4,0},{8,12},{12,8},{16,20},{20,16},{24,28},{28,24},{32,36},... | collective-permute-start | bytes 221192 | tf_op jit(solution)/shard_map/ppermute | solution.py:411
  71.2 12.4 %all_to_all.48 = f32[32,1,1024]{2,1,0:T(1,128)S(1)} all-to-all(f32[32,1,1024]{2,1,0:T(1,128)S(1)} %bitcast.34), channel_id=1, replica_groups={{0,8,16,24,32,40,48,56,64,72,80,88,96,104,112,120,128,136,144,152,160,1..., dimensions={0} | all-to-all | bytes 262144 | tf_op jit(solution)/shard_map/all_to_all | solution.py:405
  83.5 1.5 shard_map.84.refs_1_
  85.1 1.2 collective-permute-start.7
  87.8 1.4 collective-permute-done.7.refs_4_
  90.0 1.8 shard_map.85
  91.9 13.3 %all_to_all.49 = f32[32,1,1152]{2,1,0:T(1,128)S(1)} all-to-all(f32[32,1,1152]{2,1,0:T(1,128)S(1)} %bitcast.29), channel_id=1, replica_groups={{0,8,16,24,32,40,48,56,64,72,80,88,96,104,112,120,128,136,144,152,160,1..., dimensions={0} | all-to-all | bytes 294912 | tf_op jit(solution)/shard_map/all_to_all | solution.py:405
  105.3 4.6 %collective-permute-start.8 = (f32[72,256]{1,0:T(8,128)S(1)}, f32[72,256]{1,0:T(8,128)S(1)}, u32[]{:S(2)}, u32[]{:S(2)}) collective-permute-start(f32[72,256]{1,0:T(8,128)S(1)} %shard_map.86.refs_0_), channel_id=1, source_target_pairs={{0,4},{4,0},{8,12},{12,8},{16,20},{20,16},{24,28},{28,24},{32,36},... | collective-permute-start | bytes 221192 | tf_op jit(solution)/shard_map/ppermute | solution.py:411
  111.1 12.4 %all_to_all.50 = f32[32,1,1024]{2,1,0:T(1,128)S(1)} all-to-all(f32[32,1,1024]{2,1,0:T(1,128)S(1)} %bitcast.32), channel_id=1, replica_groups={{0,8,16,24,32,40,48,56,64,72,80,88,96,104,112,120,128,136,144,152,160,1..., dimensions={0} | all-to-all | bytes 262144 | tf_op jit(solution)/shard_map/all_to_all | solution.py:405
  123.5 1.5 shard_map.88.refs_1_
  125.0 1.9 collective-permute-start.11
  128.0 1.2 collective-permute-done.11.refs_4_
  129.1 1.5 collective-permute-done.10.refs_3_
  130.6 1.8 shard_map.89
  132.5 13.5 %all_to_all.51 = f32[32,1,1152]{2,1,0:T(1,128)S(1)} all-to-all(f32[32,1,1152]{2,1,0:T(1,128)S(1)} %bitcast.28), channel_id=1, replica_groups={{0,8,16,24,32,40,48,56,64,72,80,88,96,104,112,120,128,136,144,152,160,1..., dimensions={0} | all-to-all | bytes 294912 | tf_op jit(solution)/shard_map/all_to_all | solution.py:405
  146.1 4.3 %collective-permute-start.12 = (f32[72,256]{1,0:T(8,128)S(1)}, f32[72,256]{1,0:T(8,128)S(1)}, u32[]{:S(2)}, u32[]{:S(2)}) collective-permute-start(f32[72,256]{1,0:T(8,128)S(1)} %shard_map.90.refs_0_), channel_id=1, source_target_pairs={{0,4},{4,0},{8,12},{12,8},{16,20},{20,16},{24,28},{28,24},{32,36},... | collective-permute-start | bytes 221192 | tf_op jit(solution)/shard_map/ppermute | solution.py:411
  151.6 12.4 %all_to_all.52 = f32[32,1,1024]{2,1,0:T(1,128)S(1)} all-to-all(f32[32,1,1024]{2,1,0:T(1,128)S(1)} %bitcast.33), channel_id=1, replica_groups={{0,8,16,24,32,40,48,56,64,72,80,88,96,104,112,120,128,136,144,152,160,1..., dimensions={0} | all-to-all | bytes 262144 | tf_op jit(solution)/shard_map/all_to_all | solution.py:405
  164.0 1.5 shard_map.92.refs_1_
  165.5 1.2 collective-permute-start.15
  168.2 1.4 collective-permute-done.15.refs_4_
  170.4 1.8 shard_map.93
  172.3 13.3 %all_to_all.53 = f32[32,1,1152]{2,1,0:T(1,128)S(1)} all-to-all(f32[32,1,1152]{2,1,0:T(1,128)S(1)} %bitcast.23), channel_id=1, replica_groups={{0,8,16,24,32,40,48,56,64,72,80,88,96,104,112,120,128,136,144,152,160,1..., dimensions={0} | all-to-all | bytes 294912 | tf_op jit(solution)/shard_map/all_to_all | solution.py:405
  185.7 4.4 %collective-permute-start.16 = (f32[72,256]{1,0:T(8,128)S(1)}, f32[72,256]{1,0:T(8,128)S(1)}, u32[]{:S(2)}, u32[]{:S(2)}) collective-permute-start(f32[72,256]{1,0:T(8,128)S(1)} %shard_map.94.refs_0_), channel_id=1, source_target_pairs={{0,4},{4,0},{8,12},{12,8},{16,20},{20,16},{24,28},{28,24},{32,36},... | collective-permute-start | bytes 221192 | tf_op jit(solution)/shard_map/ppermute | solution.py:411
  (30 shorter events, 14.2 us)
Async XLA Ops:
  26.1 3.3 %collective-permute-start = (f32[96,256]{1,0:T(8,128)S(1)}, f32[96,256]{1,0:T(8,128)S(1)}, u32[]{:S(2)}, u32[]{:S(2)}) collective-permute-start(f32[96,256]{1,0:T(8,128)S(1)} %get-tuple-element.46.mine_ref), channel_id=1, source_target_pairs={{0,4},{4,0},{8,12},{12,8},{16,20},{20,16},{24,28},{28,24},{32,36},... | collective-permute-start | bytes 294920 | tf_op jit(solution)/shard_map/ppermute | solution.py:411
  43.5 4.1 %collective-permute-start.3 = (f32[24,128]{1,0:T(8,128)S(1)}, f32[24,128]{1,0:T(8,128)S(1)}, u32[]{:S(2)}, u32[]{:S(2)}) collective-permute-start(f32[24,128]{1,0:T(8,128)S(1)} %shard_map.80.refs_1_), channel_id=1, source_target_pairs={{0,2},{1,3},{2,0},{3,1},{4,6},{5,7},{6,4},{7,5},{8,10},{9,11},{10,... | collective-permute-start | bytes 36872 | tf_op jit(solution)/shard_map/ppermute | solution.py:459
  46.5 4.0 %collective-permute-start.2 = (f32[24,128]{1,0:T(8,128)S(1)}, f32[24,128]{1,0:T(8,128)S(1)}, u32[]{:S(2)}, u32[]{:S(2)}) collective-permute-start(f32[24,128]{1,0:T(8,128)S(1)} %shard_map.80.refs_1_), channel_id=1, source_target_pairs={{0,3},{1,2},{2,1},{3,0},{4,7},{5,6},{6,5},{7,4},{8,11},{9,10},{10,... | collective-permute-start | bytes 36872 | tf_op jit(solution)/shard_map/ppermute | solution.py:459
  47.3 3.2 %collective-permute-start.1 = (f32[24,128]{1,0:T(8,128)S(1)}, f32[24,128]{1,0:T(8,128)S(1)}, u32[]{:S(2)}, u32[]{:S(2)}) collective-permute-start(f32[24,128]{1,0:T(8,128)S(1)} %shard_map.80.refs_1_), channel_id=1, source_target_pairs={{0,1},{1,0},{2,3},{3,2},{4,5},{5,4},{6,7},{7,6},{8,9},{9,8},{10,11... | collective-permute-start | bytes 36872 | tf_op jit(solution)/shard_map/ppermute | solution.py:459
  65.6 5.3 %collective-permute-start.4 = (f32[72,256]{1,0:T(8,128)S(1)}, f32[72,256]{1,0:T(8,128)S(1)}, u32[]{:S(2)}, u32[]{:S(2)}) collective-permute-start(f32[72,256]{1,0:T(8,128)S(1)} %shard_map.82.refs_0_), channel_id=1, source_target_pairs={{0,4},{4,0},{8,12},{12,8},{16,20},{20,16},{24,28},{28,24},{32,36},... | collective-permute-start | bytes 221192 | tf_op jit(solution)/shard_map/ppermute | solution.py:411
  85.1 4.1 %collective-permute-start.7 = (f32[24,128]{1,0:T(8,128)S(1)}, f32[24,128]{1,0:T(8,128)S(1)}, u32[]{:S(2)}, u32[]{:S(2)}) collective-permute-start(f32[24,128]{1,0:T(8,128)S(1)} %shard_map.84.refs_1_), channel_id=1, source_target_pairs={{0,2},{1,3},{2,0},{3,1},{4,6},{5,7},{6,4},{7,5},{8,10},{9,11},{10,... | collective-permute-start | bytes 36872 | tf_op jit(solution)/shard_map/ppermute | solution.py:459
  86.3 3.8 %collective-permute-start.6 = (f32[24,128]{1,0:T(8,128)S(1)}, f32[24,128]{1,0:T(8,128)S(1)}, u32[]{:S(2)}, u32[]{:S(2)}) collective-permute-start(f32[24,128]{1,0:T(8,128)S(1)} %shard_map.84.refs_1_), channel_id=1, source_target_pairs={{0,3},{1,2},{2,1},{3,0},{4,7},{5,6},{6,5},{7,4},{8,11},{9,10},{10,... | collective-permute-start | bytes 36872 | tf_op jit(solution)/shard_map/ppermute | solution.py:459
  87.1 2.9 %collective-permute-start.5 = (f32[24,128]{1,0:T(8,128)S(1)}, f32[24,128]{1,0:T(8,128)S(1)}, u32[]{:S(2)}, u32[]{:S(2)}) collective-permute-start(f32[24,128]{1,0:T(8,128)S(1)} %shard_map.84.refs_1_), channel_id=1, source_target_pairs={{0,1},{1,0},{2,3},{3,2},{4,5},{5,4},{6,7},{7,6},{8,9},{9,8},{10,11... | collective-permute-start | bytes 36872 | tf_op jit(solution)/shard_map/ppermute | solution.py:459
  105.3 5.5 %collective-permute-start.8 = (f32[72,256]{1,0:T(8,128)S(1)}, f32[72,256]{1,0:T(8,128)S(1)}, u32[]{:S(2)}, u32[]{:S(2)}) collective-permute-start(f32[72,256]{1,0:T(8,128)S(1)} %shard_map.86.refs_0_), channel_id=1, source_target_pairs={{0,4},{4,0},{8,12},{12,8},{16,20},{20,16},{24,28},{28,24},{32,36},... | collective-permute-start | bytes 221192 | tf_op jit(solution)/shard_map/ppermute | solution.py:411
  125.0 4.1 %collective-permute-start.11 = (f32[24,128]{1,0:T(8,128)S(1)}, f32[24,128]{1,0:T(8,128)S(1)}, u32[]{:S(2)}, u32[]{:S(2)}) collective-permute-start(f32[24,128]{1,0:T(8,128)S(1)} %shard_map.88.refs_1_), channel_id=1, source_target_pairs={{0,2},{1,3},{2,0},{3,1},{4,6},{5,7},{6,4},{7,5},{8,10},{9,11},{10,... | collective-permute-start | bytes 36872 | tf_op jit(solution)/shard_map/ppermute | solution.py:459
  126.9 3.8 %collective-permute-start.10 = (f32[24,128]{1,0:T(8,128)S(1)}, f32[24,128]{1,0:T(8,128)S(1)}, u32[]{:S(2)}, u32[]{:S(2)}) collective-permute-start(f32[24,128]{1,0:T(8,128)S(1)} %shard_map.88.refs_1_), channel_id=1, source_target_pairs={{0,3},{1,2},{2,1},{3,0},{4,7},{5,6},{6,5},{7,4},{8,11},{9,10},{10,... | collective-permute-start | bytes 36872 | tf_op jit(solution)/shard_map/ppermute | solution.py:459
  128.0 2.7 %collective-permute-start.9 = (f32[24,128]{1,0:T(8,128)S(1)}, f32[24,128]{1,0:T(8,128)S(1)}, u32[]{:S(2)}, u32[]{:S(2)}) collective-permute-start(f32[24,128]{1,0:T(8,128)S(1)} %shard_map.88.refs_1_), channel_id=1, source_target_pairs={{0,1},{1,0},{2,3},{3,2},{4,5},{5,4},{6,7},{7,6},{8,9},{9,8},{10,11... | collective-permute-start | bytes 36872 | tf_op jit(solution)/shard_map/ppermute | solution.py:459
  146.1 5.2 %collective-permute-start.12 = (f32[72,256]{1,0:T(8,128)S(1)}, f32[72,256]{1,0:T(8,128)S(1)}, u32[]{:S(2)}, u32[]{:S(2)}) collective-permute-start(f32[72,256]{1,0:T(8,128)S(1)} %shard_map.90.refs_0_), channel_id=1, source_target_pairs={{0,4},{4,0},{8,12},{12,8},{16,20},{20,16},{24,28},{28,24},{32,36},... | collective-permute-start | bytes 221192 | tf_op jit(solution)/shard_map/ppermute | solution.py:411
  165.5 4.1 %collective-permute-start.15 = (f32[24,128]{1,0:T(8,128)S(1)}, f32[24,128]{1,0:T(8,128)S(1)}, u32[]{:S(2)}, u32[]{:S(2)}) collective-permute-start(f32[24,128]{1,0:T(8,128)S(1)} %shard_map.92.refs_1_), channel_id=1, source_target_pairs={{0,2},{1,3},{2,0},{3,1},{4,6},{5,7},{6,4},{7,5},{8,10},{9,11},{10,... | collective-permute-start | bytes 36872 | tf_op jit(solution)/shard_map/ppermute | solution.py:459
  166.7 3.8 %collective-permute-start.14 = (f32[24,128]{1,0:T(8,128)S(1)}, f32[24,128]{1,0:T(8,128)S(1)}, u32[]{:S(2)}, u32[]{:S(2)}) collective-permute-start(f32[24,128]{1,0:T(8,128)S(1)} %shard_map.92.refs_1_), channel_id=1, source_target_pairs={{0,3},{1,2},{2,1},{3,0},{4,7},{5,6},{6,5},{7,4},{8,11},{9,10},{10,... | collective-permute-start | bytes 36872 | tf_op jit(solution)/shard_map/ppermute | solution.py:459
  167.7 2.7 %collective-permute-start.13 = (f32[24,128]{1,0:T(8,128)S(1)}, f32[24,128]{1,0:T(8,128)S(1)}, u32[]{:S(2)}, u32[]{:S(2)}) collective-permute-start(f32[24,128]{1,0:T(8,128)S(1)} %shard_map.92.refs_1_), channel_id=1, source_target_pairs={{0,1},{1,0},{2,3},{3,2},{4,5},{5,4},{6,7},{7,6},{8,9},{9,8},{10,11... | collective-permute-start | bytes 36872 | tf_op jit(solution)/shard_map/ppermute | solution.py:459
  185.7 5.3 %collective-permute-start.16 = (f32[72,256]{1,0:T(8,128)S(1)}, f32[72,256]{1,0:T(8,128)S(1)}, u32[]{:S(2)}, u32[]{:S(2)}) collective-permute-start(f32[72,256]{1,0:T(8,128)S(1)} %shard_map.94.refs_0_), channel_id=1, source_target_pairs={{0,4},{4,0},{8,12},{12,8},{16,20},{20,16},{24,28},{28,24},{32,36},... | collective-permute-start | bytes 221192 | tf_op jit(solution)/shard_map/ppermute | solution.py:411

commit v9 on v8

--- a/solution.py
+++ b/solution.py
@@ -33,12 +33,21 @@
 
 def spread(packed, field_ref):
     rows, soundings, _ = field_ref.shape
+    columns = []
     for group in range(soundings // 8):
-        for row in range(rows):
-            lane = rows * group + row
-            field_ref[row, 8 * group : 8 * group + 8, :] = jnp.broadcast_to(
-                packed[:, lane : lane + 1], (8, LANES)
-            )
+        start = rows * group // LANES * LANES
+        shift = rows * group % LANES
+        half = packed[:, start : start + LANES]
+        columns.append(pltpu.roll(half, LANES - shift, 1) if shift else half)
+    high, middle, _ = three_parts(jnp.concatenate(columns, axis=0))
+    parts = jnp.concatenate([high, middle], axis=1)
+    source = lax.broadcasted_iota(jnp.int32, (2 * LANES, 2 * LANES), 0) % LANES
+    target = lane_ids((2 * LANES, 2 * LANES)) // LANES
+    for row in range(0, rows, 2):
+        pick = jnp.where(source == row + target, 1.0, 0.0).astype(BF16)
+        pair = jnp.dot(parts, pick, preferred_element_type=F32)
+        field_ref[row] = pair[:, :LANES]
+        field_ref[row + 1] = pair[:, LANES:]
 
 
 def transposed_product(footprint_ref, field_ref, out_ref, block, row, place, keep_ref=None):
@@ -314,7 +323,7 @@
             part = footprint_ref[block, start : start + 2 * SUB, :]
             sums_ref[row, start : start + 2 * SUB, :] += part[:, :LANES] * left + part[:, LANES:] * right
 
-    each(0, blocks, 4, product)
+    each(0, blocks, 8, product)
     lanes = lane_ids((8, LANES))
     per_half = LANES // rows
     halves = []

time: 192 us -> 191 us (level)
  no operation moved by 1% of the time
where the time goes in v9:
time: 191 us
  blocking collectives  124 us (65%)
  starting transfers between devices  32.1 us (17%)
  Pallas kernels  19.3 us (10%)
  waiting for transfers between devices  14.9 us (8%)
    all_to_all x9, blocking collectives, exchange(): lax.all_to_all(flat, 'orb', split_axis=0, concat_axis=0, axis_index_group...  124 us
    ppermute x5, starting transfers between devices, swap(): return lax.ppermute(array, 'orb', swapped)  19.9 us
    ppermute x12, starting transfers between devices, per_device(): lax.ppermute(partial, 'rep', [(device, device ^ by) for device in range(r...  12.2 us
    ppermute x12, waiting for transfers between devices, per_device(): lax.ppermute(partial, 'rep', [(device, device ^ by) for device in range(r...  10.3 us
    pallas_call x4, Pallas kernels, per_device(): call(functools.partial(adjoint_kernel, iteration, last), [delivered] + ([...  6.6 us
    pallas_call x4, Pallas kernels, per_device(): call(forward_kernel, [shape((24, LANES), F32)], 'svvv', scratch=[field])  6 us
    ppermute x5, waiting for transfers between devices, swap(): return lax.ppermute(array, 'orb', swapped)  4.59 us
    pallas_call x1, Pallas kernels, per_device(): call(functools.partial(start_kernel, cells), [delivered, pltpu.SMEM((3 *...  4.07 us
  transfers between devices with their start and end apart: 17, of which 13 were waited for; matrix products, arithmetic and copies ran while one was open for 0% of the time, Pallas kernels for 0%

profile of v9, /device:TPU:1, one launch (start us, length us, event | category | flops | bytes accessed | tf_op | source)
XLA Modules:
  0.0 190.7 jit_solution(2932435368495837814)
XLA Ops:
  0.6 4.1 %shard_map.77 = (f32[288,128]{1,0:T(8,128)S(1)}, s32[144]{0:T(256)S(4)}, f32[8,256]{1,0:T(8,128)S(1)}, f32[32,256]{1,0:T(8,128)S(1)}, f32[48,256,256]{2,1,0:T(8,128)S(1)}) custom-call(s32[48]{0:T(128)} %rows_hbm.1, s32[48]{0:T(128)} %cells_hbm.1, f32[8,256]{1,0:T(8,128)} %observed_hbm.1, f32[8,256]{1,0:T(8,128)} %weights_hbm.1, f32[32,256]{1,0:T(8,128)} %prior_hbm.1, ...), custom_call_target="tpu_custom_call" | custom-call | tf_op jit(solution)/shard_map/pallas_call | solution.py:426
  4.7 21.1 %all_to_all.45 = f32[32,1,1152]{2,1,0:T(1,128)S(1)} all-to-all(f32[32,1,1152]{2,1,0:T(1,128)S(1)} %bitcast.31), channel_id=1, replica_groups={{0,8,16,24,32,40,48,56,64,72,80,88,96,104,112,120,128,136,144,152,160,1..., dimensions={0} | all-to-all | bytes 294912 | tf_op jit(solution)/shard_map/all_to_all | solution.py:414
  26.1 2.4 %collective-permute-start = (f32[96,256]{1,0:T(8,128)S(1)}, f32[96,256]{1,0:T(8,128)S(1)}, u32[]{:S(2)}, u32[]{:S(2)}) collective-permute-start(f32[96,256]{1,0:T(8,128)S(1)} %get-tuple-element.46.mine_ref), channel_id=1, source_target_pairs={{0,4},{4,0},{8,12},{12,8},{16,20},{20,16},{24,28},{28,24},{32,36},... | collective-permute-start | bytes 294920 | tf_op jit(solution)/shard_map/ppermute | solution.py:420
  29.6 12.4 %all_to_all.46 = f32[32,1,1024]{2,1,0:T(1,128)S(1)} all-to-all(f32[32,1,1024]{2,1,0:T(1,128)S(1)} %bitcast.35), channel_id=1, replica_groups={{0,8,16,24,32,40,48,56,64,72,80,88,96,104,112,120,128,136,144,152,160,1..., dimensions={0} | all-to-all | bytes 262144 | tf_op jit(solution)/shard_map/all_to_all | solution.py:414
  42.0 1.5 shard_map.80.refs_1_
  43.5 3.0 %collective-permute-start.3 = (f32[24,128]{1,0:T(8,128)S(1)}, f32[24,128]{1,0:T(8,128)S(1)}, u32[]{:S(2)}, u32[]{:S(2)}) collective-permute-start(f32[24,128]{1,0:T(8,128)S(1)} %shard_map.80.refs_1_), channel_id=1, source_target_pairs={{0,2},{1,3},{2,0},{3,1},{4,6},{5,7},{6,4},{7,5},{8,10},{9,11},{10,... | collective-permute-start | bytes 36872 | tf_op jit(solution)/shard_map/ppermute | solution.py:468
  47.6 2.8 %collective-permute-done.2.refs_3_ = f32[24,128]{1,0:T(8,128)S(1)} collective-permute-done((f32[24,128]{1,0:T(8,128)S(1)}, f32[24,128]{1,0:T(8,128)S(1)}, u32[]{:S(2)}, u32[]{:S(2)}) %collective-permute-start.2) | collective-permute-done | bytes 12320 | tf_op jit(solution)/shard_map/ppermute | solution.py:468
  50.5 1.7 shard_map.81
  52.2 13.0 %all_to_all.47 = f32[32,1,1152]{2,1,0:T(1,128)S(1)} all-to-all(f32[32,1,1152]{2,1,0:T(1,128)S(1)} %bitcast.30), channel_id=1, replica_groups={{0,8,16,24,32,40,48,56,64,72,80,88,96,104,112,120,128,136,144,152,160,1..., dimensions={0} | all-to-all | bytes 294912 | tf_op jit(solution)/shard_map/all_to_all | solution.py:414
  65.4 4.4 %collective-permute-start.4 = (f32[72,256]{1,0:T(8,128)S(1)}, f32[72,256]{1,0:T(8,128)S(1)}, u32[]{:S(2)}, u32[]{:S(2)}) collective-permute-start(f32[72,256]{1,0:T(8,128)S(1)} %shard_map.82.refs_0_), channel_id=1, source_target_pairs={{0,4},{4,0},{8,12},{12,8},{16,20},{20,16},{24,28},{28,24},{32,36},... | collective-permute-start | bytes 221192 | tf_op jit(solution)/shard_map/ppermute | solution.py:420
  71.0 12.4 %all_to_all.48 = f32[32,1,1024]{2,1,0:T(1,128)S(1)} all-to-all(f32[32,1,1024]{2,1,0:T(1,128)S(1)} %bitcast.34), channel_id=1, replica_groups={{0,8,16,24,32,40,48,56,64,72,80,88,96,104,112,120,128,136,144,152,160,1..., dimensions={0} | all-to-all | bytes 262144 | tf_op jit(solution)/shard_map/all_to_all | solution.py:414
  83.3 1.5 shard_map.84.refs_1_
  84.8 1.2 collective-permute-start.7
  87.6 1.4 collective-permute-done.7.refs_4_
  89.8 1.6 shard_map.85
  91.5 13.3 %all_to_all.49 = f32[32,1,1152]{2,1,0:T(1,128)S(1)} all-to-all(f32[32,1,1152]{2,1,0:T(1,128)S(1)} %bitcast.29), channel_id=1, replica_groups={{0,8,16,24,32,40,48,56,64,72,80,88,96,104,112,120,128,136,144,152,160,1..., dimensions={0} | all-to-all | bytes 294912 | tf_op jit(solution)/shard_map/all_to_all | solution.py:414
  104.9 4.6 %collective-permute-start.8 = (f32[72,256]{1,0:T(8,128)S(1)}, f32[72,256]{1,0:T(8,128)S(1)}, u32[]{:S(2)}, u32[]{:S(2)}) collective-permute-start(f32[72,256]{1,0:T(8,128)S(1)} %shard_map.86.refs_0_), channel_id=1, source_target_pairs={{0,4},{4,0},{8,12},{12,8},{16,20},{20,16},{24,28},{28,24},{32,36},... | collective-permute-start | bytes 221192 | tf_op jit(solution)/shard_map/ppermute | solution.py:420
  110.7 12.4 %all_to_all.50 = f32[32,1,1024]{2,1,0:T(1,128)S(1)} all-to-all(f32[32,1,1024]{2,1,0:T(1,128)S(1)} %bitcast.32), channel_id=1, replica_groups={{0,8,16,24,32,40,48,56,64,72,80,88,96,104,112,120,128,136,144,152,160,1..., dimensions={0} | all-to-all | bytes 262144 | tf_op jit(solution)/shard_map/all_to_all | solution.py:414
  123.0 1.5 shard_map.88.refs_1_
  124.5 1.9 collective-permute-start.11
  127.5 1.2 collective-permute-done.11.refs_4_
  128.7 1.5 collective-permute-done.10.refs_3_
  130.2 1.6 shard_map.89
  131.8 13.5 %all_to_all.51 = f32[32,1,1152]{2,1,0:T(1,128)S(1)} all-to-all(f32[32,1,1152]{2,1,0:T(1,128)S(1)} %bitcast.28), channel_id=1, replica_groups={{0,8,16,24,32,40,48,56,64,72,80,88,96,104,112,120,128,136,144,152,160,1..., dimensions={0} | all-to-all | bytes 294912 | tf_op jit(solution)/shard_map/all_to_all | solution.py:414
  145.5 4.3 %collective-permute-start.12 = (f32[72,256]{1,0:T(8,128)S(1)}, f32[72,256]{1,0:T(8,128)S(1)}, u32[]{:S(2)}, u32[]{:S(2)}) collective-permute-start(f32[72,256]{1,0:T(8,128)S(1)} %shard_map.90.refs_0_), channel_id=1, source_target_pairs={{0,4},{4,0},{8,12},{12,8},{16,20},{20,16},{24,28},{28,24},{32,36},... | collective-permute-start | bytes 221192 | tf_op jit(solution)/shard_map/ppermute | solution.py:420
  151.0 12.4 %all_to_all.52 = f32[32,1,1024]{2,1,0:T(1,128)S(1)} all-to-all(f32[32,1,1024]{2,1,0:T(1,128)S(1)} %bitcast.33), channel_id=1, replica_groups={{0,8,16,24,32,40,48,56,64,72,80,88,96,104,112,120,128,136,144,152,160,1..., dimensions={0} | all-to-all | bytes 262144 | tf_op jit(solution)/shard_map/all_to_all | solution.py:414
  163.3 1.5 shard_map.92.refs_1_
  164.8 1.2 collective-permute-start.15
  167.6 1.4 collective-permute-done.15.refs_4_
  169.8 1.6 shard_map.93
  171.4 13.3 %all_to_all.53 = f32[32,1,1152]{2,1,0:T(1,128)S(1)} all-to-all(f32[32,1,1152]{2,1,0:T(1,128)S(1)} %bitcast.23), channel_id=1, replica_groups={{0,8,16,24,32,40,48,56,64,72,80,88,96,104,112,120,128,136,144,152,160,1..., dimensions={0} | all-to-all | bytes 294912 | tf_op jit(solution)/shard_map/all_to_all | solution.py:414
  184.9 4.2 %collective-permute-start.16 = (f32[72,256]{1,0:T(8,128)S(1)}, f32[72,256]{1,0:T(8,128)S(1)}, u32[]{:S(2)}, u32[]{:S(2)}) collective-permute-start(f32[72,256]{1,0:T(8,128)S(1)} %shard_map.94.refs_0_), channel_id=1, source_target_pairs={{0,4},{4,0},{8,12},{12,8},{16,20},{20,16},{24,28},{28,24},{32,36},... | collective-permute-start | bytes 221192 | tf_op jit(solution)/shard_map/ppermute | solution.py:420
  (30 shorter events, 14.2 us)
Async XLA Ops:
  26.1 3.3 %collective-permute-start = (f32[96,256]{1,0:T(8,128)S(1)}, f32[96,256]{1,0:T(8,128)S(1)}, u32[]{:S(2)}, u32[]{:S(2)}) collective-permute-start(f32[96,256]{1,0:T(8,128)S(1)} %get-tuple-element.46.mine_ref), channel_id=1, source_target_pairs={{0,4},{4,0},{8,12},{12,8},{16,20},{20,16},{24,28},{28,24},{32,36},... | collective-permute-start | bytes 294920 | tf_op jit(solution)/shard_map/ppermute | solution.py:420
  43.5 4.1 %collective-permute-start.3 = (f32[24,128]{1,0:T(8,128)S(1)}, f32[24,128]{1,0:T(8,128)S(1)}, u32[]{:S(2)}, u32[]{:S(2)}) collective-permute-start(f32[24,128]{1,0:T(8,128)S(1)} %shard_map.80.refs_1_), channel_id=1, source_target_pairs={{0,2},{1,3},{2,0},{3,1},{4,6},{5,7},{6,4},{7,5},{8,10},{9,11},{10,... | collective-permute-start | bytes 36872 | tf_op jit(solution)/shard_map/ppermute | solution.py:468
  46.5 4.0 %collective-permute-start.2 = (f32[24,128]{1,0:T(8,128)S(1)}, f32[24,128]{1,0:T(8,128)S(1)}, u32[]{:S(2)}, u32[]{:S(2)}) collective-permute-start(f32[24,128]{1,0:T(8,128)S(1)} %shard_map.80.refs_1_), channel_id=1, source_target_pairs={{0,3},{1,2},{2,1},{3,0},{4,7},{5,6},{6,5},{7,4},{8,11},{9,10},{10,... | collective-permute-start | bytes 36872 | tf_op jit(solution)/shard_map/ppermute | solution.py:468
  47.3 3.2 %collective-permute-start.1 = (f32[24,128]{1,0:T(8,128)S(1)}, f32[24,128]{1,0:T(8,128)S(1)}, u32[]{:S(2)}, u32[]{:S(2)}) collective-permute-start(f32[24,128]{1,0:T(8,128)S(1)} %shard_map.80.refs_1_), channel_id=1, source_target_pairs={{0,1},{1,0},{2,3},{3,2},{4,5},{5,4},{6,7},{7,6},{8,9},{9,8},{10,11... | collective-permute-start | bytes 36872 | tf_op jit(solution)/shard_map/ppermute | solution.py:468
  65.4 5.3 %collective-permute-start.4 = (f32[72,256]{1,0:T(8,128)S(1)}, f32[72,256]{1,0:T(8,128)S(1)}, u32[]{:S(2)}, u32[]{:S(2)}) collective-permute-start(f32[72,256]{1,0:T(8,128)S(1)} %shard_map.82.refs_0_), channel_id=1, source_target_pairs={{0,4},{4,0},{8,12},{12,8},{16,20},{20,16},{24,28},{28,24},{32,36},... | collective-permute-start | bytes 221192 | tf_op jit(solution)/shard_map/ppermute | solution.py:420
  84.8 4.1 %collective-permute-start.7 = (f32[24,128]{1,0:T(8,128)S(1)}, f32[24,128]{1,0:T(8,128)S(1)}, u32[]{:S(2)}, u32[]{:S(2)}) collective-permute-start(f32[24,128]{1,0:T(8,128)S(1)} %shard_map.84.refs_1_), channel_id=1, source_target_pairs={{0,2},{1,3},{2,0},{3,1},{4,6},{5,7},{6,4},{7,5},{8,10},{9,11},{10,... | collective-permute-start | bytes 36872 | tf_op jit(solution)/shard_map/ppermute | solution.py:468
  86.0 3.8 %collective-permute-start.6 = (f32[24,128]{1,0:T(8,128)S(1)}, f32[24,128]{1,0:T(8,128)S(1)}, u32[]{:S(2)}, u32[]{:S(2)}) collective-permute-start(f32[24,128]{1,0:T(8,128)S(1)} %shard_map.84.refs_1_), channel_id=1, source_target_pairs={{0,3},{1,2},{2,1},{3,0},{4,7},{5,6},{6,5},{7,4},{8,11},{9,10},{10,... | collective-permute-start | bytes 36872 | tf_op jit(solution)/shard_map/ppermute | solution.py:468
  86.9 2.9 %collective-permute-start.5 = (f32[24,128]{1,0:T(8,128)S(1)}, f32[24,128]{1,0:T(8,128)S(1)}, u32[]{:S(2)}, u32[]{:S(2)}) collective-permute-start(f32[24,128]{1,0:T(8,128)S(1)} %shard_map.84.refs_1_), channel_id=1, source_target_pairs={{0,1},{1,0},{2,3},{3,2},{4,5},{5,4},{6,7},{7,6},{8,9},{9,8},{10,11... | collective-permute-start | bytes 36872 | tf_op jit(solution)/shard_map/ppermute | solution.py:468
  104.9 5.5 %collective-permute-start.8 = (f32[72,256]{1,0:T(8,128)S(1)}, f32[72,256]{1,0:T(8,128)S(1)}, u32[]{:S(2)}, u32[]{:S(2)}) collective-permute-start(f32[72,256]{1,0:T(8,128)S(1)} %shard_map.86.refs_0_), channel_id=1, source_target_pairs={{0,4},{4,0},{8,12},{12,8},{16,20},{20,16},{24,28},{28,24},{32,36},... | collective-permute-start | bytes 221192 | tf_op jit(solution)/shard_map/ppermute | solution.py:420
  124.5 4.1 %collective-permute-start.11 = (f32[24,128]{1,0:T(8,128)S(1)}, f32[24,128]{1,0:T(8,128)S(1)}, u32[]{:S(2)}, u32[]{:S(2)}) collective-permute-start(f32[24,128]{1,0:T(8,128)S(1)} %shard_map.88.refs_1_), channel_id=1, source_target_pairs={{0,2},{1,3},{2,0},{3,1},{4,6},{5,7},{6,4},{7,5},{8,10},{9,11},{10,... | collective-permute-start | bytes 36872 | tf_op jit(solution)/shard_map/ppermute | solution.py:468
  126.4 3.8 %collective-permute-start.10 = (f32[24,128]{1,0:T(8,128)S(1)}, f32[24,128]{1,0:T(8,128)S(1)}, u32[]{:S(2)}, u32[]{:S(2)}) collective-permute-start(f32[24,128]{1,0:T(8,128)S(1)} %shard_map.88.refs_1_), channel_id=1, source_target_pairs={{0,3},{1,2},{2,1},{3,0},{4,7},{5,6},{6,5},{7,4},{8,11},{9,10},{10,... | collective-permute-start | bytes 36872 | tf_op jit(solution)/shard_map/ppermute | solution.py:468
  127.5 2.7 %collective-permute-start.9 = (f32[24,128]{1,0:T(8,128)S(1)}, f32[24,128]{1,0:T(8,128)S(1)}, u32[]{:S(2)}, u32[]{:S(2)}) collective-permute-start(f32[24,128]{1,0:T(8,128)S(1)} %shard_map.88.refs_1_), channel_id=1, source_target_pairs={{0,1},{1,0},{2,3},{3,2},{4,5},{5,4},{6,7},{7,6},{8,9},{9,8},{10,11... | collective-permute-start | bytes 36872 | tf_op jit(solution)/shard_map/ppermute | solution.py:468
  145.5 5.2 %collective-permute-start.12 = (f32[72,256]{1,0:T(8,128)S(1)}, f32[72,256]{1,0:T(8,128)S(1)}, u32[]{:S(2)}, u32[]{:S(2)}) collective-permute-start(f32[72,256]{1,0:T(8,128)S(1)} %shard_map.90.refs_0_), channel_id=1, source_target_pairs={{0,4},{4,0},{8,12},{12,8},{16,20},{20,16},{24,28},{28,24},{32,36},... | collective-permute-start | bytes 221192 | tf_op jit(solution)/shard_map/ppermute | solution.py:420
  164.8 4.1 %collective-permute-start.15 = (f32[24,128]{1,0:T(8,128)S(1)}, f32[24,128]{1,0:T(8,128)S(1)}, u32[]{:S(2)}, u32[]{:S(2)}) collective-permute-start(f32[24,128]{1,0:T(8,128)S(1)} %shard_map.92.refs_1_), channel_id=1, source_target_pairs={{0,2},{1,3},{2,0},{3,1},{4,6},{5,7},{6,4},{7,5},{8,10},{9,11},{10,... | collective-permute-start | bytes 36872 | tf_op jit(solution)/shard_map/ppermute | solution.py:468
  166.0 3.8 %collective-permute-start.14 = (f32[24,128]{1,0:T(8,128)S(1)}, f32[24,128]{1,0:T(8,128)S(1)}, u32[]{:S(2)}, u32[]{:S(2)}) collective-permute-start(f32[24,128]{1,0:T(8,128)S(1)} %shard_map.92.refs_1_), channel_id=1, source_target_pairs={{0,3},{1,2},{2,1},{3,0},{4,7},{5,6},{6,5},{7,4},{8,11},{9,10},{10,... | collective-permute-start | bytes 36872 | tf_op jit(solution)/shard_map/ppermute | solution.py:468
  167.1 2.7 %collective-permute-start.13 = (f32[24,128]{1,0:T(8,128)S(1)}, f32[24,128]{1,0:T(8,128)S(1)}, u32[]{:S(2)}, u32[]{:S(2)}) collective-permute-start(f32[24,128]{1,0:T(8,128)S(1)} %shard_map.92.refs_1_), channel_id=1, source_target_pairs={{0,1},{1,0},{2,3},{3,2},{4,5},{5,4},{6,7},{7,6},{8,9},{9,8},{10,11... | collective-permute-start | bytes 36872 | tf_op jit(solution)/shard_map/ppermute | solution.py:468
  184.9 5.1 %collective-permute-start.16 = (f32[72,256]{1,0:T(8,128)S(1)}, f32[72,256]{1,0:T(8,128)S(1)}, u32[]{:S(2)}, u32[]{:S(2)}) collective-permute-start(f32[72,256]{1,0:T(8,128)S(1)} %shard_map.94.refs_0_), channel_id=1, source_target_pairs={{0,4},{4,0},{8,12},{12,8},{16,20},{20,16},{24,28},{28,24},{32,36},... | collective-permute-start | bytes 221192 | tf_op jit(solution)/shard_map/ppermute | solution.py:420

commit v10 on v9

--- a/solution.py
+++ b/solution.py
@@ -39,7 +39,12 @@
         shift = rows * group % LANES
         half = packed[:, start : start + LANES]
         columns.append(pltpu.roll(half, LANES - shift, 1) if shift else half)
-    high, middle, _ = three_parts(jnp.concatenate(columns, axis=0))
+    spread_columns(jnp.concatenate(columns, axis=0), field_ref)
+
+
+def spread_columns(columns, field_ref):
+    rows = field_ref.shape[0]
+    high, middle, _ = three_parts(columns)
     parts = jnp.concatenate([high, middle], axis=1)
     source = lax.broadcasted_iota(jnp.int32, (2 * LANES, 2 * LANES), 0) % LANES
     target = lane_ids((2 * LANES, 2 * LANES)) // LANES
@@ -123,9 +128,7 @@
     for copy in small[:-1]:
         copy.wait()
     weights = weights_ref[...]
-    columns = in_columns(weights * observed_ref[...])
-    for row in range(rows):
-        field_ref[row] = jnp.broadcast_to(columns[:, row : row + 1], (soundings, LANES))
+    spread_columns(in_columns(weights * observed_ref[...]), field_ref)
     columns = in_columns(weights)
     groups = LANES // rows
     lanes = lane_ids((8, LANES)) // rows

time: 191 us -> 191 us (level)
  no operation moved by 1% of the time
where the time goes in v10:
time: 191 us
  blocking collectives  124 us (65%)
  starting transfers between devices  32.1 us (17%)
  Pallas kernels  19.2 us (10%)
  waiting for transfers between devices  14.9 us (8%)
    all_to_all x9, blocking collectives, exchange(): lax.all_to_all(flat, 'orb', split_axis=0, concat_axis=0, axis_index_group...  124 us
    ppermute x5, starting transfers between devices, swap(): return lax.ppermute(array, 'orb', swapped)  19.9 us
    ppermute x12, starting transfers between devices, per_device(): lax.ppermute(partial, 'rep', [(device, device ^ by) for device in range(r...  12.2 us
    ppermute x12, waiting for transfers between devices, per_device(): lax.ppermute(partial, 'rep', [(device, device ^ by) for device in range(r...  10.3 us
    pallas_call x4, Pallas kernels, per_device(): call(functools.partial(adjoint_kernel, iteration, last), [delivered] + ([...  6.6 us
    pallas_call x4, Pallas kernels, per_device(): call(forward_kernel, [shape((24, LANES), F32)], 'svvv', scratch=[field])  6.01 us
    ppermute x5, waiting for transfers between devices, swap(): return lax.ppermute(array, 'orb', swapped)  4.59 us
    pallas_call x1, Pallas kernels, per_device(): call(functools.partial(start_kernel, cells), [delivered, pltpu.SMEM((3 *...  3.94 us
  transfers between devices with their start and end apart: 17, of which 13 were waited for; matrix products, arithmetic and copies ran while one was open for 0% of the time, Pallas kernels for 0%

profile of v10, /device:TPU:1, one launch (start us, length us, event | category | flops | bytes accessed | tf_op | source)
XLA Modules:
  0.0 190.8 jit_solution(14523052997558829021)
XLA Ops:
  0.6 3.9 %shard_map.77 = (f32[288,128]{1,0:T(8,128)S(1)}, s32[144]{0:T(256)S(4)}, f32[8,256]{1,0:T(8,128)S(1)}, f32[32,256]{1,0:T(8,128)S(1)}, f32[48,256,256]{2,1,0:T(8,128)S(1)}) custom-call(s32[48]{0:T(128)} %rows_hbm.1, s32[48]{0:T(128)} %cells_hbm.1, f32[8,256]{1,0:T(8,128)} %observed_hbm.1, f32[8,256]{1,0:T(8,128)} %weights_hbm.1, f32[32,256]{1,0:T(8,128)} %prior_hbm.1, ...), custom_call_target="tpu_custom_call" | custom-call | tf_op jit(solution)/shard_map/pallas_call | solution.py:429
  4.6 21.1 %all_to_all.45 = f32[32,1,1152]{2,1,0:T(1,128)S(1)} all-to-all(f32[32,1,1152]{2,1,0:T(1,128)S(1)} %bitcast.31), channel_id=1, replica_groups={{0,8,16,24,32,40,48,56,64,72,80,88,96,104,112,120,128,136,144,152,160,1..., dimensions={0} | all-to-all | bytes 294912 | tf_op jit(solution)/shard_map/all_to_all | solution.py:417
  26.0 2.4 %collective-permute-start = (f32[96,256]{1,0:T(8,128)S(1)}, f32[96,256]{1,0:T(8,128)S(1)}, u32[]{:S(2)}, u32[]{:S(2)}) collective-permute-start(f32[96,256]{1,0:T(8,128)S(1)} %get-tuple-element.46.mine_ref), channel_id=1, source_target_pairs={{0,4},{4,0},{8,12},{12,8},{16,20},{20,16},{24,28},{28,24},{32,36},... | collective-permute-start | bytes 294920 | tf_op jit(solution)/shard_map/ppermute | solution.py:423
  29.5 12.4 %all_to_all.46 = f32[32,1,1024]{2,1,0:T(1,128)S(1)} all-to-all(f32[32,1,1024]{2,1,0:T(1,128)S(1)} %bitcast.35), channel_id=1, replica_groups={{0,8,16,24,32,40,48,56,64,72,80,88,96,104,112,120,128,136,144,152,160,1..., dimensions={0} | all-to-all | bytes 262144 | tf_op jit(solution)/shard_map/all_to_all | solution.py:417
  41.9 1.5 shard_map.80.refs_1_
  43.4 3.0 %collective-permute-start.3 = (f32[24,128]{1,0:T(8,128)S(1)}, f32[24,128]{1,0:T(8,128)S(1)}, u32[]{:S(2)}, u32[]{:S(2)}) collective-permute-start(f32[24,128]{1,0:T(8,128)S(1)} %shard_map.80.refs_1_), channel_id=1, source_target_pairs={{0,2},{1,3},{2,0},{3,1},{4,6},{5,7},{6,4},{7,5},{8,10},{9,11},{10,... | collective-permute-start | bytes 36872 | tf_op jit(solution)/shard_map/ppermute | solution.py:471
  47.5 2.8 %collective-permute-done.2.refs_3_ = f32[24,128]{1,0:T(8,128)S(1)} collective-permute-done((f32[24,128]{1,0:T(8,128)S(1)}, f32[24,128]{1,0:T(8,128)S(1)}, u32[]{:S(2)}, u32[]{:S(2)}) %collective-permute-start.2) | collective-permute-done | bytes 12320 | tf_op jit(solution)/shard_map/ppermute | solution.py:471
  50.4 1.7 shard_map.81
  52.0 13.0 %all_to_all.47 = f32[32,1,1152]{2,1,0:T(1,128)S(1)} all-to-all(f32[32,1,1152]{2,1,0:T(1,128)S(1)} %bitcast.30), channel_id=1, replica_groups={{0,8,16,24,32,40,48,56,64,72,80,88,96,104,112,120,128,136,144,152,160,1..., dimensions={0} | all-to-all | bytes 294912 | tf_op jit(solution)/shard_map/all_to_all | solution.py:417
  65.2 4.4 %collective-permute-start.4 = (f32[72,256]{1,0:T(8,128)S(1)}, f32[72,256]{1,0:T(8,128)S(1)}, u32[]{:S(2)}, u32[]{:S(2)}) collective-permute-start(f32[72,256]{1,0:T(8,128)S(1)} %shard_map.82.refs_0_), channel_id=1, source_target_pairs={{0,4},{4,0},{8,12},{12,8},{16,20},{20,16},{24,28},{28,24},{32,36},... | collective-permute-start | bytes 221192 | tf_op jit(solution)/shard_map/ppermute | solution.py:423
  70.8 12.4 %all_to_all.48 = f32[32,1,1024]{2,1,0:T(1,128)S(1)} all-to-all(f32[32,1,1024]{2,1,0:T(1,128)S(1)} %bitcast.34), channel_id=1, replica_groups={{0,8,16,24,32,40,48,56,64,72,80,88,96,104,112,120,128,136,144,152,160,1..., dimensions={0} | all-to-all | bytes 262144 | tf_op jit(solution)/shard_map/all_to_all | solution.py:417
  83.2 1.5 shard_map.84.refs_1_
  84.7 1.2 collective-permute-start.7
  87.4 1.4 collective-permute-done.7.refs_4_
  89.7 1.6 shard_map.85
  91.3 13.3 %all_to_all.49 = f32[32,1,1152]{2,1,0:T(1,128)S(1)} all-to-all(f32[32,1,1152]{2,1,0:T(1,128)S(1)} %bitcast.29), channel_id=1, replica_groups={{0,8,16,24,32,40,48,56,64,72,80,88,96,104,112,120,128,136,144,152,160,1..., dimensions={0} | all-to-all | bytes 294912 | tf_op jit(solution)/shard_map/all_to_all | solution.py:417
  104.8 4.4 %collective-permute-start.8 = (f32[72,256]{1,0:T(8,128)S(1)}, f32[72,256]{1,0:T(8,128)S(1)}, u32[]{:S(2)}, u32[]{:S(2)}) collective-permute-start(f32[72,256]{1,0:T(8,128)S(1)} %shard_map.86.refs_0_), channel_id=1, source_target_pairs={{0,4},{4,0},{8,12},{12,8},{16,20},{20,16},{24,28},{28,24},{32,36},... | collective-permute-start | bytes 221192 | tf_op jit(solution)/shard_map/ppermute | solution.py:423
  110.4 12.5 %all_to_all.50 = f32[32,1,1024]{2,1,0:T(1,128)S(1)} all-to-all(f32[32,1,1024]{2,1,0:T(1,128)S(1)} %bitcast.32), channel_id=1, replica_groups={{0,8,16,24,32,40,48,56,64,72,80,88,96,104,112,120,128,136,144,152,160,1..., dimensions={0} | all-to-all | bytes 262144 | tf_op jit(solution)/shard_map/all_to_all | solution.py:417
  122.9 1.5 shard_map.88.refs_1_
  124.4 1.9 collective-permute-start.11
  127.4 1.2 collective-permute-done.11.refs_4_
  128.6 1.5 collective-permute-done.10.refs_3_
  130.1 1.6 shard_map.89
  131.7 13.5 %all_to_all.51 = f32[32,1,1152]{2,1,0:T(1,128)S(1)} all-to-all(f32[32,1,1152]{2,1,0:T(1,128)S(1)} %bitcast.28), channel_id=1, replica_groups={{0,8,16,24,32,40,48,56,64,72,80,88,96,104,112,120,128,136,144,152,160,1..., dimensions={0} | all-to-all | bytes 294912 | tf_op jit(solution)/shard_map/all_to_all | solution.py:417
  145.3 4.3 %collective-permute-start.12 = (f32[72,256]{1,0:T(8,128)S(1)}, f32[72,256]{1,0:T(8,128)S(1)}, u32[]{:S(2)}, u32[]{:S(2)}) collective-permute-start(f32[72,256]{1,0:T(8,128)S(1)} %shard_map.90.refs_0_), channel_id=1, source_target_pairs={{0,4},{4,0},{8,12},{12,8},{16,20},{20,16},{24,28},{28,24},{32,36},... | collective-permute-start | bytes 221192 | tf_op jit(solution)/shard_map/ppermute | solution.py:423
  150.8 12.4 %all_to_all.52 = f32[32,1,1024]{2,1,0:T(1,128)S(1)} all-to-all(f32[32,1,1024]{2,1,0:T(1,128)S(1)} %bitcast.33), channel_id=1, replica_groups={{0,8,16,24,32,40,48,56,64,72,80,88,96,104,112,120,128,136,144,152,160,1..., dimensions={0} | all-to-all | bytes 262144 | tf_op jit(solution)/shard_map/all_to_all | solution.py:417
  163.2 1.5 shard_map.92.refs_1_
  164.7 1.2 collective-permute-start.15
  167.4 1.4 collective-permute-done.15.refs_4_
  169.7 1.6 shard_map.93
  171.3 13.3 %all_to_all.53 = f32[32,1,1152]{2,1,0:T(1,128)S(1)} all-to-all(f32[32,1,1152]{2,1,0:T(1,128)S(1)} %bitcast.23), channel_id=1, replica_groups={{0,8,16,24,32,40,48,56,64,72,80,88,96,104,112,120,128,136,144,152,160,1..., dimensions={0} | all-to-all | bytes 294912 | tf_op jit(solution)/shard_map/all_to_all | solution.py:417
  184.8 4.4 %collective-permute-start.16 = (f32[72,256]{1,0:T(8,128)S(1)}, f32[72,256]{1,0:T(8,128)S(1)}, u32[]{:S(2)}, u32[]{:S(2)}) collective-permute-start(f32[72,256]{1,0:T(8,128)S(1)} %shard_map.94.refs_0_), channel_id=1, source_target_pairs={{0,4},{4,0},{8,12},{12,8},{16,20},{20,16},{24,28},{28,24},{32,36},... | collective-permute-start | bytes 221192 | tf_op jit(solution)/shard_map/ppermute | solution.py:423
  (30 shorter events, 14.2 us)
Async XLA Ops:
  26.0 3.3 %collective-permute-start = (f32[96,256]{1,0:T(8,128)S(1)}, f32[96,256]{1,0:T(8,128)S(1)}, u32[]{:S(2)}, u32[]{:S(2)}) collective-permute-start(f32[96,256]{1,0:T(8,128)S(1)} %get-tuple-element.46.mine_ref), channel_id=1, source_target_pairs={{0,4},{4,0},{8,12},{12,8},{16,20},{20,16},{24,28},{28,24},{32,36},... | collective-permute-start | bytes 294920 | tf_op jit(solution)/shard_map/ppermute | solution.py:423
  43.4 4.1 %collective-permute-start.3 = (f32[24,128]{1,0:T(8,128)S(1)}, f32[24,128]{1,0:T(8,128)S(1)}, u32[]{:S(2)}, u32[]{:S(2)}) collective-permute-start(f32[24,128]{1,0:T(8,128)S(1)} %shard_map.80.refs_1_), channel_id=1, source_target_pairs={{0,2},{1,3},{2,0},{3,1},{4,6},{5,7},{6,4},{7,5},{8,10},{9,11},{10,... | collective-permute-start | bytes 36872 | tf_op jit(solution)/shard_map/ppermute | solution.py:471
  46.4 4.0 %collective-permute-start.2 = (f32[24,128]{1,0:T(8,128)S(1)}, f32[24,128]{1,0:T(8,128)S(1)}, u32[]{:S(2)}, u32[]{:S(2)}) collective-permute-start(f32[24,128]{1,0:T(8,128)S(1)} %shard_map.80.refs_1_), channel_id=1, source_target_pairs={{0,3},{1,2},{2,1},{3,0},{4,7},{5,6},{6,5},{7,4},{8,11},{9,10},{10,... | collective-permute-start | bytes 36872 | tf_op jit(solution)/shard_map/ppermute | solution.py:471
  47.1 3.2 %collective-permute-start.1 = (f32[24,128]{1,0:T(8,128)S(1)}, f32[24,128]{1,0:T(8,128)S(1)}, u32[]{:S(2)}, u32[]{:S(2)}) collective-permute-start(f32[24,128]{1,0:T(8,128)S(1)} %shard_map.80.refs_1_), channel_id=1, source_target_pairs={{0,1},{1,0},{2,3},{3,2},{4,5},{5,4},{6,7},{7,6},{8,9},{9,8},{10,11... | collective-permute-start | bytes 36872 | tf_op jit(solution)/shard_map/ppermute | solution.py:471
  65.2 5.3 %collective-permute-start.4 = (f32[72,256]{1,0:T(8,128)S(1)}, f32[72,256]{1,0:T(8,128)S(1)}, u32[]{:S(2)}, u32[]{:S(2)}) collective-permute-start(f32[72,256]{1,0:T(8,128)S(1)} %shard_map.82.refs_0_), channel_id=1, source_target_pairs={{0,4},{4,0},{8,12},{12,8},{16,20},{20,16},{24,28},{28,24},{32,36},... | collective-permute-start | bytes 221192 | tf_op jit(solution)/shard_map/ppermute | solution.py:423
  84.7 4.1 %collective-permute-start.7 = (f32[24,128]{1,0:T(8,128)S(1)}, f32[24,128]{1,0:T(8,128)S(1)}, u32[]{:S(2)}, u32[]{:S(2)}) collective-permute-start(f32[24,128]{1,0:T(8,128)S(1)} %shard_map.84.refs_1_), channel_id=1, source_target_pairs={{0,2},{1,3},{2,0},{3,1},{4,6},{5,7},{6,4},{7,5},{8,10},{9,11},{10,... | collective-permute-start | bytes 36872 | tf_op jit(solution)/shard_map/ppermute | solution.py:471
  85.9 3.8 %collective-permute-start.6 = (f32[24,128]{1,0:T(8,128)S(1)}, f32[24,128]{1,0:T(8,128)S(1)}, u32[]{:S(2)}, u32[]{:S(2)}) collective-permute-start(f32[24,128]{1,0:T(8,128)S(1)} %shard_map.84.refs_1_), channel_id=1, source_target_pairs={{0,3},{1,2},{2,1},{3,0},{4,7},{5,6},{6,5},{7,4},{8,11},{9,10},{10,... | collective-permute-start | bytes 36872 | tf_op jit(solution)/shard_map/ppermute | solution.py:471
  86.7 2.9 %collective-permute-start.5 = (f32[24,128]{1,0:T(8,128)S(1)}, f32[24,128]{1,0:T(8,128)S(1)}, u32[]{:S(2)}, u32[]{:S(2)}) collective-permute-start(f32[24,128]{1,0:T(8,128)S(1)} %shard_map.84.refs_1_), channel_id=1, source_target_pairs={{0,1},{1,0},{2,3},{3,2},{4,5},{5,4},{6,7},{7,6},{8,9},{9,8},{10,11... | collective-permute-start | bytes 36872 | tf_op jit(solution)/shard_map/ppermute | solution.py:471
  104.8 5.3 %collective-permute-start.8 = (f32[72,256]{1,0:T(8,128)S(1)}, f32[72,256]{1,0:T(8,128)S(1)}, u32[]{:S(2)}, u32[]{:S(2)}) collective-permute-start(f32[72,256]{1,0:T(8,128)S(1)} %shard_map.86.refs_0_), channel_id=1, source_target_pairs={{0,4},{4,0},{8,12},{12,8},{16,20},{20,16},{24,28},{28,24},{32,36},... | collective-permute-start | bytes 221192 | tf_op jit(solution)/shard_map/ppermute | solution.py:423
  124.4 4.1 %collective-permute-start.11 = (f32[24,128]{1,0:T(8,128)S(1)}, f32[24,128]{1,0:T(8,128)S(1)}, u32[]{:S(2)}, u32[]{:S(2)}) collective-permute-start(f32[24,128]{1,0:T(8,128)S(1)} %shard_map.88.refs_1_), channel_id=1, source_target_pairs={{0,2},{1,3},{2,0},{3,1},{4,6},{5,7},{6,4},{7,5},{8,10},{9,11},{10,... | collective-permute-start | bytes 36872 | tf_op jit(solution)/shard_map/ppermute | solution.py:471
  126.3 3.8 %collective-permute-start.10 = (f32[24,128]{1,0:T(8,128)S(1)}, f32[24,128]{1,0:T(8,128)S(1)}, u32[]{:S(2)}, u32[]{:S(2)}) collective-permute-start(f32[24,128]{1,0:T(8,128)S(1)} %shard_map.88.refs_1_), channel_id=1, source_target_pairs={{0,3},{1,2},{2,1},{3,0},{4,7},{5,6},{6,5},{7,4},{8,11},{9,10},{10,... | collective-permute-start | bytes 36872 | tf_op jit(solution)/shard_map/ppermute | solution.py:471
  127.4 2.7 %collective-permute-start.9 = (f32[24,128]{1,0:T(8,128)S(1)}, f32[24,128]{1,0:T(8,128)S(1)}, u32[]{:S(2)}, u32[]{:S(2)}) collective-permute-start(f32[24,128]{1,0:T(8,128)S(1)} %shard_map.88.refs_1_), channel_id=1, source_target_pairs={{0,1},{1,0},{2,3},{3,2},{4,5},{5,4},{6,7},{7,6},{8,9},{9,8},{10,11... | collective-permute-start | bytes 36872 | tf_op jit(solution)/shard_map/ppermute | solution.py:471
  145.3 5.2 %collective-permute-start.12 = (f32[72,256]{1,0:T(8,128)S(1)}, f32[72,256]{1,0:T(8,128)S(1)}, u32[]{:S(2)}, u32[]{:S(2)}) collective-permute-start(f32[72,256]{1,0:T(8,128)S(1)} %shard_map.90.refs_0_), channel_id=1, source_target_pairs={{0,4},{4,0},{8,12},{12,8},{16,20},{20,16},{24,28},{28,24},{32,36},... | collective-permute-start | bytes 221192 | tf_op jit(solution)/shard_map/ppermute | solution.py:423
  164.7 4.1 %collective-permute-start.15 = (f32[24,128]{1,0:T(8,128)S(1)}, f32[24,128]{1,0:T(8,128)S(1)}, u32[]{:S(2)}, u32[]{:S(2)}) collective-permute-start(f32[24,128]{1,0:T(8,128)S(1)} %shard_map.92.refs_1_), channel_id=1, source_target_pairs={{0,2},{1,3},{2,0},{3,1},{4,6},{5,7},{6,4},{7,5},{8,10},{9,11},{10,... | collective-permute-start | bytes 36872 | tf_op jit(solution)/shard_map/ppermute | solution.py:471
  165.9 3.8 %collective-permute-start.14 = (f32[24,128]{1,0:T(8,128)S(1)}, f32[24,128]{1,0:T(8,128)S(1)}, u32[]{:S(2)}, u32[]{:S(2)}) collective-permute-start(f32[24,128]{1,0:T(8,128)S(1)} %shard_map.92.refs_1_), channel_id=1, source_target_pairs={{0,3},{1,2},{2,1},{3,0},{4,7},{5,6},{6,5},{7,4},{8,11},{9,10},{10,... | collective-permute-start | bytes 36872 | tf_op jit(solution)/shard_map/ppermute | solution.py:471
  166.9 2.7 %collective-permute-start.13 = (f32[24,128]{1,0:T(8,128)S(1)}, f32[24,128]{1,0:T(8,128)S(1)}, u32[]{:S(2)}, u32[]{:S(2)}) collective-permute-start(f32[24,128]{1,0:T(8,128)S(1)} %shard_map.92.refs_1_), channel_id=1, source_target_pairs={{0,1},{1,0},{2,3},{3,2},{4,5},{5,4},{6,7},{7,6},{8,9},{9,8},{10,11... | collective-permute-start | bytes 36872 | tf_op jit(solution)/shard_map/ppermute | solution.py:471
  184.8 5.3 %collective-permute-start.16 = (f32[72,256]{1,0:T(8,128)S(1)}, f32[72,256]{1,0:T(8,128)S(1)}, u32[]{:S(2)}, u32[]{:S(2)}) collective-permute-start(f32[72,256]{1,0:T(8,128)S(1)} %shard_map.94.refs_0_), channel_id=1, source_target_pairs={{0,4},{4,0},{8,12},{12,8},{16,20},{20,16},{24,28},{28,24},{32,36},... | collective-permute-start | bytes 221192 | tf_op jit(solution)/shard_map/ppermute | solution.py:423
